TPU v7x, 256 devices: a whole 4x4x8 slice. The times are simulated.
256 devices in a mesh: filt: 8 (over y, core), rows: 16 (over x_lo, z), rep: 2 (over x_hi).
Axes of the slice: x: 4 (x_hi: 2, x_lo: 2; x = x_hi * 2 + x_lo), y: 4, z: 8, core: 2. Of those that a mesh axis runs over, the one named last changes fastest.
Arguments:
- features: bfloat16 [2, 64, 64, 2048], P('rep', 'rows', None, 'filt'), may hold values from -6 to 6
- kernel: bfloat16 [3, 3, 2048, 2048], P(None, None, 'rows', 'filt'), may hold values from -0.046875 to 0.046875
- cotangent: bfloat16 [2, 32, 32, 2048], P('rep', 'rows', None, 'filt'), may hold values from -6 to 6
Outputs:
- pooled: bfloat16 [2, 32, 32, 2048], P('rep', 'rows', None, 'filt')
- input_grad: bfloat16 [2, 64, 64, 2048], P('rep', 'rows', None, 'filt')
- kernel_grad: float32 [3, 3, 2048, 2048], P(None, None, 'rows', 'filt')
All inputs are finite; a program needn't handle non-finite values.
Results may differ from a plain program's by a relative error of at most 0.0032.
Values may be sent and summed in bfloat16 or wider, within the bound.
No kernel may reach another device: no remote copies, remote signals or barrier semaphores. Data moves between devices by JAX's collectives and lax.ppermute only.
A program may use at most 128 MiB of HBM per device.

v0:
```python
import jax
import jax.numpy as jnp
from jax import lax
from jax.sharding import PartitionSpec as P


def padded(block, sides, width):
    for axis, dim in sides:
        count = lax.axis_size(axis)
        forward = [(i, i + 1) for i in range(count - 1)]
        backward = [(target, source) for source, target in forward]
        low = lax.ppermute(
            lax.slice_in_dim(block, block.shape[dim] - width, None, axis=dim), axis, forward
        )
        high = lax.ppermute(lax.slice_in_dim(block, 0, width, axis=dim), axis, backward)
        block = jnp.concatenate([low, block, high], axis=dim)
    return block


def silu_slope(values):
    logistic = jax.nn.sigmoid(values)
    return logistic * (1.0 + values * (1.0 - logistic))


def local(features, kernel, cotangent):
    images, tile_rows, columns, local_channels = features.shape
    values = features.astype(jnp.float32)
    activated = jax.nn.silu(values).astype(jnp.bfloat16)
    gathered = lax.all_gather(activated, "filt", axis=3, tiled=True)
    rimmed = padded(gathered, (("rows", 1),), 1)
    framed = jnp.pad(rimmed, ((0, 0), (0, 0), (1, 1), (0, 0)))
    all_channels = framed.shape[3]
    full_kernel = lax.all_gather(kernel, "rows", axis=2, tiled=True)
    token_count = images * tile_rows * columns
    conv_sum = jnp.zeros((token_count, local_channels), jnp.float32)
    windows = []
    for row_tap in range(3):
        for col_tap in range(3):
            window = framed[
                :, row_tap : row_tap + tile_rows, col_tap : col_tap + columns, :
            ].reshape(token_count, all_channels)
            windows.append(window)
            conv_sum = conv_sum + jnp.dot(
                window, full_kernel[row_tap, col_tap], preferred_element_type=jnp.float32
            )
    pre_pool = values + conv_sum.reshape(images, tile_rows, columns, local_channels)
    pooled = (
        pre_pool.reshape(images, tile_rows // 2, 2, columns // 2, 2, local_channels)
        .mean(axis=(2, 4))
        .astype(jnp.bfloat16)
    )
    up_grad = (
        jnp.repeat(jnp.repeat(cotangent.astype(jnp.float32), 2, axis=1), 2, axis=2) * 0.25
    ).astype(jnp.bfloat16)
    grad_framed = padded(up_grad, (("rows", 1),), 1)
    grad_framed = jnp.pad(grad_framed, ((0, 0), (0, 0), (1, 1), (0, 0)))
    back_sum = jnp.zeros((token_count, all_channels), jnp.float32)
    for row_tap in range(3):
        for col_tap in range(3):
            grad_window = grad_framed[
                :, 2 - row_tap : 2 - row_tap + tile_rows, 2 - col_tap : 2 - col_tap + columns, :
            ].reshape(token_count, local_channels)
            back_sum = back_sum + lax.dot_general(
                grad_window,
                full_kernel[row_tap, col_tap],
                (((1,), (1,)), ((), ())),
                preferred_element_type=jnp.float32,
            )
    act_grad = lax.psum_scatter(
        back_sum.reshape(images, tile_rows, columns, all_channels),
        "filt",
        scatter_dimension=3,
        tiled=True,
    )
    input_grad = (up_grad.astype(jnp.float32) + act_grad * silu_slope(values)).astype(jnp.bfloat16)
    grad_flat = up_grad.reshape(token_count, local_channels)
    kernel_terms = jnp.stack(
        [
            lax.dot_general(
                window, grad_flat, (((0,), (0,)), ((), ())), preferred_element_type=jnp.float32
            )
            for window in windows
        ]
    ).reshape(3, 3, all_channels, local_channels)
    summed = lax.psum_scatter(kernel_terms, "rows", scatter_dimension=2, tiled=True)
    kernel_grad = lax.psum(summed, "rep")
    return (pooled, input_grad, kernel_grad)


def solution(mesh):
    placed = (
        P("rep", "rows", None, "filt"),
        P(None, None, "rows", "filt"),
        P("rep", "rows", None, "filt"),
    )
    return jax.shard_map(
        local,
        mesh=mesh,
        in_specs=placed,
        out_specs=(
            P("rep", "rows", None, "filt"),
            P("rep", "rows", None, "filt"),
            P(None, None, "rows", "filt"),
        ),
        check_vma=False,
    )
```

profile of v0, /device:TPU:56, one launch (start us, length us, event | category | flops | bytes accessed | tf_op | source)
XLA Modules:
  0.0 463.6 jit_solution(2636339312772503632)
XLA Ops:
  7.2 1.6 fusion.46
  8.9 0.7 all-gather.5.cloned.1.call-update
  9.7 28.3 %all-gather.3.cloned.1.call-done = bf16[1,4,64,2048]{3,2,1,0:T(8,128)(2,1)} async-done(((bf16[1,4,64,256]{3,2,1,0:T(8,128)(2,1)}), bf16[1,4,64,2048]{3,2,1,0:T(8,128)(2,1)}) %all-gather.3.cloned.1.call-update) | async-done | bytes 1048592 | tf_op jit(solution)/shard_map/all_gather | solution.py:29
  38.0 1.2 fusion.66
  39.2 3.5 collective-permute-start
  42.6 2.4 collective-permute-start.1
  45.0 0.8 fusion.58
  46.0 3.6 collective-permute-done
  49.5 3.2 collective-permute-done.1
  52.7 0.7 copy-done.4
  53.4 1.6 pad_maximum_fusion.1
  55.0 1.7 fusion.15
  56.7 1.8 fusion.9
  58.5 1.8 fusion.8
  60.3 1.9 fusion.7
  62.2 1.9 fusion.6
  64.1 1.9 fusion.5
  65.9 1.9 fusion.4
  67.8 1.8 fusion.3
  69.6 1.8 fusion.2
  71.4 1.8 fusion.1
  73.4 4.5 collective-permute-start.2
  77.9 1.9 collective-permute-start.3
  79.8 0.7 convert_element_type.106
  80.5 4.8 %collective-permute-done.3 = bf16[1,1,64,256]{3,2,1,0:T(8,128)(2,1)S(1)} collective-permute-done((bf16[1,1,64,256]{3,2,1,0:T(8,128)(2,1)S(1)}, bf16[1,1,64,256]{3,2,1,0:T(8,128)(2,1)S(1)}, u32[]{:S(2)}, u32[]{:S(2)}) %collective-permute-start.3) | collective-permute-done | bytes 32800 | tf_op jit(solution)/shard_map/ppermute | solution.py:15
  85.4 0.7 pad_maximum_fusion.2
  86.0 0.8 fusion.67
  86.8 64.2 %all-gather.5.cloned.1.call-done = bf16[3,3,2048,256]{3,2,1,0:T(8,128)(2,1)} async-done(((bf16[3,3,128,256]{3,2,1,0:T(8,128)(2,1)}), bf16[3,3,2048,256]{3,2,1,0:T(8,128)(2,1)}) %all-gather.5.cloned.1.call-update) | async-done | bytes 9437200 | tf_op jit(solution)/shard_map/all_gather | solution.py:33
  151.1 1.8 fusion.28
  152.9 2.5 fusion.40
  155.4 1.7 convolution_add_fusion.6
  160.4 1.9 fusion.10
  162.6 2.2 fusion.65
  164.7 2.1 fusion.35
  166.8 2.4 fusion.36
  169.2 2.4 fusion.34
  171.5 2.4 fusion.37
  173.9 2.5 fusion.38
  176.4 2.4 fusion.41
  178.8 179.4 %reduce-scatter.5.cloned.1.call-done = f32[3,3,128,256]{3,2,1,0:T(8,128)} async-done(((f32[3,3,2048,256]{3,2,1,0:T(8,128)}), f32[3,3,128,256]{3,2,1,0:T(8,128)}) %reduce-scatter.5.cloned.1.call-update) | async-done | bytes 1179664 | tf_op jit(solution)/shard_map/reduce_scatter | solution.py:85
  358.3 1.8 fusion.39
  360.1 1.9 fusion.33
  362.0 1.7 fusion.18
  363.7 30.3 %reduce-scatter.3.cloned.1.call-done = f32[1,4,64,256]{3,2,1,0:T(8,128)} async-done(((f32[1,4,64,2048]{3,2,1,0:T(8,128)}), f32[1,4,64,256]{3,2,1,0:T(8,128)}) %reduce-scatter.3.cloned.1.call-update) | async-done | bytes 262160 | tf_op jit(solution)/shard_map/reduce_scatter | solution.py:69
  394.0 1.7 fusion.51
  396.1 0.6 fusion.57
  396.7 58.0 %all-reduce.4.cloned.1.call-done = f32[3,3,128,256]{3,2,1,0:T(8,128)} async-done(((f32[3,3,128,256]{3,2,1,0:T(8,128)}), f32[3,3,128,256]{3,2,1,0:T(8,128)}) %all-reduce.4.cloned.1.call-update) | async-done | bytes 1179664 | tf_op jit(solution)/shard_map/psum | solution.py:86
  454.7 2.4 copy.15
  (56 shorter events, 4.3 us)
Async XLA Ops:
  7.2 30.8 %all-gather.3.cloned.1.call-start = ((), (), s32[]{:S(2)}) async-start(), calls=%async_computation.2 | async-start | bytes 1179648 | tf_op jit(solution)/shard_map/all_gather | solution.py:29
  8.9 142.2 %all-gather.5.cloned.1.call-start = ((), (), s32[]{:S(2)}) async-start(), calls=%async_computation.3 | async-start | bytes 10027008 | tf_op jit(solution)/shard_map/all_gather | solution.py:33
  9.6 348.6 %reduce-scatter.5.cloned.1.call-start = ((), (), s32[]{:S(2)}) async-start(), calls=%async_computation.5 | async-start | bytes 20054016 | tf_op jit(solution)/shard_map/reduce_scatter | solution.py:85
  38.0 17.0 %copy-start.1 = (bf16[1,4,64,2048]{3,2,1,0:T(8,128)(2,1)S(1)}, bf16[1,4,64,2048]{3,2,1,0:T(8,128)(2,1)}, u32[]{:S(2)}) copy-start(bf16[1,4,64,2048]{3,2,1,0:T(8,128)(2,1)} %all-gather.3.cloned.1.call-done) | copy-start | bytes 3145732
  39.2 10.3 %collective-permute-start = (bf16[1,1,64,2048]{3,2,1,0:T(8,128)(2,1)S(1)}, bf16[1,1,64,2048]{3,2,1,0:T(8,128)(2,1)S(1)}, u32[]{:S(2)}, u32[]{:S(2)}) collective-permute-start(bf16[1,1,64,2048]{3,2,1,0:T(8,128)(2,1)S(1)} %get-tuple-element.11), channel_id=1, source_target_pairs={{0,2},{2,4},{4,6},{6,8},{8,10},{10,12},{12,14},{14,16},{16,18},{18... | collective-permute-start | bytes 786440 | tf_op jit(solution)/shard_map/ppermute | solution.py:12
  42.6 10.1 %collective-permute-start.1 = (bf16[1,1,64,2048]{3,2,1,0:T(8,128)(2,1)S(1)}, bf16[1,1,64,2048]{3,2,1,0:T(8,128)(2,1)S(1)}, u32[]{:S(2)}, u32[]{:S(2)}) collective-permute-start(bf16[1,1,64,2048]{3,2,1,0:T(8,128)(2,1)S(1)} %get-tuple-element.12), channel_id=1, source_target_pairs={{2,0},{4,2},{6,4},{8,6},{10,8},{12,10},{14,12},{16,14},{18,16},{20... | collective-permute-start | bytes 786440 | tf_op jit(solution)/shard_map/ppermute | solution.py:15
  52.7 0.7 copy-start.4
  55.0 3.5 copy-start.7
  55.0 14.6 %copy-start.5 = (bf16[1,4,64,2048]{3,2,1,0:T(8,128)(2,1)}, bf16[1,4,64,2048]{3,2,1,0:T(8,128)(2,1)S(1)}, u32[]{:S(2)}) copy-start(bf16[1,4,64,2048]{3,2,1,0:T(8,128)(2,1)S(1)} %get-tuple-element.10) | copy-start | bytes 3145732
  73.3 320.8 %reduce-scatter.3.cloned.1.call-start = ((), (), s32[]{:S(2)}) async-start(), calls=%async_computation.4 | async-start | bytes 2359296 | tf_op jit(solution)/shard_map/reduce_scatter | solution.py:69
  73.4 7.1 %collective-permute-start.2 = (bf16[1,1,64,256]{3,2,1,0:T(8,128)(2,1)S(1)}, bf16[1,1,64,256]{3,2,1,0:T(8,128)(2,1)S(1)}, u32[]{:S(2)}, u32[]{:S(2)}) collective-permute-start(bf16[1,1,64,256]{3,2,1,0:T(8,128)(2,1)S(1)} %get-tuple-element.23), channel_id=1, source_target_pairs={{0,2},{2,4},{4,6},{6,8},{8,10},{10,12},{12,14},{14,16},{16,18},{18... | collective-permute-start | bytes 98312 | tf_op jit(solution)/shard_map/ppermute | solution.py:12
  77.9 7.4 %collective-permute-start.3 = (bf16[1,1,64,256]{3,2,1,0:T(8,128)(2,1)S(1)}, bf16[1,1,64,256]{3,2,1,0:T(8,128)(2,1)S(1)}, u32[]{:S(2)}, u32[]{:S(2)}) collective-permute-start(bf16[1,1,64,256]{3,2,1,0:T(8,128)(2,1)S(1)} %get-tuple-element.24), channel_id=1, source_target_pairs={{2,0},{4,2},{6,4},{8,6},{10,8},{12,10},{14,12},{16,14},{18,16},{20... | collective-permute-start | bytes 98312 | tf_op jit(solution)/shard_map/ppermute | solution.py:15
  151.1 4.3 copy-start.11
  151.1 6.1 %copy-start = (bf16[3,3,2048,256]{3,2,1,0:T(8,128)(2,1)S(1)}, bf16[3,3,2048,256]{3,2,1,0:T(8,128)(2,1)}, u32[]{:S(2)}) copy-start(bf16[3,3,2048,256]{3,2,1,0:T(8,128)(2,1)} %all-gather.5.cloned.1.call-done) | copy-start | bytes 28311556
  152.9 4.2 copy-start.13
  157.1 0.9 copy-start.12
  157.6 0.9 copy-start.14
  158.5 0.9 copy-start.10
  162.3 292.4 %all-reduce.4.cloned.1.call-start = ((), (), s32[]{:S(2)}) async-start(), calls=%async_computation.6 | async-start | bytes 2359296 | tf_op jit(solution)/shard_map/psum | solution.py:86
  164.7 4.4 copy-start.8
  173.9 184.3 %copy-start.6 = (bf16[1,4,64,2048]{3,2,1,0:T(8,128)(2,1)S(1)}, bf16[1,4,64,2048]{3,2,1,0:T(8,128)(2,1)}, u32[]{:S(2)}) copy-start(bf16[1,4,64,2048]{3,2,1,0:T(8,128)(2,1)} %copy-done.5) | copy-start | bytes 3145732
  176.4 183.7 %copy-start.3 = (bf16[1,4,64,2048]{3,2,1,0:T(8,128)(2,1)S(1)}, bf16[1,4,64,2048]{3,2,1,0:T(8,128)(2,1)}, u32[]{:S(2)}) copy-start(bf16[1,4,64,2048]{3,2,1,0:T(8,128)(2,1)} %get-tuple-element.7) | copy-start | bytes 3145732
  358.2 3.8 copy-start.2
  358.2 3.7 copy-start.15
  358.2 3.7 copy-start.16
  360.0 34.0 %copy-start.9 = (bf16[1,4,64,256]{3,2,1,0:T(8,128)(2,1)S(1)}, bf16[1,4,64,256]{3,2,1,0:T(8,128)(2,1)}, u32[]{:S(2)}) copy-start(bf16[1,4,64,256]{3,2,1,0:T(8,128)(2,1)} %param.3) | copy-start | bytes 393220
Sparse Core Ops, SparseCore 0:
  10.4 27.5 all-gather.2
  39.8 111.2 all-gather.4
  153.6 204.5 reduce-scatter.4
  360.6 33.3 reduce-scatter.2
  396.4 58.2 all-reduce.3
where the time goes:
time: 466 us; the launch traced here: 464 us
  waiting for transfers between devices  373 us (80%)
  matrix products  46.3 us (10%)
  between operations  14.1 us (3%)
  starting transfers between devices  12.7 us (3%)
  local copies, waits for them, and re-layouts  9.11 us (2%)
  other arithmetic  8.89 us (2%)
    reduce_scatter x1, waiting for transfers between devices, local(): lax.psum_scatter(kernel_terms, 'rows', scatter_dimension=2, tiled=True)  179 us
    all_gather x1, waiting for transfers between devices, local(): full_kernel = lax.all_gather(kernel, 'rows', axis=2, tiled=True)  64.2 us
    psum x1, waiting for transfers between devices, local(): kernel_grad = lax.psum(summed, 'rep')  58 us
    reduce_scatter x1, waiting for transfers between devices, local(): lax.psum_scatter(back_sum.reshape(images, tile_rows, columns, all_channel...  30.3 us
    all_gather x1, waiting for transfers between devices, local(): gathered = lax.all_gather(activated, 'filt', axis=3, tiled=True)  28.3 us
    dot_general x9, matrix products, local(): jnp.dot(window, full_kernel[row_tap, col_tap], preferred_element_type=jnp...  19.4 us
    dot_general x9, matrix products, local(): lax.dot_general(window, grad_flat, (((0,), (0,)), ((), ())), preferred_el...  16.6 us
    dot_general x9, matrix products, local(): lax.dot_general(grad_window, full_kernel[row_tap, col_tap], (((1,), (1,))...  10.3 us
  transfers between devices with their start and end apart: 9, of which 8 were waited for; matrix products, arithmetic and copies ran while one was open for 13% of the time, Pallas kernels for 0%

commit v1 on v0

v1 whole, which is shorter than its diff:
```python
import jax
import jax.numpy as jnp
from jax import lax
from jax.sharding import PartitionSpec as P

AXES = ("filt", "rows", "rep")


def swap_tiles(same, other):
    sizes = [lax.axis_size(axis) for axis in AXES]
    stay, cross = [], []
    for f in range(sizes[0]):
        for r in range(sizes[1]):
            for g in range(sizes[2]):
                a, h = r // 2, r % 2
                source = (f * sizes[1] + r) * sizes[2] + g
                stay.append((source, (a * sizes[1] + 2 * f + h) * sizes[2] + g))
                cross.append((source, (a * sizes[1] + 2 * f + 1 - h) * sizes[2] + g))
    return lax.ppermute(same, AXES, stay), lax.ppermute(other, AXES, cross)


def local(features, kernel, cotangent):
    tile_rows, columns, local_channels = features.shape[1:]
    half = local_channels // 2
    odd = lax.axis_index("rows") % 2 == 1
    filt_count = lax.axis_size("filt")
    row_count = lax.axis_size("rows")
    height = tile_rows * row_count
    kernel_flat = kernel.reshape(9 * half, local_channels)

    packed = jnp.concatenate(
        [
            features.reshape(tile_rows * columns, local_channels),
            cotangent.reshape(tile_rows * columns // 4, local_channels),
        ],
        axis=0,
    )
    low, high = packed[:, :half], packed[:, half:]
    got_same, got_other = swap_tiles(jnp.where(odd, high, low), jnp.where(odd, low, high))
    tiles = jnp.stack([jnp.where(odd, got_other, got_same), jnp.where(odd, got_same, got_other)])
    tokens = tile_rows * columns
    values = tiles[:, :tokens].reshape(2 * tile_rows, columns, half).astype(jnp.float32)
    own_cot = tiles[:, tokens:].reshape(tile_rows, columns // 2, half).astype(jnp.float32)
    own_up = jnp.repeat(jnp.repeat(own_cot, 2, axis=0), 2, axis=1) * 0.25
    logistic = jax.nn.sigmoid(values)
    activated = jax.nn.silu(values).astype(jnp.bfloat16)
    act = lax.all_gather(activated, "filt", axis=0, tiled=True)

    copies = jnp.broadcast_to(cotangent, (row_count,) + cotangent.shape[1:])
    cot = lax.all_to_all(copies, "rows", 0, 0, tiled=True).reshape(height // 2, columns // 2, local_channels)

    up = jnp.repeat(jnp.repeat(cot, 2, axis=0), 2, axis=1)[None]
    back = lax.conv_general_dilated(
        up,
        kernel[::-1, ::-1],
        (1, 1),
        ((1, 1), (1, 1)),
        dimension_numbers=("NHWC", "HWOI", "NHWC"),
        preferred_element_type=jnp.float32,
    )
    back = (back[0] * 0.25).astype(jnp.bfloat16)
    back = lax.all_to_all(back, "filt", 0, 0, tiled=True)
    act_grad = back.reshape(filt_count, 2 * tile_rows, columns, half).astype(jnp.float32).sum(axis=0)
    slope = logistic * (1.0 + values * (1.0 - logistic))
    input_grad = (own_up + act_grad * slope).astype(jnp.bfloat16).reshape(2, tokens, half)
    sent = jnp.where(odd, input_grad[1], input_grad[0]), jnp.where(odd, input_grad[0], input_grad[1])
    got_same, got_other = swap_tiles(*sent)
    input_grad = jnp.concatenate(
        [jnp.where(odd, got_other, got_same), jnp.where(odd, got_same, got_other)], axis=-1
    ).reshape(features.shape)

    framed = jnp.pad(act, ((1, 1), (1, 1), (0, 0))).astype(jnp.float32)
    boxes = framed[:-1] + framed[1:]
    boxes = boxes[:, :-1] + boxes[:, 1:]
    coarse = boxes.astype(jnp.bfloat16)
    fine = (boxes - coarse.astype(jnp.float32)).astype(jnp.bfloat16)

    def windows(source):
        return jnp.concatenate(
            [
                source[p : p + height : 2, q : q + columns : 2].reshape(height * columns // 4, half)
                for p in range(3)
                for q in range(3)
            ],
            axis=1,
        )

    coarse, fine = windows(coarse), windows(fine)
    cot_flat = cot.reshape(height * columns // 4, local_channels)
    kernel_term = lax.dot_general(
        coarse, cot_flat, (((0,), (0,)), ((), ())), preferred_element_type=jnp.float32
    ) * 0.25
    arrived = lax.ppermute(kernel_term.astype(jnp.bfloat16), "rep", [(0, 1), (1, 0)])
    kernel_grad = (kernel_term + arrived.astype(jnp.float32)).reshape(kernel.shape)

    conv = jnp.dot(coarse, kernel_flat, preferred_element_type=jnp.float32)
    conv = conv + jnp.dot(fine, kernel_flat, preferred_element_type=jnp.float32)
    conv = conv.astype(jnp.bfloat16).reshape(height // 2, columns // 2, local_channels)
    conv = lax.all_to_all(conv, "rows", 0, 0, tiled=True)
    conv = conv.reshape(row_count, tile_rows // 2, columns // 2, local_channels).astype(jnp.float32).sum(axis=0)
    cells = features.astype(jnp.float32).reshape(tile_rows // 2, 2, columns // 2, 2, local_channels)
    pooled = ((cells.sum(axis=(1, 3)) + conv) * 0.25).astype(jnp.bfloat16)[None]
    return (pooled, input_grad, kernel_grad)


def solution(mesh):
    tiles = P("rep", "rows", None, "filt")
    weights = P(None, None, "rows", "filt")
    return jax.shard_map(
        local,
        mesh=mesh,
        in_specs=(tiles, weights, tiles),
        out_specs=(tiles, tiles, weights),
        check_vma=False,
    )
```

time: 466 us -> 284 us (0.61)
  waiting for transfers between devices: 373 us -> 32.4 us
  local copies, waits for them, and re-layouts: 9.11 us -> 157 us
  matrix products: 46.3 us -> 9.81 us
  blocking collectives: 0 us -> 24.3 us
  starting transfers between devices: 12.7 us -> 35.9 us
    reduce_scatter x2 -> x0, waiting for transfers between devices: 210 us -> none  [the longest x1 179 us: local(): lax.psum_scatter(kernel_terms, 'rows', scatter_dimension=2, tiled=True)]
    slice x4 -> x18, local copies, waits for them, and re-layouts: 4.11 us -> 142 us  [windows(): source[p:p + height:2, q:q + columns:2].reshape(height * columns // 4, half)]
    all_gather x2 -> x1, waiting for transfers between devices: 92.5 us -> 15.5 us  [local(): act = lax.all_gather(activated, 'filt', axis=0, tiled=True)]
    psum x1 -> x0, waiting for transfers between devices: 58 us -> none  [local(): kernel_grad = lax.psum(summed, 'rep')]
    dot_general x27 -> x3, matrix products: 46.3 us -> 4.13 us  [the longest x1 1.65 us: local(): conv = conv + jnp.dot(fine, kernel_flat, preferred_element_type=jnp.float32)]
    all_to_all x0 -> x1, blocking collectives: none -> 24.3 us  [local(): lax.all_to_all(copies, 'rows', 0, 0, tiled=True)]
    all_to_all x0 -> x2, starting transfers between devices: none -> 12.5 us  [the longest x1 7.82 us: local(): conv = lax.all_to_all(conv, 'rows', 0, 0, tiled=True)]
    ppermute x4 -> x5, starting transfers between devices: 12.3 us -> 23.4 us  [the longest x4 20.4 us: swap_tiles(): return (lax.ppermute(same, AXES, stay), lax.ppermute(other, AXES, cross))]
  transfers between devices with their start and end apart: 9 -> 8, of which waited for: 8 -> 5; matrix products, arithmetic and copies ran while one was open for 13% -> 57% of each run, Pallas kernels for 0% -> 0%
where the time goes in v1:
time: 284 us; the launch traced here: 281 us
  local copies, waits for them, and re-layouts  157 us (55%)
  starting transfers between devices  35.9 us (13%)
  waiting for transfers between devices  32.4 us (11%)
  blocking collectives  24.3 us (9%)
  between operations  14.6 us (5%)
  matrix products  9.81 us (3%)
  other arithmetic  7.49 us (3%)
    slice x18, local copies, waits for them, and re-layouts, windows(): source[p:p + height:2, q:q + columns:2].reshape(height * columns // 4, half)  142 us
    all_to_all x1, blocking collectives, local(): lax.all_to_all(copies, 'rows', 0, 0, tiled=True)  24.3 us
    ppermute x4, starting transfers between devices, swap_tiles(): return (lax.ppermute(same, AXES, stay), lax.ppermute(other, AXES, cross))  20.4 us
    all_gather x1, waiting for transfers between devices, local(): act = lax.all_gather(activated, 'filt', axis=0, tiled=True)  15.5 us
    all_to_all x1, waiting for transfers between devices, local(): conv = lax.all_to_all(conv, 'rows', 0, 0, tiled=True)  9.35 us
    all_to_all x1, starting transfers between devices, local(): conv = lax.all_to_all(conv, 'rows', 0, 0, tiled=True)  7.82 us
    unnamed x44, local copies, waits for them, and re-layouts  5.98 us
    ppermute x4, waiting for transfers between devices, swap_tiles(): return (lax.ppermute(same, AXES, stay), lax.ppermute(other, AXES, cross))  5.9 us
  transfers between devices with their start and end apart: 8, of which 5 were waited for; matrix products, arithmetic and copies ran while one was open for 57% of the time, Pallas kernels for 0%

profile of v1, /device:TPU:56, one launch (start us, length us, event | category | flops | bytes accessed | tf_op | source)
XLA Modules:
  0.0 281.3 jit_solution(7874803419722778057)
XLA Ops:
  7.2 0.9 broadcast_in_dim.23
  8.1 24.3 %all_to_all.15 = bf16[16,2,32,256]{3,2,1,0:T(8,128)(2,1)S(1)} all-to-all(bf16[16,2,32,256]{3,2,1,0:T(8,128)(2,1)S(1)} %broadcast_in_dim.23), channel_id=1, replica_groups=mesh['filt'=8,'rows'=16,'rep'=2] {'rows'}, dimensions={0} | all-to-all | bytes 1048576 | tf_op jit(solution)/shard_map/all_to_all | solution.py:50
  32.6 0.8 broadcast_in_dim.24
  34.5 1.3 copy.28
  36.0 5.7 %multiply_convert_fusion = bf16[64,8,9,128]{3,1,2,0:T(8,128)(2,1)S(1)} fusion(bf16[3,3,128,256]{3,2,1,0:T(8,128)(2,1)S(1)} %copy-done, bf16[64,1,7,2,256]{4,2,3,0,1:T(8,128)(2,1)S(1)} %slice.126, bf16[64,1,8,9,256]{4,2,3,0,1:T(8,128)(2,1)S(1)} %copy.28, pred[8,9]{0,1:T(8,128)(4,1)S(1)} %copy-done.13), kind=kOutput, calls=%fused_computation.12 | convolution fusion | flops 2700017664 | bytes 4587592 | tf_op jit(solution)/shard_map/conv_general_dilated | solution.py:53
  42.1 1.6 copy.30
  43.8 4.7 %all-to-all-start.2 = ((bf16[64,64,128]{2,1,0:T(8,128)(2,1)}), bf16[64,64,128]{2,1,0:T(8,128)(2,1)S(1)}, u32[]{:S(2)}, u32[]{:S(2)}) async-start(bf16[64,64,128]{2,1,0:T(8,128)(2,1)} %copy.30), calls=%async_computation.2 | async-start | bytes 2097152 | tf_op jit(solution)/shard_map/all_to_all | solution.py:62
  48.5 2.1 collective-permute-start
  50.6 8.4 %collective-permute-start.1 = (bf16[320,128]{1,0:T(8,128)(2,1)S(1)}, bf16[320,128]{1,0:T(8,128)(2,1)S(1)}, u32[]{:S(2)}, u32[]{:S(2)}) collective-permute-start(bf16[320,128]{1,0:T(8,128)(2,1)S(1)} %get-tuple-element.9), channel_id=1, source_target_pairs={{0,0},{1,1},{2,2},{3,3},{4,32},{5,33},{6,34},{7,35},{8,64},{9,65},... | collective-permute-start | bytes 245768 | tf_op jit(solution)/shard_map/ppermute | solution.py:19
  59.0 3.3 %collective-permute-done = bf16[320,128]{1,0:T(8,128)(2,1)S(1)} collective-permute-done((bf16[320,128]{1,0:T(8,128)(2,1)S(1)}, bf16[320,128]{1,0:T(8,128)(2,1)S(1)}, u32[]{:S(2)}, u32[]{:S(2)}) %collective-permute-start) | collective-permute-done | bytes 81952 | tf_op jit(solution)/shard_map/ppermute | solution.py:19
  62.4 2.5 collective-permute-done.1
  65.6 0.7 copy.24
  67.1 5.0 %collective-permute-start.2 = (bf16[256,128]{1,0:T(8,128)(2,1)}, bf16[256,128]{1,0:T(8,128)(2,1)}, u32[]{:S(2)}, u32[]{:S(2)}) collective-permute-start(bf16[256,128]{1,0:T(8,128)(2,1)} %bitcast.39), channel_id=1, source_target_pairs={{0,2},{1,3},{2,0},{3,1},{4,34},{5,35},{6,32},{7,33},{8,66},{9,67},... | collective-permute-start | bytes 196616 | tf_op jit(solution)/shard_map/ppermute | solution.py:19
  72.7 5.0 %collective-permute-start.3 = (bf16[256,128]{1,0:T(8,128)(2,1)}, bf16[256,128]{1,0:T(8,128)(2,1)}, u32[]{:S(2)}, u32[]{:S(2)}) collective-permute-start(bf16[256,128]{1,0:T(8,128)(2,1)} %bitcast.40), channel_id=1, source_target_pairs={{0,0},{1,1},{2,2},{3,3},{4,32},{5,33},{6,34},{7,35},{8,64},{9,65},... | collective-permute-start | bytes 196616 | tf_op jit(solution)/shard_map/ppermute | solution.py:19
  77.7 15.5 %all-gather.2.cloned.1.call-done = bf16[64,64,128]{2,1,0:T(8,128)(2,1)} async-done(((bf16[8,64,128]{2,1,0:T(8,128)(2,1)}), bf16[64,64,128]{2,1,0:T(8,128)(2,1)}) %all-gather.2.cloned.1.call-update) | async-done | bytes 1048592 | tf_op jit(solution)/shard_map/all_gather | solution.py:47
  93.2 1.5 pad_convert_fusion
  95.4 9.8 %slice.95 = bf16[32,32,128]{2,1,0:T(8,128)(2,1)} slice(bf16[65,65,128]{2,1,0:T(8,128)(2,1)S(1)} %get-tuple-element.4), slice={[0:64:2], [0:64:2], [0:128:1]} | slice | bytes 524288 | tf_op jit(solution)/shard_map/slice | solution.py:81
  105.2 9.7 %slice.96 = bf16[32,32,128]{2,1,0:T(8,128)(2,1)} slice(bf16[65,65,128]{2,1,0:T(8,128)(2,1)S(1)} %get-tuple-element.4), slice={[0:64:2], [1:65:2], [0:128:1]} | slice | bytes 524288 | tf_op jit(solution)/shard_map/slice | solution.py:81
  114.9 9.7 %slice.97 = bf16[32,32,128]{2,1,0:T(8,128)(2,1)} slice(bf16[65,65,128]{2,1,0:T(8,128)(2,1)S(1)} %get-tuple-element.4), slice={[0:64:2], [2:65:2], [0:128:1]} | slice | bytes 524288 | tf_op jit(solution)/shard_map/slice | solution.py:81
  124.6 9.7 %slice.98 = bf16[32,32,128]{2,1,0:T(8,128)(2,1)} slice(bf16[65,65,128]{2,1,0:T(8,128)(2,1)S(1)} %get-tuple-element.4), slice={[1:65:2], [0:64:2], [0:128:1]} | slice | bytes 524288 | tf_op jit(solution)/shard_map/slice | solution.py:81
  134.3 9.7 %slice.99 = bf16[32,32,128]{2,1,0:T(8,128)(2,1)} slice(bf16[65,65,128]{2,1,0:T(8,128)(2,1)S(1)} %get-tuple-element.4), slice={[1:65:2], [1:65:2], [0:128:1]} | slice | bytes 524288 | tf_op jit(solution)/shard_map/slice | solution.py:81
  144.0 9.7 %slice.100 = bf16[32,32,128]{2,1,0:T(8,128)(2,1)} slice(bf16[65,65,128]{2,1,0:T(8,128)(2,1)S(1)} %get-tuple-element.4), slice={[1:65:2], [2:65:2], [0:128:1]} | slice | bytes 524288 | tf_op jit(solution)/shard_map/slice | solution.py:81
  153.8 9.8 %slice.101 = bf16[32,32,128]{2,1,0:T(8,128)(2,1)} slice(bf16[65,65,128]{2,1,0:T(8,128)(2,1)S(1)} %get-tuple-element.4), slice={[2:65:2], [0:64:2], [0:128:1]} | slice | bytes 524288 | tf_op jit(solution)/shard_map/slice | solution.py:81
  163.6 9.8 %slice.102 = bf16[32,32,128]{2,1,0:T(8,128)(2,1)} slice(bf16[65,65,128]{2,1,0:T(8,128)(2,1)S(1)} %get-tuple-element.4), slice={[2:65:2], [1:65:2], [0:128:1]} | slice | bytes 524288 | tf_op jit(solution)/shard_map/slice | solution.py:81
  173.4 9.9 %slice.103 = bf16[32,32,128]{2,1,0:T(8,128)(2,1)} slice(bf16[65,65,128]{2,1,0:T(8,128)(2,1)S(1)} %get-tuple-element.4), slice={[2:65:2], [2:65:2], [0:128:1]} | slice | bytes 524288 | tf_op jit(solution)/shard_map/slice | solution.py:81
  183.3 9.7 %slice.104 = bf16[32,32,128]{2,1,0:T(8,128)(2,1)} slice(bf16[65,65,128]{2,1,0:T(8,128)(2,1)S(1)} %get-tuple-element.3), slice={[0:64:2], [0:64:2], [0:128:1]} | slice | bytes 524288 | tf_op jit(solution)/shard_map/slice | solution.py:81
  193.0 9.7 %slice.105 = bf16[32,32,128]{2,1,0:T(8,128)(2,1)} slice(bf16[65,65,128]{2,1,0:T(8,128)(2,1)S(1)} %get-tuple-element.3), slice={[0:64:2], [1:65:2], [0:128:1]} | slice | bytes 524288 | tf_op jit(solution)/shard_map/slice | solution.py:81
  202.7 9.7 %slice.106 = bf16[32,32,128]{2,1,0:T(8,128)(2,1)} slice(bf16[65,65,128]{2,1,0:T(8,128)(2,1)S(1)} %get-tuple-element.3), slice={[0:64:2], [2:65:2], [0:128:1]} | slice | bytes 524288 | tf_op jit(solution)/shard_map/slice | solution.py:81
  212.5 9.7 %slice.107 = bf16[32,32,128]{2,1,0:T(8,128)(2,1)} slice(bf16[65,65,128]{2,1,0:T(8,128)(2,1)S(1)} %get-tuple-element.3), slice={[1:65:2], [0:64:2], [0:128:1]} | slice | bytes 524288 | tf_op jit(solution)/shard_map/slice | solution.py:81
  222.2 9.7 %slice.108 = bf16[32,32,128]{2,1,0:T(8,128)(2,1)} slice(bf16[65,65,128]{2,1,0:T(8,128)(2,1)S(1)} %get-tuple-element.3), slice={[1:65:2], [1:65:2], [0:128:1]} | slice | bytes 524288 | tf_op jit(solution)/shard_map/slice | solution.py:81
  231.9 0.9 slice.109
  232.8 1.4 slice.110
  234.2 1.4 slice.111
  235.6 1.7 slice.112
  237.4 1.1 constant_dynamic-update-slice_fusion.8
  238.5 1.0 constant_dynamic-update-slice_fusion.7
  239.5 1.0 constant_dynamic-update-slice_fusion.6
  240.5 1.0 constant_dynamic-update-slice_fusion.5
  241.5 1.0 constant_dynamic-update-slice_fusion.4
  242.9 1.6 fusion.22
  244.5 3.0 %collective-permute-start.4 = (bf16[1152,256]{1,0:T(8,128)(2,1)}, bf16[1152,256]{1,0:T(8,128)(2,1)}, u32[]{:S(2)}, u32[]{:S(2)}) collective-permute-start(bf16[1152,256]{1,0:T(8,128)(2,1)} %get-tuple-element.15), channel_id=1, source_target_pairs={{0,1},{1,0},{2,3},{3,2},{4,5},{5,4},{6,7},{7,6},{8,9},{9,8},{10,11... | collective-permute-start | bytes 1769480 | tf_op jit(solution)/shard_map/ppermute | solution.py:93
  247.6 0.8 fusion.23
  249.1 1.6 fusion.11
  250.8 7.8 %all-to-all-start = ((bf16[32,32,256]{2,1,0:T(8,128)(2,1)}), bf16[32,32,256]{2,1,0:T(8,128)(2,1)S(1)}, u32[]{:S(2)}, u32[]{:S(2)}) async-start(bf16[32,32,256]{2,1,0:T(8,128)(2,1)} %bitcast.25), calls=%async_computation | async-start | bytes 1048576 | tf_op jit(solution)/shard_map/all_to_all | solution.py:99
  258.9 0.9 broadcast_select_fusion.5
  260.5 1.7 collective-permute-done.4
  262.2 2.2 convert_add_fusion
  264.4 9.3 %all-to-all-done = bf16[32,32,256]{2,1,0:T(8,128)(2,1)S(1)} async-done(((bf16[32,32,256]{2,1,0:T(8,128)(2,1)}), bf16[32,32,256]{2,1,0:T(8,128)(2,1)S(1)}, u32[]{:S(2)}, u32[]{:S(2)}) %all-to-all-start) | async-done | bytes 524320 | tf_op jit(solution)/shard_map/all_to_all | solution.py:99
  (72 shorter events, 7.3 us)
Async XLA Ops:
  7.2 28.9 %copy-start = (bf16[3,3,128,256]{3,2,1,0:T(8,128)(2,1)S(1)}, bf16[3,3,128,256]{3,2,1,0:T(8,128)(2,1)}, u32[]{:S(2)}) copy-start(bf16[3,3,128,256]{3,2,1,0:T(8,128)(2,1)} %param.4) | copy-start | bytes 1769476
  34.5 1.5 copy-start.13
  42.1 6.4 %copy-start.10 = (bf16[1,4,64,256]{3,2,1,0:T(8,128)(2,1)S(1)}, bf16[1,4,64,256]{3,2,1,0:T(8,128)(2,1)}, u32[]{:S(2)}) copy-start(bf16[1,4,64,256]{3,2,1,0:T(8,128)(2,1)} %param.3) | copy-start | bytes 393220
  42.1 6.4 %copy-start.12 = (bf16[1,2,32,256]{3,2,1,0:T(8,128)(2,1)S(1)}, bf16[1,2,32,256]{3,2,1,0:T(8,128)(2,1)}, u32[]{:S(2)}) copy-start(bf16[1,2,32,256]{3,2,1,0:T(8,128)(2,1)} %param.5) | copy-start | bytes 98308
  43.8 21.3 %all-to-all-start.2 = ((bf16[64,64,128]{2,1,0:T(8,128)(2,1)}), bf16[64,64,128]{2,1,0:T(8,128)(2,1)S(1)}, u32[]{:S(2)}, u32[]{:S(2)}) async-start(bf16[64,64,128]{2,1,0:T(8,128)(2,1)} %copy.30), calls=%async_computation.2 | async-start | bytes 2097152 | tf_op jit(solution)/shard_map/all_to_all | solution.py:62
  48.5 44.7 %all-gather.2.cloned.1.call-start = ((), (), s32[]{:S(2)}) async-start(), calls=%async_computation.3 | async-start | bytes 1179648 | tf_op jit(solution)/shard_map/all_gather | solution.py:47
  48.5 13.8 %collective-permute-start = (bf16[320,128]{1,0:T(8,128)(2,1)S(1)}, bf16[320,128]{1,0:T(8,128)(2,1)S(1)}, u32[]{:S(2)}, u32[]{:S(2)}) collective-permute-start(bf16[320,128]{1,0:T(8,128)(2,1)S(1)} %get-tuple-element.10), channel_id=1, source_target_pairs={{0,2},{1,3},{2,0},{3,1},{4,34},{5,35},{6,32},{7,33},{8,66},{9,67},... | collective-permute-start | bytes 245768 | tf_op jit(solution)/shard_map/ppermute | solution.py:19
  50.6 14.3 %collective-permute-start.1 = (bf16[320,128]{1,0:T(8,128)(2,1)S(1)}, bf16[320,128]{1,0:T(8,128)(2,1)S(1)}, u32[]{:S(2)}, u32[]{:S(2)}) collective-permute-start(bf16[320,128]{1,0:T(8,128)(2,1)S(1)} %get-tuple-element.9), channel_id=1, source_target_pairs={{0,0},{1,1},{2,2},{3,3},{4,32},{5,33},{6,34},{7,35},{8,64},{9,65},... | collective-permute-start | bytes 245768 | tf_op jit(solution)/shard_map/ppermute | solution.py:19
  67.1 191.8 %collective-permute-start.2 = (bf16[256,128]{1,0:T(8,128)(2,1)}, bf16[256,128]{1,0:T(8,128)(2,1)}, u32[]{:S(2)}, u32[]{:S(2)}) collective-permute-start(bf16[256,128]{1,0:T(8,128)(2,1)} %bitcast.39), channel_id=1, source_target_pairs={{0,2},{1,3},{2,0},{3,1},{4,34},{5,35},{6,32},{7,33},{8,66},{9,67},... | collective-permute-start | bytes 196616 | tf_op jit(solution)/shard_map/ppermute | solution.py:19
  72.7 186.2 %collective-permute-start.3 = (bf16[256,128]{1,0:T(8,128)(2,1)}, bf16[256,128]{1,0:T(8,128)(2,1)}, u32[]{:S(2)}, u32[]{:S(2)}) collective-permute-start(bf16[256,128]{1,0:T(8,128)(2,1)} %bitcast.40), channel_id=1, source_target_pairs={{0,0},{1,1},{2,2},{3,3},{4,32},{5,33},{6,34},{7,35},{8,64},{9,65},... | collective-permute-start | bytes 196616 | tf_op jit(solution)/shard_map/ppermute | solution.py:19
  237.4 5.2 %copy-start.9 = (bf16[32,32,128]{2,1,0:T(8,128)(2,1)S(1)}, bf16[32,32,128]{2,1,0:T(8,128)(2,1)}, u32[]{:S(2)}) copy-start(bf16[32,32,128]{2,1,0:T(8,128)(2,1)} %slice.100) | copy-start | bytes 786436
  237.4 5.3 %copy-start.8 = (bf16[32,32,128]{2,1,0:T(8,128)(2,1)S(1)}, bf16[32,32,128]{2,1,0:T(8,128)(2,1)}, u32[]{:S(2)}) copy-start(bf16[32,32,128]{2,1,0:T(8,128)(2,1)} %slice.101) | copy-start | bytes 786436
  237.4 5.3 %copy-start.7 = (bf16[32,32,128]{2,1,0:T(8,128)(2,1)S(1)}, bf16[32,32,128]{2,1,0:T(8,128)(2,1)}, u32[]{:S(2)}) copy-start(bf16[32,32,128]{2,1,0:T(8,128)(2,1)} %slice.102) | copy-start | bytes 786436
  237.4 5.4 %copy-start.6 = (bf16[32,32,128]{2,1,0:T(8,128)(2,1)S(1)}, bf16[32,32,128]{2,1,0:T(8,128)(2,1)}, u32[]{:S(2)}) copy-start(bf16[32,32,128]{2,1,0:T(8,128)(2,1)} %slice.103) | copy-start | bytes 786436
  242.9 4.6 %copy-start.5 = (bf16[32,32,128]{2,1,0:T(8,128)(2,1)S(1)}, bf16[32,32,128]{2,1,0:T(8,128)(2,1)}, u32[]{:S(2)}) copy-start(bf16[32,32,128]{2,1,0:T(8,128)(2,1)} %slice.104) | copy-start | bytes 786436
  244.5 17.6 %collective-permute-start.4 = (bf16[1152,256]{1,0:T(8,128)(2,1)}, bf16[1152,256]{1,0:T(8,128)(2,1)}, u32[]{:S(2)}, u32[]{:S(2)}) collective-permute-start(bf16[1152,256]{1,0:T(8,128)(2,1)} %get-tuple-element.15), channel_id=1, source_target_pairs={{0,1},{1,0},{2,3},{3,2},{4,5},{5,4},{6,7},{7,6},{8,9},{9,8},{10,11... | collective-permute-start | bytes 1769480 | tf_op jit(solution)/shard_map/ppermute | solution.py:93
  247.6 1.0 copy-start.4
  247.6 1.0 copy-start.3
  247.6 1.1 copy-start.2
  247.6 1.2 copy-start.1
  249.1 9.5 %copy-start.11 = (bf16[1,4,64,256]{3,2,1,0:T(8,128)(2,1)S(1)}, bf16[1,4,64,256]{3,2,1,0:T(8,128)(2,1)}, u32[]{:S(2)}) copy-start(bf16[1,4,64,256]{3,2,1,0:T(8,128)(2,1)} %param.3) | copy-start | bytes 393220
  250.8 22.9 %all-to-all-start = ((bf16[32,32,256]{2,1,0:T(8,128)(2,1)}), bf16[32,32,256]{2,1,0:T(8,128)(2,1)S(1)}, u32[]{:S(2)}, u32[]{:S(2)}) async-start(bf16[32,32,256]{2,1,0:T(8,128)(2,1)} %bitcast.25), calls=%async_computation | async-start | bytes 1048576 | tf_op jit(solution)/shard_map/all_to_all | solution.py:99
Sparse Core Ops, SparseCore 0:
  66.5 26.6 all-gather.1

commit v2 on v1

v2 whole, which is shorter than its diff:
```python
import jax
import jax.numpy as jnp
from jax import lax
from jax.experimental import pallas as pl
from jax.experimental.pallas import tpu as pltpu
from jax.sharding import PartitionSpec as P

AXES = ("filt", "rows", "rep")
VMEM = pl.BlockSpec(memory_space=pltpu.VMEM)
SMEM = pl.BlockSpec(memory_space=pltpu.SMEM)
F32 = jnp.float32
BF16 = jnp.bfloat16


def call(body, outs, scratch, scalars, *args):
    return pl.pallas_call(
        body,
        out_shape=[jax.ShapeDtypeStruct(shape, dtype) for shape, dtype in outs],
        in_specs=[SMEM] * scalars + [VMEM] * (len(args) - scalars),
        out_specs=[VMEM] * len(outs),
        scratch_shapes=scratch,
        compiler_params=pltpu.CompilerParams(vmem_limit_bytes=48 << 20),
        name=body.__name__,
    )(*args)


def swap_tiles(pair):
    sizes = [lax.axis_size(axis) for axis in AXES]
    stay, cross = [], []
    for f in range(sizes[0]):
        for r in range(sizes[1]):
            for g in range(sizes[2]):
                a, h = r // 2, r % 2
                source = (f * sizes[1] + r) * sizes[2] + g
                stay.append((source, (a * sizes[1] + 2 * f + h) * sizes[2] + g))
                cross.append((source, (a * sizes[1] + 2 * f + 1 - h) * sizes[2] + g))
    return lax.ppermute(pair[0], AXES, stay), lax.ppermute(pair[1], AXES, cross)


def split_tile(odd_ref, feat_ref, cot_ref, same_ref, other_ref, copies_ref, cells_ref, wide_ref):
    odd = odd_ref[0] == 1
    rows, columns, channels = feat_ref.shape
    half, cells = channels // 2, columns // 2
    for part in range(2):
        wide_ref[part] = feat_ref[:, :, part * half : (part + 1) * half].astype(F32)
    for m in range(rows // 2):
        totals = [jnp.zeros((cells, half), F32)] * 2
        for a in range(2):
            for b in range(2):
                low, high = (wide_ref[part, 2 * m + a, pl.ds(b, cells, stride=2), :] for part in range(2))
                totals = [totals[0] + low, totals[1] + high]
                same_ref[4 * m + 2 * a + b] = jnp.where(odd, high, low).astype(BF16)
                other_ref[4 * m + 2 * a + b] = jnp.where(odd, low, high).astype(BF16)
        cells_ref[m, :, :half] = totals[0]
        cells_ref[m, :, half:] = totals[1]
        grad = cot_ref[m].astype(F32)
        low, high = grad[:, :half], grad[:, half:]
        same_ref[2 * rows + m] = jnp.where(odd, high, low).astype(BF16)
        other_ref[2 * rows + m] = jnp.where(odd, low, high).astype(BF16)
    for k in range(copies_ref.shape[0]):
        copies_ref[k] = cot_ref[...]


def activate(odd_ref, same_ref, other_ref, act_ref, slope_ref, up_ref):
    odd = odd_ref[0] == 1
    count, cells, half = same_ref.shape
    planes = act_ref.shape[0] // 2
    same, other = same_ref[...].astype(F32), other_ref[...].astype(F32)
    first, second = jnp.where(odd, other, same), jnp.where(odd, same, other)
    for t, tile in enumerate((first, second)):
        values = tile[:planes]
        logistic = 1.0 / (1.0 + jnp.exp(-values))
        act_ref[t * planes : (t + 1) * planes] = (values * logistic).astype(BF16)
        slope_ref[t * planes : (t + 1) * planes] = logistic * (1.0 + values * (1.0 - logistic))
        up_ref[t * (planes // 4) : (t + 1) * (planes // 4)] = tile[planes:] * 0.25


def back_conv(cot_ref, kernel_ref, out_ref, left_ref, right_ref):
    height, cells, channels = cot_ref.shape
    half = out_ref.shape[-1]
    tokens = height * cells
    column = lax.broadcasted_iota(jnp.int32, (tokens, channels), 0) % cells
    wide = cot_ref[...].astype(F32).reshape(tokens, channels)
    before = jnp.where(column == 0, 0.0, pltpu.roll(wide, 1, 0)).astype(BF16)
    after = jnp.where(column == cells - 1, 0.0, pltpu.roll(wide, tokens - 1, 0)).astype(BF16)
    blank = jnp.zeros((cells, 4 * channels), BF16)
    left_ref[0:cells] = blank
    left_ref[tokens + cells : tokens + 2 * cells] = blank
    middle = pl.ds(cells, tokens)
    center = cot_ref[...].reshape(tokens, channels)
    left_ref[middle, 0:channels] = center
    left_ref[middle, channels : 2 * channels] = center
    left_ref[middle, 2 * channels : 3 * channels] = before
    left_ref[middle, 3 * channels : 4 * channels] = after
    empty = jnp.zeros((half, channels), BF16)
    for p in range(3):
        taps = [kernel_ref[(3 * p + q) * half : (3 * p + q + 1) * half, :] for q in range(3)]
        blocks = ((taps[0], taps[1]), (taps[1], taps[2]), (taps[2], empty), (empty, taps[0]))
        for k, block in enumerate(blocks):
            for b in range(2):
                right_ref[p, b * half : (b + 1) * half, k * channels : (k + 1) * channels] = block[b]
    for a in range(2):
        total = None
        for p in range(3):
            start = cells * (1 + ((0, 0, -1), (1, 0, 0))[a][p])
            term = lax.dot_general(
                left_ref[start : start + tokens, :],
                right_ref[p],
                (((1,), (1,)), ((), ())),
                preferred_element_type=F32,
            )
            total = term if total is None else total + term
        total = (total * 0.25).astype(BF16).reshape(height, cells, 2 * half)
        for b in range(2):
            out_ref[:, a, b] = total[:, :, b * half : (b + 1) * half]


def forward_and_kernel(act_ref, cot_ref, kernel_ref, conv_ref, keep_ref, send_ref, coarse_ref, fine_ref):
    height, _, _, cells, half = act_ref.shape
    column = lax.broadcasted_iota(jnp.int32, (cells, half), 0)

    def plane(i, a, b):
        return act_ref[i, a, b].astype(F32)

    def put(i, p, even, odd):
        before = jnp.where(column == 0, 0.0, pltpu.roll(odd, 1, 0))
        after = jnp.where(column == cells - 1, 0.0, pltpu.roll(even, cells - 1, 0))
        rows = pl.ds(pl.multiple_of(i * cells, cells), cells)
        return rows, (before + even, even + odd, odd + after)

    def store(rows, p, sums):
        for q, box in enumerate(sums):
            coarse = box.astype(BF16)
            lanes = slice((3 * p + q) * half, (3 * p + q + 1) * half)
            coarse_ref[rows, lanes] = coarse
            fine_ref[rows, lanes] = (box - coarse.astype(F32)).astype(BF16)

    rows, sums = put(0, 0, plane(0, 0, 0), plane(0, 0, 1))
    store(rows, 0, sums)
    rows, sums = put(height - 1, 2, plane(height - 1, 1, 0), plane(height - 1, 1, 1))
    store(rows, 2, sums)

    def whole(i, _):
        rows, sums = put(i, 1, plane(i, 0, 0) + plane(i, 1, 0), plane(i, 0, 1) + plane(i, 1, 1))
        store(rows, 1, sums)
        return 0

    def between(i, _):
        rows, sums = put(
            i, 0, plane(i - 1, 1, 0) + plane(i, 0, 0), plane(i - 1, 1, 1) + plane(i, 0, 1)
        )
        store(rows, 0, sums)
        store(pl.ds(pl.multiple_of((i - 1) * cells, cells), cells), 2, sums)
        return 0

    lax.fori_loop(0, height, whole, 0, unroll=4)
    lax.fori_loop(1, height, between, 0, unroll=4)

    tokens = height * cells
    grad = lax.dot_general(
        coarse_ref[...],
        cot_ref[...].reshape(tokens, -1),
        (((0,), (0,)), ((), ())),
        preferred_element_type=F32,
    ) * 0.25
    keep_ref[...] = grad
    send_ref[...] = grad.astype(BF16)
    conv = jnp.dot(coarse_ref[...], kernel_ref[...], preferred_element_type=F32)
    conv = conv + jnp.dot(fine_ref[...], kernel_ref[...], preferred_element_type=F32)
    conv_ref[...] = conv.astype(BF16).reshape(conv_ref.shape)


def input_side(odd_ref, back_ref, slope_ref, up_ref, same_ref, other_ref):
    odd = odd_ref[0] == 1
    planes = same_ref.shape[0]
    grads = []
    for t in range(2):
        block = slice(t * planes, (t + 1) * planes)
        total = back_ref[0, block].astype(F32)
        for k in range(1, back_ref.shape[0]):
            total = total + back_ref[k, block].astype(F32)
        total = total * slope_ref[block]
        up = up_ref[t * (planes // 4) : (t + 1) * (planes // 4)]
        grads.append([total[k] + up[k // 4] for k in range(planes)])
    for k in range(planes):
        same_ref[k] = jnp.where(odd, grads[1][k], grads[0][k]).astype(BF16)
        other_ref[k] = jnp.where(odd, grads[0][k], grads[1][k]).astype(BF16)


def join_tile(odd_ref, same_ref, other_ref, out_ref, low_ref, high_ref):
    odd = odd_ref[0] == 1
    rows, columns, channels = out_ref.shape
    half = channels // 2
    for k in range(2 * rows):
        row, b = 2 * (k // 4) + (k // 2) % 2, k % 2
        same, other = same_ref[k].astype(F32), other_ref[k].astype(F32)
        low_ref[row, pl.ds(b, columns // 2, stride=2), :] = jnp.where(odd, other, same)
        high_ref[row, pl.ds(b, columns // 2, stride=2), :] = jnp.where(odd, same, other)
    out_ref[:, :, :half] = low_ref[...].astype(BF16)
    out_ref[:, :, half:] = high_ref[...].astype(BF16)


def local(features, kernel, cotangent):
    tile_rows, columns, channels = features.shape[1:]
    half, cells = channels // 2, columns // 2
    filt_count, row_count = lax.axis_size("filt"), lax.axis_size("rows")
    height = tile_rows * row_count // 2
    odd = (lax.axis_index("rows") % 2).astype(jnp.int32).reshape(1)
    kernel_flat = kernel.reshape(9 * half, channels)
    planes = 2 * tile_rows

    packed = planes + tile_rows // 2
    same, other, copies, cell_sums = call(
        split_tile,
        [
            ((packed, cells, half), BF16),
            ((packed, cells, half), BF16),
            ((row_count,) + cotangent.shape[1:], BF16),
            ((tile_rows // 2, cells, channels), F32),
        ],
        [pltpu.VMEM((2, tile_rows, columns, half), F32)],
        1,
        odd,
        features[0],
        cotangent[0],
    )
    same, other = swap_tiles((same, other))
    cot = lax.all_to_all(copies, "rows", 0, 0, tiled=True).reshape(height, cells, channels)
    act, slope, up = call(
        activate,
        [
            ((2 * planes, cells, half), BF16),
            ((2 * planes, cells, half), F32),
            ((tile_rows, cells, half), F32),
        ],
        [],
        1,
        odd,
        same,
        other,
    )
    act = lax.all_gather(act, "filt", axis=0, tiled=True).reshape(height, 2, 2, cells, half)

    (back,) = call(
        back_conv,
        [((height, 2, 2, cells, half), BF16)],
        [
            pltpu.VMEM(((height + 2) * cells, 4 * channels), BF16),
            pltpu.VMEM((3, 2 * half, 4 * channels), BF16),
        ],
        0,
        cot,
        kernel_flat,
    )
    back = lax.all_to_all(back, "filt", 0, 0, tiled=True)
    conv, kernel_term, outgoing = call(
        forward_and_kernel,
        [
            ((height, cells, channels), BF16),
            ((9 * half, channels), F32),
            ((9 * half, channels), BF16),
        ],
        [
            pltpu.VMEM((height * cells, 9 * half), BF16),
            pltpu.VMEM((height * cells, 9 * half), BF16),
        ],
        0,
        act,
        cot,
        kernel_flat,
    )
    arrived = lax.ppermute(outgoing, "rep", [(0, 1), (1, 0)])
    conv = lax.all_to_all(conv, "rows", 0, 0, tiled=True)

    same, other = call(
        input_side,
        [((planes, cells, half), BF16), ((planes, cells, half), BF16)],
        [],
        1,
        odd,
        back.reshape(filt_count, 2 * planes, cells, half),
        slope,
        up,
    )
    same, other = swap_tiles((same, other))
    (input_grad,) = call(
        join_tile,
        [(features.shape[1:], BF16)],
        [pltpu.VMEM((tile_rows, columns, half), F32)] * 2,
        1,
        odd,
        same,
        other,
    )
    kernel_grad = (kernel_term + arrived.astype(F32)).reshape(kernel.shape)
    conv = conv.reshape(row_count, tile_rows // 2, cells, channels).astype(F32).sum(axis=0)
    pooled = ((cell_sums + conv) * 0.25).astype(BF16)
    return (pooled[None], input_grad[None], kernel_grad)


def solution(mesh):
    tiles = P("rep", "rows", None, "filt")
    weights = P(None, None, "rows", "filt")
    return jax.shard_map(
        local,
        mesh=mesh,
        in_specs=(tiles, weights, tiles),
        out_specs=(tiles, tiles, weights),
        check_vma=False,
    )
```

time: 284 us -> 114 us (0.40)
  local copies, waits for them, and re-layouts: 157 us -> 4.46 us
  Pallas kernels: 0 us -> 9.82 us
  matrix products: 9.81 us -> 0 us
  blocking collectives: 24.3 us -> 19 us
  other arithmetic: 7.49 us -> 2.9 us
    slice x18 -> x0, local copies, waits for them, and re-layouts: 142 us -> none  [windows(): source[p:p + height:2, q:q + columns:2].reshape(height * columns // 4, half)]
    ppermute x5, waiting for transfers between devices: 7.56 us -> 24.2 us  [the longest x2 16.3 us: swap_tiles(): lax.ppermute(pair[0], AXES, stay)]
    all_gather x1, waiting for transfers between devices: 15.5 us -> 0.01 us  [local(): lax.all_gather(act, 'filt', axis=0, tiled=True)]
    pallas_call x0 -> x6, Pallas kernels: none -> 9.82 us  [call(): pl.pallas_call(body, out_shape=[jax.ShapeDtypeStruct(shape, dtype) for sh...]
    all_to_all x1, waiting for transfers between devices: 9.35 us -> 0.01 us  [local(): conv = lax.all_to_all(conv, 'rows', 0, 0, tiled=True)]
    conv_general_dilated x1 -> x0, matrix products: 5.68 us -> none  [local(): lax.conv_general_dilated(up, kernel[::-1, ::-1], (1, 1), ((1, 1), (1, 1))...]
    all_to_all x1, waiting for transfers between devices: 0.01 us -> 5.49 us  [local(): back = lax.all_to_all(back, 'filt', 0, 0, tiled=True)]
    all_to_all x1, blocking collectives: 24.3 us -> 19 us  [local(): lax.all_to_all(copies, 'rows', 0, 0, tiled=True)]
  transfers between devices with their start and end apart: 8 -> 8, of which waited for: 5 -> 5; matrix products, arithmetic and copies ran while one was open for 57% -> 2% of each run, Pallas kernels for 0% -> 8%
where the time goes in v2:
time: 114 us; the launch traced here: 113 us
  starting transfers between devices  33.2 us (29%)
  waiting for transfers between devices  29.7 us (26%)
  blocking collectives  19 us (17%)
  between operations  14.1 us (12%)
  Pallas kernels  9.82 us (9%)
  local copies, waits for them, and re-layouts  4.46 us (4%)
  other arithmetic  2.9 us (3%)
    all_to_all x1, blocking collectives, local(): lax.all_to_all(copies, 'rows', 0, 0, tiled=True)  19 us
    ppermute x2, starting transfers between devices, swap_tiles(): lax.ppermute(pair[0], AXES, stay)  17.6 us
    ppermute x2, waiting for transfers between devices, swap_tiles(): lax.ppermute(pair[0], AXES, stay)  16.3 us
    pallas_call x6, Pallas kernels, call(): pl.pallas_call(body, out_shape=[jax.ShapeDtypeStruct(shape, dtype) for sh...  9.82 us
    ppermute x2, waiting for transfers between devices, swap_tiles(): lax.ppermute(pair[1], AXES, cross)  7.88 us
    all_to_all x1, starting transfers between devices, local(): back = lax.all_to_all(back, 'filt', 0, 0, tiled=True)  6.09 us
    all_to_all x1, waiting for transfers between devices, local(): back = lax.all_to_all(back, 'filt', 0, 0, tiled=True)  5.49 us
    all_to_all x1, starting transfers between devices, local(): conv = lax.all_to_all(conv, 'rows', 0, 0, tiled=True)  5.27 us
  transfers between devices with their start and end apart: 8, of which 5 were waited for; matrix products, arithmetic and copies ran while one was open for 2% of the time, Pallas kernels for 8%

profile of v2, /device:TPU:56, one launch (start us, length us, event | category | flops | bytes accessed | tf_op | source)
XLA Modules:
  0.0 113.2 jit_solution(17697961228774964220)
XLA Ops:
  7.2 0.0 copy-start
  7.2 0.0 all-gather.2.cloned.1.call-start
  7.2 0.0 copy-start.5
  7.2 0.9 copy-done.5
  8.2 0.0 copy-start.6
  8.2 0.8 copy-done.6
  8.9 0.1 split_tile.1
  9.0 8.8 %collective-permute-start = (bf16[10,32,128]{2,1,0:T(8,128)(2,1)S(1)}, bf16[10,32,128]{2,1,0:T(8,128)(2,1)S(1)}, u32[]{:S(2)}, u32[]{:S(2)}) collective-permute-start(bf16[10,32,128]{2,1,0:T(8,128)(2,1)S(1)} %get-tuple-element.16), channel_id=1, source_target_pairs={{0,0},{1,1},{2,2},{3,3},{4,32},{5,33},{6,34},{7,35},{8,64},{9,65},... | collective-permute-start | bytes 245768 | tf_op jit(solution)/shard_map/ppermute | solution.py:37
  17.8 0.8 collective-permute-start.1
  18.6 4.2 %collective-permute-done.same_ref = bf16[10,32,128]{2,1,0:T(8,128)(2,1)S(1)} collective-permute-done((bf16[10,32,128]{2,1,0:T(8,128)(2,1)S(1)}, bf16[10,32,128]{2,1,0:T(8,128)(2,1)S(1)}, u32[]{:S(2)}, u32[]{:S(2)}) %collective-permute-start) | collective-permute-done | bytes 81952 | tf_op jit(solution)/shard_map/ppermute | solution.py:37
  22.8 5.9 %collective-permute-done.1.other_ref = bf16[10,32,128]{2,1,0:T(8,128)(2,1)S(1)} collective-permute-done((bf16[10,32,128]{2,1,0:T(8,128)(2,1)S(1)}, bf16[10,32,128]{2,1,0:T(8,128)(2,1)S(1)}, u32[]{:S(2)}, u32[]{:S(2)}) %collective-permute-start.1) | collective-permute-done | bytes 81952 | tf_op jit(solution)/shard_map/ppermute | solution.py:37
  28.7 0.8 activate.1
  29.5 0.0 copy-start.3
  29.5 0.7 copy-done.3
  30.2 0.0 all-gather.2.cloned.1.call-update
  30.3 19.0 %all_to_all.15 = bf16[16,2,32,256]{3,2,1,0:T(8,128)(2,1)S(1)} all-to-all(bf16[16,2,32,256]{3,2,1,0:T(8,128)(2,1)S(1)} %get-tuple-element.19), channel_id=1, replica_groups=mesh['filt'=8,'rows'=16,'rep'=2] {'rows'}, dimensions={0} | all-to-all | bytes 1048576 | tf_op jit(solution)/shard_map/all_to_all | solution.py:228
  49.3 0.0 copy-done
  49.3 4.4 %back_conv.1 = bf16[32,2,2,32,128]{4,3,2,1,0:T(8,128)(2,1)} custom-call(bf16[32,32,256]{2,1,0:T(8,128)(2,1)S(1)} %bitcast.13, bf16[1152,256]{1,0:T(8,128)(2,1)S(1)} %bitcast.16), custom_call_target="tpu_custom_call" | custom-call | tf_op jit(solution)/shard_map/back_conv/pallas_call | solution.py:16
  53.7 6.1 %all-to-all-start.2 = ((bf16[32,2,2,32,128]{4,3,2,1,0:T(8,128)(2,1)}), bf16[32,2,2,32,128]{4,3,2,1,0:T(8,128)(2,1)S(1)}, u32[]{:S(2)}, u32[]{:S(2)}) async-start(bf16[32,2,2,32,128]{4,3,2,1,0:T(8,128)(2,1)} %back_conv.1), calls=%async_computation.2 | async-start | bytes 2097152 | tf_op jit(solution)/shard_map/all_to_all | solution.py:255
  59.8 0.0 all-gather.2.cloned.1.call-done
  59.8 0.0 copy-start.1
  59.8 1.2 %copy-done.1 = bf16[128,32,128]{2,1,0:T(8,128)(2,1)S(1)} copy-done((bf16[128,32,128]{2,1,0:T(8,128)(2,1)S(1)}, bf16[128,32,128]{2,1,0:T(8,128)(2,1)}, u32[]{:S(2)}) %copy-start.1) | copy-done | bytes 1048600
  61.0 3.7 %forward_and_kernel.1 = (bf16[32,32,256]{2,1,0:T(8,128)(2,1)S(1)}, f32[1152,256]{1,0:T(8,128)S(1)}, bf16[1152,256]{1,0:T(8,128)(2,1)}) custom-call(bf16[32,2,2,32,128]{4,3,2,1,0:T(8,128)(2,1)S(1)} %bitcast.18, bf16[32,32,256]{2,1,0:T(8,128)(2,1)S(1)} %bitcast.14, bf16[1152,256]{1,0:T(8,128)(2,1)S(1)} %bitcast.17), custom_call_target="tpu_custom_call" | custom-call | tf_op jit(solution)/shard_map/forward_and_kernel/pallas_call | solution.py:16
  64.7 0.0 copy-start.2
  64.7 0.8 copy-done.2
  65.5 0.0 copy-start.4
  65.5 2.7 %collective-permute-start.4 = (bf16[1152,256]{1,0:T(8,128)(2,1)}, bf16[1152,256]{1,0:T(8,128)(2,1)}, u32[]{:S(2)}, u32[]{:S(2)}) collective-permute-start(bf16[1152,256]{1,0:T(8,128)(2,1)} %get-tuple-element.26), channel_id=1, source_target_pairs={{0,1},{1,0},{2,3},{3,2},{4,5},{5,4},{6,7},{7,6},{8,9},{9,8},{10,11... | collective-permute-start | bytes 1769480 | tf_op jit(solution)/shard_map/ppermute | solution.py:272
  68.1 5.5 %all-to-all-done.2 = bf16[32,2,2,32,128]{4,3,2,1,0:T(8,128)(2,1)S(1)} async-done(((bf16[32,2,2,32,128]{4,3,2,1,0:T(8,128)(2,1)}), bf16[32,2,2,32,128]{4,3,2,1,0:T(8,128)(2,1)S(1)}, u32[]{:S(2)}, u32[]{:S(2)}) %all-to-all-start.2) | async-done | bytes 1048608 | tf_op jit(solution)/shard_map/all_to_all | solution.py:255
  73.6 5.3 %all-to-all-start.1 = ((bf16[32,32,256]{2,1,0:T(8,128)(2,1)}), bf16[32,32,256]{2,1,0:T(8,128)(2,1)S(1)}, u32[]{:S(2)}, u32[]{:S(2)}) async-start(bf16[32,32,256]{2,1,0:T(8,128)(2,1)} %copy-done.2), calls=%async_computation.1 | async-start | bytes 1048576 | tf_op jit(solution)/shard_map/all_to_all | solution.py:273
  78.9 0.0 copy-done.4
  78.9 0.2 input_side.1
  79.1 8.8 %collective-permute-start.2 = (bf16[8,32,128]{2,1,0:T(8,128)(2,1)S(1)}, bf16[8,32,128]{2,1,0:T(8,128)(2,1)S(1)}, u32[]{:S(2)}, u32[]{:S(2)}) collective-permute-start(bf16[8,32,128]{2,1,0:T(8,128)(2,1)S(1)} %get-tuple-element.23), channel_id=1, source_target_pairs={{0,0},{1,1},{2,2},{3,3},{4,32},{5,33},{6,34},{7,35},{8,64},{9,65},... | collective-permute-start | bytes 196616 | tf_op jit(solution)/shard_map/ppermute | solution.py:37
  87.9 0.8 collective-permute-start.3
  88.7 12.1 %collective-permute-done.2.same_ref = bf16[8,32,128]{2,1,0:T(8,128)(2,1)S(1)} collective-permute-done((bf16[8,32,128]{2,1,0:T(8,128)(2,1)S(1)}, bf16[8,32,128]{2,1,0:T(8,128)(2,1)S(1)}, u32[]{:S(2)}, u32[]{:S(2)}) %collective-permute-start.2) | collective-permute-done | bytes 65568 | tf_op jit(solution)/shard_map/ppermute | solution.py:37
  100.8 2.0 %collective-permute-done.3.other_ref = bf16[8,32,128]{2,1,0:T(8,128)(2,1)S(1)} collective-permute-done((bf16[8,32,128]{2,1,0:T(8,128)(2,1)S(1)}, bf16[8,32,128]{2,1,0:T(8,128)(2,1)S(1)}, u32[]{:S(2)}, u32[]{:S(2)}) %collective-permute-start.3) | collective-permute-done | bytes 65568 | tf_op jit(solution)/shard_map/ppermute | solution.py:37
  102.8 0.7 join_tile.1
  103.5 0.0 collective-permute-done.4
  103.5 2.2 %convert_add_fusion = f32[1152,256]{1,0:T(8,128)} fusion(f32[1152,256]{1,0:T(8,128)S(1)} %get-tuple-element.25, bf16[1152,256]{1,0:T(8,128)(2,1)} %collective-permute-done.4), kind=kLoop, calls=%fused_computation | loop fusion | flops 589824 | bytes 2949120 | tf_op jit(solution)/shard_map/add | solution.py:295
  105.7 0.0 all-to-all-done.1
  105.7 0.1 convert_reduce_fusion
  105.8 0.6 fusion
Async XLA Ops:
  7.2 42.1 %copy-start = (bf16[3,3,128,256]{3,2,1,0:T(8,128)(2,1)S(1)}, bf16[3,3,128,256]{3,2,1,0:T(8,128)(2,1)}, u32[]{:S(2)}) copy-start(bf16[3,3,128,256]{3,2,1,0:T(8,128)(2,1)} %param.4) | copy-start | bytes 1769476
  7.2 52.6 %all-gather.2.cloned.1.call-start = ((), (), s32[]{:S(2)}) async-start(), calls=%async_computation.3 | async-start | bytes 1179648 | tf_op jit(solution)/shard_map/all_gather | solution.py:242
  7.2 1.0 copy-start.5
  8.2 0.8 copy-start.6
  9.0 13.8 %collective-permute-start = (bf16[10,32,128]{2,1,0:T(8,128)(2,1)S(1)}, bf16[10,32,128]{2,1,0:T(8,128)(2,1)S(1)}, u32[]{:S(2)}, u32[]{:S(2)}) collective-permute-start(bf16[10,32,128]{2,1,0:T(8,128)(2,1)S(1)} %get-tuple-element.16), channel_id=1, source_target_pairs={{0,0},{1,1},{2,2},{3,3},{4,32},{5,33},{6,34},{7,35},{8,64},{9,65},... | collective-permute-start | bytes 245768 | tf_op jit(solution)/shard_map/ppermute | solution.py:37
  17.8 10.9 %collective-permute-start.1 = (bf16[10,32,128]{2,1,0:T(8,128)(2,1)S(1)}, bf16[10,32,128]{2,1,0:T(8,128)(2,1)S(1)}, u32[]{:S(2)}, u32[]{:S(2)}) collective-permute-start(bf16[10,32,128]{2,1,0:T(8,128)(2,1)S(1)} %get-tuple-element.17), channel_id=1, source_target_pairs={{0,2},{1,3},{2,0},{3,1},{4,34},{5,35},{6,32},{7,33},{8,66},{9,67},... | collective-permute-start | bytes 245768 | tf_op jit(solution)/shard_map/ppermute | solution.py:37
  29.5 0.7 copy-start.3
  53.7 20.0 %all-to-all-start.2 = ((bf16[32,2,2,32,128]{4,3,2,1,0:T(8,128)(2,1)}), bf16[32,2,2,32,128]{4,3,2,1,0:T(8,128)(2,1)S(1)}, u32[]{:S(2)}, u32[]{:S(2)}) async-start(bf16[32,2,2,32,128]{4,3,2,1,0:T(8,128)(2,1)} %back_conv.1), calls=%async_computation.2 | async-start | bytes 2097152 | tf_op jit(solution)/shard_map/all_to_all | solution.py:255
  59.8 1.2 %copy-start.1 = (bf16[128,32,128]{2,1,0:T(8,128)(2,1)S(1)}, bf16[128,32,128]{2,1,0:T(8,128)(2,1)}, u32[]{:S(2)}) copy-start(bf16[128,32,128]{2,1,0:T(8,128)(2,1)} %all-gather.2.cloned.1.call-done) | copy-start | bytes 3145732
  64.7 0.8 copy-start.2
  65.5 13.4 %copy-start.4 = (f32[16,32,128]{2,1,0:T(8,128)S(1)}, f32[16,32,128]{2,1,0:T(8,128)}, u32[]{:S(2)}) copy-start(f32[16,32,128]{2,1,0:T(8,128)} %copy-done.3) | copy-start | bytes 786436
  65.5 38.0 %collective-permute-start.4 = (bf16[1152,256]{1,0:T(8,128)(2,1)}, bf16[1152,256]{1,0:T(8,128)(2,1)}, u32[]{:S(2)}, u32[]{:S(2)}) collective-permute-start(bf16[1152,256]{1,0:T(8,128)(2,1)} %get-tuple-element.26), channel_id=1, source_target_pairs={{0,1},{1,0},{2,3},{3,2},{4,5},{5,4},{6,7},{7,6},{8,9},{9,8},{10,11... | collective-permute-start | bytes 1769480 | tf_op jit(solution)/shard_map/ppermute | solution.py:272
  73.6 32.0 %all-to-all-start.1 = ((bf16[32,32,256]{2,1,0:T(8,128)(2,1)}), bf16[32,32,256]{2,1,0:T(8,128)(2,1)S(1)}, u32[]{:S(2)}, u32[]{:S(2)}) async-start(bf16[32,32,256]{2,1,0:T(8,128)(2,1)} %copy-done.2), calls=%async_computation.1 | async-start | bytes 1048576 | tf_op jit(solution)/shard_map/all_to_all | solution.py:273
  79.1 21.7 %collective-permute-start.2 = (bf16[8,32,128]{2,1,0:T(8,128)(2,1)S(1)}, bf16[8,32,128]{2,1,0:T(8,128)(2,1)S(1)}, u32[]{:S(2)}, u32[]{:S(2)}) collective-permute-start(bf16[8,32,128]{2,1,0:T(8,128)(2,1)S(1)} %get-tuple-element.23), channel_id=1, source_target_pairs={{0,0},{1,1},{2,2},{3,3},{4,32},{5,33},{6,34},{7,35},{8,64},{9,65},... | collective-permute-start | bytes 196616 | tf_op jit(solution)/shard_map/ppermute | solution.py:37
  87.9 14.9 %collective-permute-start.3 = (bf16[8,32,128]{2,1,0:T(8,128)(2,1)S(1)}, bf16[8,32,128]{2,1,0:T(8,128)(2,1)S(1)}, u32[]{:S(2)}, u32[]{:S(2)}) collective-permute-start(bf16[8,32,128]{2,1,0:T(8,128)(2,1)S(1)} %get-tuple-element.24), channel_id=1, source_target_pairs={{0,2},{1,3},{2,0},{3,1},{4,34},{5,35},{6,32},{7,33},{8,66},{9,67},... | collective-permute-start | bytes 196616 | tf_op jit(solution)/shard_map/ppermute | solution.py:37
Sparse Core Ops, SparseCore 0:
  30.4 22.5 all-gather.1

commit v3 on v2

--- a/solution.py
+++ b/solution.py
@@ -37,8 +37,17 @@
     return lax.ppermute(pair[0], AXES, stay), lax.ppermute(pair[1], AXES, cross)
 
 
-def split_tile(odd_ref, feat_ref, cot_ref, same_ref, other_ref, copies_ref, cells_ref, wide_ref):
-    odd = odd_ref[0] == 1
+def to_y(block, step):
+    count = lax.axis_size("filt")
+    return lax.ppermute(block, "filt", [(i, (i + 2 * step) % count) for i in range(count)])
+
+
+def to_core(block):
+    return lax.ppermute(block, "filt", [(i, i ^ 1) for i in range(lax.axis_size("filt"))])
+
+
+def split_tile(place_ref, feat_ref, cot_ref, same_ref, other_ref, copies_ref, cells_ref, wide_ref):
+    odd = place_ref[0] == 1
     rows, columns, channels = feat_ref.shape
     half, cells = channels // 2, columns // 2
     for part in range(2):
@@ -61,8 +70,8 @@
         copies_ref[k] = cot_ref[...]
 
 
-def activate(odd_ref, same_ref, other_ref, act_ref, slope_ref, up_ref):
-    odd = odd_ref[0] == 1
+def activate(place_ref, same_ref, other_ref, act_ref, slope_ref, up_ref):
+    odd = place_ref[0] == 1
     count, cells, half = same_ref.shape
     planes = act_ref.shape[0] // 2
     same, other = same_ref[...].astype(F32), other_ref[...].astype(F32)
@@ -75,9 +84,9 @@
         up_ref[t * (planes // 4) : (t + 1) * (planes // 4)] = tile[planes:] * 0.25
 
 
-def back_conv(cot_ref, kernel_ref, out_ref, left_ref, right_ref):
+def back_conv(place_ref, cot_ref, kernel_ref, cross_ref, keep_ref, left_ref, right_ref, sum_ref):
     height, cells, channels = cot_ref.shape
-    half = out_ref.shape[-1]
+    half = keep_ref.shape[-1]
     tokens = height * cells
     column = lax.broadcasted_iota(jnp.int32, (tokens, channels), 0) % cells
     wide = cot_ref[...].astype(F32).reshape(tokens, channels)
@@ -110,17 +119,38 @@
                 preferred_element_type=F32,
             )
             total = term if total is None else total + term
-        total = (total * 0.25).astype(BF16).reshape(height, cells, 2 * half)
+        total = (total * 0.25).reshape(height, cells, 2 * half)
         for b in range(2):
-            out_ref[:, a, b] = total[:, :, b * half : (b + 1) * half]
-
-
-def forward_and_kernel(act_ref, cot_ref, kernel_ref, conv_ref, keep_ref, send_ref, coarse_ref, fine_ref):
-    height, _, _, cells, half = act_ref.shape
+            sum_ref[:, 2 * a + b] = total[:, :, b * half : (b + 1) * half]
+    steps = keep_ref.shape[0]
+    y, core = place_ref[1], place_ref[2]
+    group = height // (2 * steps)
+    for step in range(steps):
+        pair = 2 * ((y + step) % steps)
+        keep_ref[step] = sum_ref[pl.ds((pair + core) * group, group)].reshape(keep_ref.shape[1:])
+        cross_ref[step] = sum_ref[pl.ds((pair + 1 - core) * group, group)].reshape(keep_ref.shape[1:]).astype(BF16)
+
+
+def add_cores(keep_ref, cross_ref, own_ref, *out_refs):
+    own_ref[...] = keep_ref[0] + cross_ref[0].astype(F32)
+    for step, out_ref in enumerate(out_refs, 1):
+        out_ref[...] = (keep_ref[step] + cross_ref[step].astype(F32)).astype(BF16)
+
+
+def forward_and_kernel(place_ref, *refs):
+    chunks, (cot_ref, kernel_ref, conv_ref, keep_ref, send_ref, act_ref, coarse_ref, fine_ref) = refs[:-8], refs[-8:]
+    steps = len(chunks) // 2
+    planes, cells, half = chunks[0].shape
+    height = act_ref.shape[0] // 4
+    y, core = place_ref[1], place_ref[2]
+    for step in range(steps):
+        pair = 2 * ((y + steps - step) % steps)
+        act_ref[pl.ds((pair + core) * planes, planes)] = chunks[2 * step][...]
+        act_ref[pl.ds((pair + 1 - core) * planes, planes)] = chunks[2 * step + 1][...]
     column = lax.broadcasted_iota(jnp.int32, (cells, half), 0)
 
     def plane(i, a, b):
-        return act_ref[i, a, b].astype(F32)
+        return act_ref[4 * i + 2 * a + b].astype(F32)
 
     def put(i, p, even, odd):
         before = jnp.where(column == 0, 0.0, pltpu.roll(odd, 1, 0))
@@ -170,15 +200,16 @@
     conv_ref[...] = conv.astype(BF16).reshape(conv_ref.shape)
 
 
-def input_side(odd_ref, back_ref, slope_ref, up_ref, same_ref, other_ref):
-    odd = odd_ref[0] == 1
+def input_side(place_ref, own_ref, *refs):
+    terms, (slope_ref, up_ref, same_ref, other_ref) = refs[:-4], refs[-4:]
+    odd = place_ref[0] == 1
     planes = same_ref.shape[0]
     grads = []
     for t in range(2):
         block = slice(t * planes, (t + 1) * planes)
-        total = back_ref[0, block].astype(F32)
-        for k in range(1, back_ref.shape[0]):
-            total = total + back_ref[k, block].astype(F32)
+        total = own_ref[block]
+        for term in terms:
+            total = total + term[block].astype(F32)
         total = total * slope_ref[block]
         up = up_ref[t * (planes // 4) : (t + 1) * (planes // 4)]
         grads.append([total[k] + up[k // 4] for k in range(planes)])
@@ -187,8 +218,8 @@
         other_ref[k] = jnp.where(odd, grads[0][k], grads[1][k]).astype(BF16)
 
 
-def join_tile(odd_ref, same_ref, other_ref, out_ref, low_ref, high_ref):
-    odd = odd_ref[0] == 1
+def join_tile(place_ref, same_ref, other_ref, out_ref, low_ref, high_ref):
+    odd = place_ref[0] == 1
     rows, columns, channels = out_ref.shape
     half = channels // 2
     for k in range(2 * rows):
@@ -205,7 +236,8 @@
     half, cells = channels // 2, columns // 2
     filt_count, row_count = lax.axis_size("filt"), lax.axis_size("rows")
     height = tile_rows * row_count // 2
-    odd = (lax.axis_index("rows") % 2).astype(jnp.int32).reshape(1)
+    filt = lax.axis_index("filt")
+    place = jnp.stack([lax.axis_index("rows") % 2, filt // 2, filt % 2]).astype(jnp.int32)
     kernel_flat = kernel.reshape(9 * half, channels)
     planes = 2 * tile_rows
 
@@ -220,7 +252,7 @@
         ],
         [pltpu.VMEM((2, tile_rows, columns, half), F32)],
         1,
-        odd,
+        place,
         features[0],
         cotangent[0],
     )
@@ -235,24 +267,37 @@
         ],
         [],
         1,
-        odd,
+        place,
         same,
         other,
     )
-    act = lax.all_gather(act, "filt", axis=0, tiled=True).reshape(height, 2, 2, cells, half)
-
-    (back,) = call(
+    steps = filt_count // 2
+    chunks = []
+    for block in [act] + [to_y(act, step) for step in range(1, steps)]:
+        chunks += [block, to_core(block)]
+
+    cross, keep = call(
         back_conv,
-        [((height, 2, 2, cells, half), BF16)],
+        [((steps, 2 * planes, cells, half), BF16), ((steps, 2 * planes, cells, half), F32)],
         [
             pltpu.VMEM(((height + 2) * cells, 4 * channels), BF16),
             pltpu.VMEM((3, 2 * half, 4 * channels), BF16),
-        ],
-        0,
+            pltpu.VMEM((height, 4, cells, half), F32),
+        ],
+        1,
+        place,
         cot,
         kernel_flat,
     )
-    back = lax.all_to_all(back, "filt", 0, 0, tiled=True)
+    own, *terms = call(
+        add_cores,
+        [((2 * planes, cells, half), F32)] + [((2 * planes, cells, half), BF16)] * (steps - 1),
+        [],
+        0,
+        keep,
+        to_core(cross),
+    )
+    terms = [to_y(term, step) for step, term in enumerate(terms, 1)]
     conv, kernel_term, outgoing = call(
         forward_and_kernel,
         [
@@ -261,11 +306,13 @@
             ((9 * half, channels), BF16),
         ],
         [
+            pltpu.VMEM((4 * height, cells, half), BF16),
             pltpu.VMEM((height * cells, 9 * half), BF16),
             pltpu.VMEM((height * cells, 9 * half), BF16),
         ],
-        0,
-        act,
+        1,
+        place,
+        *chunks,
         cot,
         kernel_flat,
     )
@@ -277,8 +324,9 @@
         [((planes, cells, half), BF16), ((planes, cells, half), BF16)],
         [],
         1,
-        odd,
-        back.reshape(filt_count, 2 * planes, cells, half),
+        place,
+        own,
+        *terms,
         slope,
         up,
     )
@@ -288,7 +336,7 @@
         [(features.shape[1:], BF16)],
         [pltpu.VMEM((tile_rows, columns, half), F32)] * 2,
         1,
-        odd,
+        place,
         same,
         other,
     )

time: 114 us -> 109 us (0.956)
  blocking collectives: 19 us -> 0 us
  between operations: 14.1 us -> 0.8 us
  starting transfers between devices: 33.2 us -> 43.1 us
  local copies, waits for them, and re-layouts: 4.46 us -> 12.8 us
  Pallas kernels: 9.82 us -> 14.3 us
  waiting for transfers between devices: 29.7 us -> 32.1 us
  other arithmetic: 2.9 us -> 4.05 us
    all_to_all x1 -> x0, blocking collectives: 19 us -> none  [local(): lax.all_to_all(copies, 'rows', 0, 0, tiled=True)]
    ppermute x0 -> x11, waiting for transfers between devices: none -> 12.7 us  [the longest x6 12.7 us: to_y(): lax.ppermute(block, 'filt', [(i, (i + 2 * step) % count) for i in range(c...]
    unnamed x14 -> x44, local copies, waits for them, and re-layouts: 4.46 us -> 12.8 us
    ppermute x0 -> x11, starting transfers between devices: none -> 7.28 us  [the longest x6 6.27 us: to_y(): lax.ppermute(block, 'filt', [(i, (i + 2 * step) % count) for i in range(c...]
    all_to_all x1, waiting for transfers between devices: 5.49 us -> 0.01 us  [local(): lax.all_to_all(copies, 'rows', 0, 0, tiled=True)]
    pallas_call x6 -> x7, Pallas kernels: 9.82 us -> 14.3 us  [call(): pl.pallas_call(body, out_shape=[jax.ShapeDtypeStruct(shape, dtype) for sh...]
    ppermute x2, starting transfers between devices: 17.6 us -> 13.8 us  [swap_tiles(): lax.ppermute(pair[0], AXES, stay)]
    ppermute x2, starting transfers between devices: 1.58 us -> 5.3 us  [swap_tiles(): lax.ppermute(pair[1], AXES, cross)]
  transfers between devices with their start and end apart: 8 -> 18, of which waited for: 5 -> 9; matrix products, arithmetic and copies ran while one was open for 2% -> 2% of each run, Pallas kernels for 8% -> 12%
where the time goes in v3:
time: 109 us; the launch traced here: 107 us
  starting transfers between devices  43.1 us (40%)
  waiting for transfers between devices  32.1 us (29%)
  Pallas kernels  14.3 us (13%)
  local copies, waits for them, and re-layouts  12.8 us (12%)
  other arithmetic  4.05 us (4%)
    pallas_call x7, Pallas kernels, call(): pl.pallas_call(body, out_shape=[jax.ShapeDtypeStruct(shape, dtype) for sh...  14.3 us
    ppermute x2, starting transfers between devices, swap_tiles(): lax.ppermute(pair[0], AXES, stay)  13.8 us
    ppermute x2, waiting for transfers between devices, swap_tiles(): lax.ppermute(pair[0], AXES, stay)  13.3 us
    unnamed x44, local copies, waits for them, and re-layouts  12.8 us
    ppermute x6, waiting for transfers between devices, to_y(): lax.ppermute(block, 'filt', [(i, (i + 2 * step) % count) for i in range(c...  12.7 us
    all_to_all x1, starting transfers between devices, local(): lax.all_to_all(copies, 'rows', 0, 0, tiled=True)  9.51 us
    ppermute x6, starting transfers between devices, to_y(): lax.ppermute(block, 'filt', [(i, (i + 2 * step) % count) for i in range(c...  6.27 us
    ppermute x2, waiting for transfers between devices, swap_tiles(): lax.ppermute(pair[1], AXES, cross)  6.07 us
  transfers between devices with their start and end apart: 18, of which 9 were waited for; matrix products, arithmetic and copies ran while one was open for 2% of the time, Pallas kernels for 12%

profile of v3, /device:TPU:56, one launch (start us, length us, event | category | flops | bytes accessed | tf_op | source)
XLA Modules:
  0.0 107.3 jit_solution(13982590713656141225)
XLA Ops:
  0.7 1.0 copy-done.18
  1.7 0.8 copy-done.21
  2.5 1.4 %split_tile.1 = (bf16[10,32,128]{2,1,0:T(8,128)(2,1)S(1)}, bf16[10,32,128]{2,1,0:T(8,128)(2,1)S(1)}, bf16[16,2,32,256]{3,2,1,0:T(8,128)(2,1)}, f32[2,32,256]{2,1,0:T(8,128)S(1)}) custom-call(s32[3]{0:T(128)S(1)} %pad_add_fusion.place_ref, bf16[4,64,256]{2,1,0:T(8,128)(2,1)S(1)} %bitcast.17, bf16[2,32,256]{2,1,0:T(8,128)(2,1)S(1)} %bitcast.18), custom_call_target="tpu_custom_call" | custom-call | tf_op jit(solution)/shard_map/split_tile/pallas_call | solution.py:16
  3.9 0.6 copy-done.19
  4.5 9.5 %all-to-all-start = ((bf16[16,2,32,256]{3,2,1,0:T(8,128)(2,1)}), bf16[16,2,32,256]{3,2,1,0:T(8,128)(2,1)S(1)}, u32[]{:S(2)}, u32[]{:S(2)}) async-start(bf16[16,2,32,256]{3,2,1,0:T(8,128)(2,1)} %get-tuple-element.25), calls=%async_computation | async-start | bytes 1048576 | tf_op jit(solution)/shard_map/all_to_all | solution.py:260
  14.0 6.9 %collective-permute-start = (bf16[10,32,128]{2,1,0:T(8,128)(2,1)S(1)}, bf16[10,32,128]{2,1,0:T(8,128)(2,1)S(1)}, u32[]{:S(2)}, u32[]{:S(2)}) collective-permute-start(bf16[10,32,128]{2,1,0:T(8,128)(2,1)S(1)} %get-tuple-element.22), channel_id=1, source_target_pairs={{0,0},{1,1},{2,2},{3,3},{4,32},{5,33},{6,34},{7,35},{8,64},{9,65},... | collective-permute-start | bytes 245768 | tf_op jit(solution)/shard_map/ppermute | solution.py:37
  20.9 2.6 %collective-permute-start.1 = (bf16[10,32,128]{2,1,0:T(8,128)(2,1)S(1)}, bf16[10,32,128]{2,1,0:T(8,128)(2,1)S(1)}, u32[]{:S(2)}, u32[]{:S(2)}) collective-permute-start(bf16[10,32,128]{2,1,0:T(8,128)(2,1)S(1)} %get-tuple-element.23), channel_id=1, source_target_pairs={{0,2},{1,3},{2,0},{3,1},{4,34},{5,35},{6,32},{7,33},{8,66},{9,67},... | collective-permute-start | bytes 245768 | tf_op jit(solution)/shard_map/ppermute | solution.py:37
  23.6 11.5 %collective-permute-done.same_ref = bf16[10,32,128]{2,1,0:T(8,128)(2,1)S(1)} collective-permute-done((bf16[10,32,128]{2,1,0:T(8,128)(2,1)S(1)}, bf16[10,32,128]{2,1,0:T(8,128)(2,1)S(1)}, u32[]{:S(2)}, u32[]{:S(2)}) %collective-permute-start) | collective-permute-done | bytes 81952 | tf_op jit(solution)/shard_map/ppermute | solution.py:37
  35.0 2.5 %collective-permute-done.1.other_ref = bf16[10,32,128]{2,1,0:T(8,128)(2,1)S(1)} collective-permute-done((bf16[10,32,128]{2,1,0:T(8,128)(2,1)S(1)}, bf16[10,32,128]{2,1,0:T(8,128)(2,1)S(1)}, u32[]{:S(2)}, u32[]{:S(2)}) %collective-permute-start.1) | collective-permute-done | bytes 81952 | tf_op jit(solution)/shard_map/ppermute | solution.py:37
  37.5 0.7 activate.1
  38.2 0.7 copy-done.2
  38.9 0.4 collective-permute-start.5
  39.3 2.9 %collective-permute-start.3 = (bf16[16,32,128]{2,1,0:T(8,128)(2,1)S(1)}, bf16[16,32,128]{2,1,0:T(8,128)(2,1)S(1)}, u32[]{:S(2)}, u32[]{:S(2)}) collective-permute-start(bf16[16,32,128]{2,1,0:T(8,128)(2,1)S(1)} %get-tuple-element.24.refs_0_), channel_id=1, source_target_pairs={{0,64},{32,96},{64,128},{96,160},{128,192},{160,224},{192,0},{224,... | collective-permute-start | bytes 393224 | tf_op jit(solution)/shard_map/ppermute | solution.py:42
  42.1 4.3 %collective-permute-done.7.refs_6_ = bf16[16,32,128]{2,1,0:T(8,128)(2,1)S(1)} collective-permute-done((bf16[16,32,128]{2,1,0:T(8,128)(2,1)S(1)}, bf16[16,32,128]{2,1,0:T(8,128)(2,1)S(1)}, u32[]{:S(2)}, u32[]{:S(2)}) %collective-permute-start.7) | collective-permute-done | bytes 131104 | tf_op jit(solution)/shard_map/ppermute | solution.py:42
  46.5 0.5 collective-permute-start.6
  47.0 0.4 collective-permute-done.3.refs_2_
  47.4 4.9 %back_conv.1 = (bf16[4,16,32,128]{3,2,1,0:T(8,128)(2,1)}, f32[4,16,32,128]{3,2,1,0:T(8,128)S(1)}) custom-call(s32[3]{0:T(128)S(1)} %pad_add_fusion.place_ref, bf16[32,32,256]{2,1,0:T(8,128)(2,1)S(1)} %bitcast.13, bf16[1152,256]{1,0:T(8,128)(2,1)S(1)} %bitcast.15), custom_call_target="tpu_custom_call" | custom-call | tf_op jit(solution)/shard_map/back_conv/pallas_call | solution.py:16
  52.3 0.5 collective-permute-start.9
  52.8 0.7 copy-done.10
  53.5 0.6 copy-done.12
  54.1 0.6 copy-done.14
  54.8 0.7 copy-done.16
  55.4 0.9 copy-done.5
  56.3 0.9 copy-done.7
  57.2 0.9 copy-done.9
  58.1 0.9 copy-done.11
  59.1 0.9 copy-done.13
  60.0 0.9 copy-done.15
  60.9 0.9 copy-done.17
  61.8 4.3 %forward_and_kernel.1 = (bf16[32,32,256]{2,1,0:T(8,128)(2,1)S(1)}, f32[1152,256]{1,0:T(8,128)S(1)}, bf16[1152,256]{1,0:T(8,128)(2,1)}) custom-call(s32[3]{0:T(128)S(1)} %pad_add_fusion.place_ref, bf16[16,32,128]{2,1,0:T(8,128)(2,1)S(1)} %get-tuple-element.24.refs_0_, bf16[16,32,128]{2,1,0:T(8,128)(2,1)S(1)} %copy-done.11, ...), custom_call_target="tpu_custom_call" | custom-call | tf_op jit(solution)/shard_map/forward_and_kernel/pallas_call | solution.py:16
  66.1 0.8 copy-done.1
  66.9 2.7 %collective-permute-start.15 = (bf16[1152,256]{1,0:T(8,128)(2,1)}, bf16[1152,256]{1,0:T(8,128)(2,1)}, u32[]{:S(2)}, u32[]{:S(2)}) collective-permute-start(bf16[1152,256]{1,0:T(8,128)(2,1)} %get-tuple-element.38), channel_id=1, source_target_pairs={{0,1},{1,0},{2,3},{3,2},{4,5},{5,4},{6,7},{7,6},{8,9},{9,8},{10,11... | collective-permute-start | bytes 1769480 | tf_op jit(solution)/shard_map/ppermute | solution.py:319
  69.6 4.5 %all-to-all-start.1 = ((bf16[32,32,256]{2,1,0:T(8,128)(2,1)}), bf16[32,32,256]{2,1,0:T(8,128)(2,1)}, u32[]{:S(2)}, u32[]{:S(2)}) async-start(bf16[32,32,256]{2,1,0:T(8,128)(2,1)} %copy-done.1), calls=%async_computation.1 | async-start | bytes 1048576 | tf_op jit(solution)/shard_map/all_to_all | solution.py:320
  74.1 1.2 %add_cores.1 = (f32[16,32,128]{2,1,0:T(8,128)S(1)}, bf16[16,32,128]{2,1,0:T(8,128)(2,1)S(1)}, bf16[16,32,128]{2,1,0:T(8,128)(2,1)S(1)}, bf16[16,32,128]{2,1,0:T(8,128)(2,1)S(1)}) custom-call(f32[4,16,32,128]{3,2,1,0:T(8,128)S(1)} %get-tuple-element.27.keep_ref, bf16[4,16,32,128]{3,2,1,0:T(8,128)(2,1)} %collective-permute-done.9.cross_ref), custom_call_target="tpu_custom_call" | custom-call | tf_op jit(solution)/shard_map/add_cores/pallas_call | solution.py:16
  75.3 2.1 %collective-permute-start.10 = (bf16[16,32,128]{2,1,0:T(8,128)(2,1)S(1)}, bf16[16,32,128]{2,1,0:T(8,128)(2,1)S(1)}, u32[]{:S(2)}, u32[]{:S(2)}) collective-permute-start(bf16[16,32,128]{2,1,0:T(8,128)(2,1)S(1)} %get-tuple-element.30), channel_id=1, source_target_pairs={{0,64},{32,96},{64,128},{96,160},{128,192},{160,224},{192,0},{224,... | collective-permute-start | bytes 393224 | tf_op jit(solution)/shard_map/ppermute | solution.py:42
  77.4 0.9 collective-permute-start.11
  78.3 4.5 %collective-permute-done.10.refs_0_ = bf16[16,32,128]{2,1,0:T(8,128)(2,1)S(1)} collective-permute-done((bf16[16,32,128]{2,1,0:T(8,128)(2,1)S(1)}, bf16[16,32,128]{2,1,0:T(8,128)(2,1)S(1)}, u32[]{:S(2)}, u32[]{:S(2)}) %collective-permute-start.10) | collective-permute-done | bytes 131104 | tf_op jit(solution)/shard_map/ppermute | solution.py:42
  82.9 2.3 %collective-permute-done.11.refs_1_ = bf16[16,32,128]{2,1,0:T(8,128)(2,1)S(1)} collective-permute-done((bf16[16,32,128]{2,1,0:T(8,128)(2,1)S(1)}, bf16[16,32,128]{2,1,0:T(8,128)(2,1)S(1)}, u32[]{:S(2)}, u32[]{:S(2)}) %collective-permute-start.11) | collective-permute-done | bytes 131104 | tf_op jit(solution)/shard_map/ppermute | solution.py:42
  85.2 1.1 %collective-permute-done.12.refs_2_ = bf16[16,32,128]{2,1,0:T(8,128)(2,1)S(1)} collective-permute-done((bf16[16,32,128]{2,1,0:T(8,128)(2,1)S(1)}, bf16[16,32,128]{2,1,0:T(8,128)(2,1)S(1)}, u32[]{:S(2)}, u32[]{:S(2)}) %collective-permute-start.12) | collective-permute-done | bytes 131104 | tf_op jit(solution)/shard_map/ppermute | solution.py:42
  86.3 0.6 input_side.1
  87.0 6.9 %collective-permute-start.13 = (bf16[8,32,128]{2,1,0:T(8,128)(2,1)S(1)}, bf16[8,32,128]{2,1,0:T(8,128)(2,1)S(1)}, u32[]{:S(2)}, u32[]{:S(2)}) collective-permute-start(bf16[8,32,128]{2,1,0:T(8,128)(2,1)S(1)} %get-tuple-element.35), channel_id=1, source_target_pairs={{0,0},{1,1},{2,2},{3,3},{4,32},{5,33},{6,34},{7,35},{8,64},{9,65},... | collective-permute-start | bytes 196616 | tf_op jit(solution)/shard_map/ppermute | solution.py:37
  93.9 2.7 %collective-permute-start.14 = (bf16[8,32,128]{2,1,0:T(8,128)(2,1)S(1)}, bf16[8,32,128]{2,1,0:T(8,128)(2,1)S(1)}, u32[]{:S(2)}, u32[]{:S(2)}) collective-permute-start(bf16[8,32,128]{2,1,0:T(8,128)(2,1)S(1)} %get-tuple-element.36), channel_id=1, source_target_pairs={{0,2},{1,3},{2,0},{3,1},{4,34},{5,35},{6,32},{7,33},{8,66},{9,67},... | collective-permute-start | bytes 196616 | tf_op jit(solution)/shard_map/ppermute | solution.py:37
  96.6 2.2 %convert_add_fusion = f32[1152,256]{1,0:T(8,128)} fusion(f32[1152,256]{1,0:T(8,128)S(1)} %get-tuple-element.37, bf16[1152,256]{1,0:T(8,128)(2,1)} %collective-permute-done.15), kind=kLoop, calls=%fused_computation | loop fusion | flops 589824 | bytes 2949120 | tf_op jit(solution)/shard_map/add | solution.py:343
  98.8 1.9 %collective-permute-done.13.same_ref = bf16[8,32,128]{2,1,0:T(8,128)(2,1)S(1)} collective-permute-done((bf16[8,32,128]{2,1,0:T(8,128)(2,1)S(1)}, bf16[8,32,128]{2,1,0:T(8,128)(2,1)S(1)}, u32[]{:S(2)}, u32[]{:S(2)}) %collective-permute-start.13) | collective-permute-done | bytes 65568 | tf_op jit(solution)/shard_map/ppermute | solution.py:37
  100.7 3.6 %collective-permute-done.14.other_ref = bf16[8,32,128]{2,1,0:T(8,128)(2,1)S(1)} collective-permute-done((bf16[8,32,128]{2,1,0:T(8,128)(2,1)S(1)}, bf16[8,32,128]{2,1,0:T(8,128)(2,1)S(1)}, u32[]{:S(2)}, u32[]{:S(2)}) %collective-permute-start.14) | collective-permute-done | bytes 65568 | tf_op jit(solution)/shard_map/ppermute | solution.py:37
  104.3 1.2 %join_tile.1 = bf16[4,64,256]{2,1,0:T(8,128)(2,1)} custom-call(s32[3]{0:T(128)S(1)} %pad_add_fusion.place_ref, bf16[8,32,128]{2,1,0:T(8,128)(2,1)S(1)} %collective-permute-done.13.same_ref, bf16[8,32,128]{2,1,0:T(8,128)(2,1)S(1)} %collective-permute-done.14.other_ref), custom_call_target="tpu_custom_call" | custom-call | tf_op jit(solution)/shard_map/join_tile/pallas_call | solution.py:16
  105.5 1.1 %convert_reduce_fusion = f32[2,32,256]{2,1,0:T(8,128)S(1)} fusion(bf16[16,2,32,256]{3,2,1,0:T(8,128)(2,1)} %bitcast.11), kind=kLoop, calls=%fused_computation.1 | loop fusion | flops 507904 | bytes 589824 | tf_op jit(solution)/shard_map/reduce_sum | solution.py:344
  106.6 0.6 fusion
  (43 shorter events, 0.2 us)
Async XLA Ops:
  0.6 46.7 %copy-start = (bf16[3,3,128,256]{3,2,1,0:T(8,128)(2,1)S(1)}, bf16[3,3,128,256]{3,2,1,0:T(8,128)(2,1)}, u32[]{:S(2)}) copy-start(bf16[3,3,128,256]{3,2,1,0:T(8,128)(2,1)} %param.4) | copy-start | bytes 1769476
  0.7 1.0 copy-start.18
  1.7 0.8 copy-start.21
  3.9 0.6 copy-start.19
  4.5 42.9 %all-to-all-start = ((bf16[16,2,32,256]{3,2,1,0:T(8,128)(2,1)}), bf16[16,2,32,256]{3,2,1,0:T(8,128)(2,1)S(1)}, u32[]{:S(2)}, u32[]{:S(2)}) async-start(bf16[16,2,32,256]{3,2,1,0:T(8,128)(2,1)} %get-tuple-element.25), calls=%async_computation | async-start | bytes 1048576 | tf_op jit(solution)/shard_map/all_to_all | solution.py:260
  14.0 21.0 %collective-permute-start = (bf16[10,32,128]{2,1,0:T(8,128)(2,1)S(1)}, bf16[10,32,128]{2,1,0:T(8,128)(2,1)S(1)}, u32[]{:S(2)}, u32[]{:S(2)}) collective-permute-start(bf16[10,32,128]{2,1,0:T(8,128)(2,1)S(1)} %get-tuple-element.22), channel_id=1, source_target_pairs={{0,0},{1,1},{2,2},{3,3},{4,32},{5,33},{6,34},{7,35},{8,64},{9,65},... | collective-permute-start | bytes 245768 | tf_op jit(solution)/shard_map/ppermute | solution.py:37
  20.9 16.6 %collective-permute-start.1 = (bf16[10,32,128]{2,1,0:T(8,128)(2,1)S(1)}, bf16[10,32,128]{2,1,0:T(8,128)(2,1)S(1)}, u32[]{:S(2)}, u32[]{:S(2)}) collective-permute-start(bf16[10,32,128]{2,1,0:T(8,128)(2,1)S(1)} %get-tuple-element.23), channel_id=1, source_target_pairs={{0,2},{1,3},{2,0},{3,1},{4,34},{5,35},{6,32},{7,33},{8,66},{9,67},... | collective-permute-start | bytes 245768 | tf_op jit(solution)/shard_map/ppermute | solution.py:37
  38.2 0.7 copy-start.2
  38.9 7.6 %collective-permute-start.7 = (bf16[16,32,128]{2,1,0:T(8,128)(2,1)S(1)}, bf16[16,32,128]{2,1,0:T(8,128)(2,1)S(1)}, u32[]{:S(2)}, u32[]{:S(2)}) collective-permute-start(bf16[16,32,128]{2,1,0:T(8,128)(2,1)S(1)} %get-tuple-element.24.refs_0_), channel_id=1, source_target_pairs={{0,192},{32,224},{64,0},{96,32},{128,64},{160,96},{192,128},{224,1... | collective-permute-start | bytes 393224 | tf_op jit(solution)/shard_map/ppermute | solution.py:42
  38.9 7.6 %collective-permute-start.5 = (bf16[16,32,128]{2,1,0:T(8,128)(2,1)S(1)}, bf16[16,32,128]{2,1,0:T(8,128)(2,1)S(1)}, u32[]{:S(2)}, u32[]{:S(2)}) collective-permute-start(bf16[16,32,128]{2,1,0:T(8,128)(2,1)S(1)} %get-tuple-element.24.refs_0_), channel_id=1, source_target_pairs={{0,128},{32,160},{64,192},{96,224},{128,0},{160,32},{192,64},{224,... | collective-permute-start | bytes 393224 | tf_op jit(solution)/shard_map/ppermute | solution.py:42
  39.3 8.1 %collective-permute-start.3 = (bf16[16,32,128]{2,1,0:T(8,128)(2,1)S(1)}, bf16[16,32,128]{2,1,0:T(8,128)(2,1)S(1)}, u32[]{:S(2)}, u32[]{:S(2)}) collective-permute-start(bf16[16,32,128]{2,1,0:T(8,128)(2,1)S(1)} %get-tuple-element.24.refs_0_), channel_id=1, source_target_pairs={{0,64},{32,96},{64,128},{96,160},{128,192},{160,224},{192,0},{224,... | collective-permute-start | bytes 393224 | tf_op jit(solution)/shard_map/ppermute | solution.py:42
  42.1 10.7 %collective-permute-start.2 = (bf16[16,32,128]{2,1,0:T(8,128)(2,1)S(1)}, bf16[16,32,128]{2,1,0:T(8,128)(2,1)S(1)}, u32[]{:S(2)}, u32[]{:S(2)}) collective-permute-start(bf16[16,32,128]{2,1,0:T(8,128)(2,1)S(1)} %get-tuple-element.24.refs_0_), channel_id=1, source_target_pairs={{0,32},{32,0},{64,96},{96,64},{128,160},{160,128},{192,224},{224,1... | collective-permute-start | bytes 393224 | tf_op jit(solution)/shard_map/ppermute | solution.py:46
  46.5 7.7 %copy-start.4 = (bf16[16,32,128]{2,1,0:T(8,128)(2,1)}, bf16[16,32,128]{2,1,0:T(8,128)(2,1)S(1)}, u32[]{:S(2)}) copy-start(bf16[16,32,128]{2,1,0:T(8,128)(2,1)S(1)} %collective-permute-done.7.refs_6_) | copy-start | bytes 393220
  46.5 7.0 %collective-permute-start.8 = (bf16[16,32,128]{2,1,0:T(8,128)(2,1)S(1)}, bf16[16,32,128]{2,1,0:T(8,128)(2,1)S(1)}, u32[]{:S(2)}, u32[]{:S(2)}) collective-permute-start(bf16[16,32,128]{2,1,0:T(8,128)(2,1)S(1)} %collective-permute-done.7.refs_6_), channel_id=1, source_target_pairs={{0,32},{32,0},{64,96},{96,64},{128,160},{160,128},{192,224},{224,1... | collective-permute-start | bytes 393224 | tf_op jit(solution)/shard_map/ppermute | solution.py:46
  46.5 7.6 %copy-start.6 = (bf16[16,32,128]{2,1,0:T(8,128)(2,1)}, bf16[16,32,128]{2,1,0:T(8,128)(2,1)S(1)}, u32[]{:S(2)}) copy-start(bf16[16,32,128]{2,1,0:T(8,128)(2,1)S(1)} %collective-permute-done.5.refs_4_) | copy-start | bytes 393220
  46.5 7.6 %collective-permute-start.6 = (bf16[16,32,128]{2,1,0:T(8,128)(2,1)S(1)}, bf16[16,32,128]{2,1,0:T(8,128)(2,1)S(1)}, u32[]{:S(2)}, u32[]{:S(2)}) collective-permute-start(bf16[16,32,128]{2,1,0:T(8,128)(2,1)S(1)} %collective-permute-done.5.refs_4_), channel_id=1, source_target_pairs={{0,32},{32,0},{64,96},{96,64},{128,160},{160,128},{192,224},{224,1... | collective-permute-start | bytes 393224 | tf_op jit(solution)/shard_map/ppermute | solution.py:46
  47.4 6.8 %copy-start.8 = (bf16[16,32,128]{2,1,0:T(8,128)(2,1)}, bf16[16,32,128]{2,1,0:T(8,128)(2,1)S(1)}, u32[]{:S(2)}) copy-start(bf16[16,32,128]{2,1,0:T(8,128)(2,1)S(1)} %collective-permute-done.3.refs_2_) | copy-start | bytes 393220
  47.4 7.4 %collective-permute-start.4 = (bf16[16,32,128]{2,1,0:T(8,128)(2,1)S(1)}, bf16[16,32,128]{2,1,0:T(8,128)(2,1)S(1)}, u32[]{:S(2)}, u32[]{:S(2)}) collective-permute-start(bf16[16,32,128]{2,1,0:T(8,128)(2,1)S(1)} %collective-permute-done.3.refs_2_), channel_id=1, source_target_pairs={{0,32},{32,0},{64,96},{96,64},{128,160},{160,128},{192,224},{224,1... | collective-permute-start | bytes 393224 | tf_op jit(solution)/shard_map/ppermute | solution.py:46
  52.3 21.8 %collective-permute-start.9 = (bf16[4,16,32,128]{3,2,1,0:T(8,128)(2,1)}, bf16[4,16,32,128]{3,2,1,0:T(8,128)(2,1)}, u32[]{:S(2)}, u32[]{:S(2)}) collective-permute-start(bf16[4,16,32,128]{3,2,1,0:T(8,128)(2,1)} %get-tuple-element.28), channel_id=1, source_target_pairs={{0,32},{32,0},{64,96},{96,64},{128,160},{160,128},{192,224},{224,1... | collective-permute-start | bytes 1572872 | tf_op jit(solution)/shard_map/ppermute | solution.py:46
  52.8 0.7 copy-start.10
  53.5 0.7 copy-start.12
  54.1 0.6 copy-start.14
  54.8 0.7 copy-start.16
  55.4 0.9 copy-start.5
  56.3 0.9 copy-start.7
  57.2 0.9 copy-start.9
  58.1 0.9 copy-start.11
  59.1 0.9 copy-start.13
  60.0 0.9 copy-start.15
  60.9 0.9 copy-start.17
  66.1 0.8 copy-start.1
  66.9 29.7 %collective-permute-start.15 = (bf16[1152,256]{1,0:T(8,128)(2,1)}, bf16[1152,256]{1,0:T(8,128)(2,1)}, u32[]{:S(2)}, u32[]{:S(2)}) collective-permute-start(bf16[1152,256]{1,0:T(8,128)(2,1)} %get-tuple-element.38), channel_id=1, source_target_pairs={{0,1},{1,0},{2,3},{3,2},{4,5},{5,4},{6,7},{7,6},{8,9},{9,8},{10,11... | collective-permute-start | bytes 1769480 | tf_op jit(solution)/shard_map/ppermute | solution.py:319
  69.6 35.9 %all-to-all-start.1 = ((bf16[32,32,256]{2,1,0:T(8,128)(2,1)}), bf16[32,32,256]{2,1,0:T(8,128)(2,1)}, u32[]{:S(2)}, u32[]{:S(2)}) async-start(bf16[32,32,256]{2,1,0:T(8,128)(2,1)} %copy-done.1), calls=%async_computation.1 | async-start | bytes 1048576 | tf_op jit(solution)/shard_map/all_to_all | solution.py:320
  74.1 12.2 %copy-start.3 = (f32[16,32,128]{2,1,0:T(8,128)S(1)}, f32[16,32,128]{2,1,0:T(8,128)}, u32[]{:S(2)}) copy-start(f32[16,32,128]{2,1,0:T(8,128)} %copy-done.2) | copy-start | bytes 786436
  75.3 7.6 %collective-permute-start.10 = (bf16[16,32,128]{2,1,0:T(8,128)(2,1)S(1)}, bf16[16,32,128]{2,1,0:T(8,128)(2,1)S(1)}, u32[]{:S(2)}, u32[]{:S(2)}) collective-permute-start(bf16[16,32,128]{2,1,0:T(8,128)(2,1)S(1)} %get-tuple-element.30), channel_id=1, source_target_pairs={{0,64},{32,96},{64,128},{96,160},{128,192},{160,224},{192,0},{224,... | collective-permute-start | bytes 393224 | tf_op jit(solution)/shard_map/ppermute | solution.py:42
  77.4 7.8 %collective-permute-start.11 = (bf16[16,32,128]{2,1,0:T(8,128)(2,1)S(1)}, bf16[16,32,128]{2,1,0:T(8,128)(2,1)S(1)}, u32[]{:S(2)}, u32[]{:S(2)}) collective-permute-start(bf16[16,32,128]{2,1,0:T(8,128)(2,1)S(1)} %get-tuple-element.31), channel_id=1, source_target_pairs={{0,128},{32,160},{64,192},{96,224},{128,0},{160,32},{192,64},{224,... | collective-permute-start | bytes 393224 | tf_op jit(solution)/shard_map/ppermute | solution.py:42
  78.3 8.0 %collective-permute-start.12 = (bf16[16,32,128]{2,1,0:T(8,128)(2,1)S(1)}, bf16[16,32,128]{2,1,0:T(8,128)(2,1)S(1)}, u32[]{:S(2)}, u32[]{:S(2)}) collective-permute-start(bf16[16,32,128]{2,1,0:T(8,128)(2,1)S(1)} %get-tuple-element.32), channel_id=1, source_target_pairs={{0,192},{32,224},{64,0},{96,32},{128,64},{160,96},{192,128},{224,1... | collective-permute-start | bytes 393224 | tf_op jit(solution)/shard_map/ppermute | solution.py:42
  87.0 13.7 %collective-permute-start.13 = (bf16[8,32,128]{2,1,0:T(8,128)(2,1)S(1)}, bf16[8,32,128]{2,1,0:T(8,128)(2,1)S(1)}, u32[]{:S(2)}, u32[]{:S(2)}) collective-permute-start(bf16[8,32,128]{2,1,0:T(8,128)(2,1)S(1)} %get-tuple-element.35), channel_id=1, source_target_pairs={{0,0},{1,1},{2,2},{3,3},{4,32},{5,33},{6,34},{7,35},{8,64},{9,65},... | collective-permute-start | bytes 196616 | tf_op jit(solution)/shard_map/ppermute | solution.py:37
  93.9 10.4 %collective-permute-start.14 = (bf16[8,32,128]{2,1,0:T(8,128)(2,1)S(1)}, bf16[8,32,128]{2,1,0:T(8,128)(2,1)S(1)}, u32[]{:S(2)}, u32[]{:S(2)}) collective-permute-start(bf16[8,32,128]{2,1,0:T(8,128)(2,1)S(1)} %get-tuple-element.36), channel_id=1, source_target_pairs={{0,2},{1,3},{2,0},{3,1},{4,34},{5,35},{6,32},{7,33},{8,66},{9,67},... | collective-permute-start | bytes 196616 | tf_op jit(solution)/shard_map/ppermute | solution.py:37
  96.6 10.1 %copy-start.20 = (f32[2,32,256]{2,1,0:T(8,128)S(1)}, f32[2,32,256]{2,1,0:T(8,128)}, u32[]{:S(2)}) copy-start(f32[2,32,256]{2,1,0:T(8,128)} %copy-done.19) | copy-start | bytes 196612

commit v4 on v3

--- a/solution.py
+++ b/solution.py
@@ -5,22 +5,25 @@
 from jax.experimental.pallas import tpu as pltpu
 from jax.sharding import PartitionSpec as P
 
+MU_POOL, MU_ADD, MU_JOIN, MU_IN, MU_BACK, MU_FWD = 10, 60, 1, 1, 4, 6
 AXES = ("filt", "rows", "rep")
 VMEM = pl.BlockSpec(memory_space=pltpu.VMEM)
+ANY = pl.BlockSpec(memory_space=pl.ANY)
 SMEM = pl.BlockSpec(memory_space=pltpu.SMEM)
 F32 = jnp.float32
 BF16 = jnp.bfloat16
 
 
-def call(body, outs, scratch, scalars, *args):
+def call(body, outs, scratch, scalars, *args, megabytes=6, free=(), micros=1):
     return pl.pallas_call(
         body,
         out_shape=[jax.ShapeDtypeStruct(shape, dtype) for shape, dtype in outs],
-        in_specs=[SMEM] * scalars + [VMEM] * (len(args) - scalars),
+        in_specs=[SMEM if k < scalars else ANY if k in free else VMEM for k in range(len(args))],
         out_specs=[VMEM] * len(outs),
         scratch_shapes=scratch,
-        compiler_params=pltpu.CompilerParams(vmem_limit_bytes=48 << 20),
+        compiler_params=pltpu.CompilerParams(vmem_limit_bytes=megabytes << 20),
         name=body.__name__,
+        cost_estimate=pl.CostEstimate(flops=micros * 10**9, bytes_accessed=micros * 3 * 10**6, transcendentals=0),
     )(*args)
 
 
@@ -46,7 +49,7 @@
     return lax.ppermute(block, "filt", [(i, i ^ 1) for i in range(lax.axis_size("filt"))])
 
 
-def split_tile(place_ref, feat_ref, cot_ref, same_ref, other_ref, copies_ref, cells_ref, wide_ref):
+def split_tile(place_ref, feat_ref, cot_ref, same_ref, other_ref, cells_ref, wide_ref):
     odd = place_ref[0] == 1
     rows, columns, channels = feat_ref.shape
     half, cells = channels // 2, columns // 2
@@ -66,6 +69,9 @@
         low, high = grad[:, :half], grad[:, half:]
         same_ref[2 * rows + m] = jnp.where(odd, high, low).astype(BF16)
         other_ref[2 * rows + m] = jnp.where(odd, low, high).astype(BF16)
+
+
+def spread(cot_ref, copies_ref):
     for k in range(copies_ref.shape[0]):
         copies_ref[k] = cot_ref[...]
 
@@ -137,16 +143,23 @@
         out_ref[...] = (keep_ref[step] + cross_ref[step].astype(F32)).astype(BF16)
 
 
-def forward_and_kernel(place_ref, *refs):
-    chunks, (cot_ref, kernel_ref, conv_ref, keep_ref, send_ref, act_ref, coarse_ref, fine_ref) = refs[:-8], refs[-8:]
+def forward(place_ref, *refs):
+    chunks, (cot_ref, kernel_ref, conv_ref, keep_ref, send_ref, act_ref, coarse_ref, fine_ref, arrived) = refs[:-9], refs[-9:]
     steps = len(chunks) // 2
     planes, cells, half = chunks[0].shape
     height = act_ref.shape[0] // 4
     y, core = place_ref[1], place_ref[2]
+    copies = []
     for step in range(steps):
         pair = 2 * ((y + steps - step) % steps)
-        act_ref[pl.ds((pair + core) * planes, planes)] = chunks[2 * step][...]
-        act_ref[pl.ds((pair + 1 - core) * planes, planes)] = chunks[2 * step + 1][...]
+        for k, tile in ((2 * step, pair + core), (2 * step + 1, pair + 1 - core)):
+            copies.append(
+                pltpu.make_async_copy(chunks[k], act_ref.at[pl.ds(tile * planes, planes)], arrived.at[k])
+            )
+    for copy in copies:
+        copy.start()
+    for copy in copies:
+        copy.wait()
     column = lax.broadcasted_iota(jnp.int32, (cells, half), 0)
 
     def plane(i, a, b):
@@ -186,18 +199,17 @@
     lax.fori_loop(0, height, whole, 0, unroll=4)
     lax.fori_loop(1, height, between, 0, unroll=4)
 
-    tokens = height * cells
+    conv = jnp.dot(coarse_ref[...], kernel_ref[...], preferred_element_type=F32)
+    conv = conv + jnp.dot(fine_ref[...], kernel_ref[...], preferred_element_type=F32)
+    conv_ref[...] = conv.astype(BF16).reshape(conv_ref.shape)
     grad = lax.dot_general(
         coarse_ref[...],
-        cot_ref[...].reshape(tokens, -1),
+        cot_ref[...].reshape(coarse_ref.shape[0], -1),
         (((0,), (0,)), ((), ())),
         preferred_element_type=F32,
     ) * 0.25
     keep_ref[...] = grad
     send_ref[...] = grad.astype(BF16)
-    conv = jnp.dot(coarse_ref[...], kernel_ref[...], preferred_element_type=F32)
-    conv = conv + jnp.dot(fine_ref[...], kernel_ref[...], preferred_element_type=F32)
-    conv_ref[...] = conv.astype(BF16).reshape(conv_ref.shape)
 
 
 def input_side(place_ref, own_ref, *refs):
@@ -218,6 +230,17 @@
         other_ref[k] = jnp.where(odd, grads[0][k], grads[1][k]).astype(BF16)
 
 
+def pool(conv_ref, cells_ref, out_ref):
+    total = cells_ref[...]
+    for k in range(conv_ref.shape[0]):
+        total = total + conv_ref[k].astype(F32)
+    out_ref[...] = (total * 0.25).astype(BF16)
+
+
+def add_images(keep_ref, arrived_ref, out_ref):
+    out_ref[...] = keep_ref[...] + arrived_ref[...].astype(F32)
+
+
 def join_tile(place_ref, same_ref, other_ref, out_ref, low_ref, high_ref):
     odd = place_ref[0] == 1
     rows, columns, channels = out_ref.shape
@@ -242,12 +265,11 @@
     planes = 2 * tile_rows
 
     packed = planes + tile_rows // 2
-    same, other, copies, cell_sums = call(
+    same, other, cell_sums = call(
         split_tile,
         [
             ((packed, cells, half), BF16),
             ((packed, cells, half), BF16),
-            ((row_count,) + cotangent.shape[1:], BF16),
             ((tile_rows // 2, cells, channels), F32),
         ],
         [pltpu.VMEM((2, tile_rows, columns, half), F32)],
@@ -257,7 +279,27 @@
         cotangent[0],
     )
     same, other = swap_tiles((same, other))
+    steps = filt_count // 2
+    (copies,) = call(
+        spread, [((row_count,) + cotangent.shape[1:], BF16)], [], 0, cotangent[0]
+    )
     cot = lax.all_to_all(copies, "rows", 0, 0, tiled=True).reshape(height, cells, channels)
+    cross, keep = call(
+        back_conv,
+        [((steps, 2 * planes, cells, half), BF16), ((steps, 2 * planes, cells, half), F32)],
+        [
+            pltpu.VMEM(((height + 2) * cells, 4 * channels), BF16),
+            pltpu.VMEM((3, 2 * half, 4 * channels), BF16),
+            pltpu.VMEM((height, 4, cells, half), F32),
+        ],
+        1,
+        place,
+        cot,
+        kernel_flat,
+        megabytes=20,
+        micros=MU_BACK,
+    )
+    same, other, cross, keep = lax.optimization_barrier((same, other, cross, keep))
     act, slope, up = call(
         activate,
         [
@@ -271,24 +313,11 @@
         same,
         other,
     )
-    steps = filt_count // 2
+    moved = [to_y(act, step) for step in range(1, steps)]
     chunks = []
-    for block in [act] + [to_y(act, step) for step in range(1, steps)]:
+    for block in [act] + moved:
         chunks += [block, to_core(block)]
 
-    cross, keep = call(
-        back_conv,
-        [((steps, 2 * planes, cells, half), BF16), ((steps, 2 * planes, cells, half), F32)],
-        [
-            pltpu.VMEM(((height + 2) * cells, 4 * channels), BF16),
-            pltpu.VMEM((3, 2 * half, 4 * channels), BF16),
-            pltpu.VMEM((height, 4, cells, half), F32),
-        ],
-        1,
-        place,
-        cot,
-        kernel_flat,
-    )
     own, *terms = call(
         add_cores,
         [((2 * planes, cells, half), F32)] + [((2 * planes, cells, half), BF16)] * (steps - 1),
@@ -299,7 +328,7 @@
     )
     terms = [to_y(term, step) for step, term in enumerate(terms, 1)]
     conv, kernel_term, outgoing = call(
-        forward_and_kernel,
+        forward,
         [
             ((height, cells, channels), BF16),
             ((9 * half, channels), F32),
@@ -309,16 +338,20 @@
             pltpu.VMEM((4 * height, cells, half), BF16),
             pltpu.VMEM((height * cells, 9 * half), BF16),
             pltpu.VMEM((height * cells, 9 * half), BF16),
+            pltpu.SemaphoreType.DMA((2 * steps,)),
         ],
         1,
         place,
         *chunks,
         cot,
         kernel_flat,
-    )
+        megabytes=20,
+        micros=MU_FWD,
+        free=range(1, 1 + 2 * steps),
+    )
+    own, conv, outgoing = lax.optimization_barrier((own, conv, outgoing))
     arrived = lax.ppermute(outgoing, "rep", [(0, 1), (1, 0)])
     conv = lax.all_to_all(conv, "rows", 0, 0, tiled=True)
-
     same, other = call(
         input_side,
         [((planes, cells, half), BF16), ((planes, cells, half), BF16)],
@@ -329,8 +362,20 @@
         *terms,
         slope,
         up,
-    )
+        micros=MU_IN,
+    )
+
     same, other = swap_tiles((same, other))
+    (pooled,) = call(
+        pool,
+        [(cotangent.shape[1:], BF16)],
+        [],
+        0,
+        conv.reshape(row_count, tile_rows // 2, cells, channels),
+        cell_sums,
+        micros=MU_POOL,
+    )
+    pooled, same, other = lax.optimization_barrier((pooled, same, other))
     (input_grad,) = call(
         join_tile,
         [(features.shape[1:], BF16)],
@@ -339,10 +384,10 @@
         place,
         same,
         other,
-    )
-    kernel_grad = (kernel_term + arrived.astype(F32)).reshape(kernel.shape)
-    conv = conv.reshape(row_count, tile_rows // 2, cells, channels).astype(F32).sum(axis=0)
-    pooled = ((cell_sums + conv) * 0.25).astype(BF16)
+        micros=MU_JOIN,
+    )
+    (kernel_grad,) = call(add_images, [((9 * half, channels), F32)], [], 0, kernel_term, arrived, micros=MU_ADD)
+    kernel_grad = kernel_grad.reshape(kernel.shape)
     return (pooled[None], input_grad[None], kernel_grad)
 
 

time: 109 us -> 89.9 us (0.82); the launches traced: 107 us -> 89.5 us
  local copies, waits for them, and re-layouts: 12.8 us -> 1.66 us
  waiting for transfers between devices: 32.1 us -> 26.3 us
  other arithmetic: 4.05 us -> 0.08 us
  Pallas kernels: 14.3 us -> 16.2 us
  starting transfers between devices: 43.1 us -> 44.5 us
    unnamed x44 -> x12, local copies, waits for them, and re-layouts: 12.8 us -> 1.66 us
    ppermute x2, waiting for transfers between devices: 13.3 us -> 7.41 us  [swap_tiles(): lax.ppermute(pair[0], AXES, stay)]
    all_to_all x1, waiting for transfers between devices: 0.01 us -> 5.26 us  [local(): lax.all_to_all(copies, 'rows', 0, 0, tiled=True)]
    ppermute x6, waiting for transfers between devices: 12.7 us -> 7.53 us  [to_y(): lax.ppermute(block, 'filt', [(i, (i + 2 * step) % count) for i in range(c...]
    add x1 -> x0, other arithmetic: 2.22 us -> none  [local(): kernel_grad = (kernel_term + arrived.astype(F32)).reshape(kernel.shape)]
    pallas_call x7 -> x10, Pallas kernels: 14.3 us -> 16.2 us  [call(): pl.pallas_call(body, out_shape=[jax.ShapeDtypeStruct(shape, dtype) for sh...]
    ppermute x2, waiting for transfers between devices: 6.07 us -> 4.56 us  [swap_tiles(): lax.ppermute(pair[1], AXES, cross)]
    reduce_sum x1 -> x0, other arithmetic: 1.13 us -> none  [local(): conv.reshape(row_count, tile_rows // 2, cells, channels).astype(F32)]
  transfers between devices with their start and end apart: 18 -> 18, of which waited for: 9 -> 12; matrix products, arithmetic and copies ran while one was open for 2% -> 0% of each run, Pallas kernels for 12% -> 15%
where the time goes in v4:
time: 89.9 us; the launch traced here: 89.5 us
  starting transfers between devices  44.5 us (49%)
  waiting for transfers between devices  26.3 us (29%)
  Pallas kernels  16.2 us (18%)
  local copies, waits for them, and re-layouts  1.66 us (2%)
    pallas_call x10, Pallas kernels, call(): pl.pallas_call(body, out_shape=[jax.ShapeDtypeStruct(shape, dtype) for sh...  16.2 us
    ppermute x2, starting transfers between devices, swap_tiles(): lax.ppermute(pair[0], AXES, stay)  13.4 us
    all_to_all x1, starting transfers between devices, local(): lax.all_to_all(copies, 'rows', 0, 0, tiled=True)  9.51 us
    ppermute x6, waiting for transfers between devices, to_y(): lax.ppermute(block, 'filt', [(i, (i + 2 * step) % count) for i in range(c...  7.53 us
    ppermute x2, waiting for transfers between devices, swap_tiles(): lax.ppermute(pair[0], AXES, stay)  7.41 us
    ppermute x6, starting transfers between devices, to_y(): lax.ppermute(block, 'filt', [(i, (i + 2 * step) % count) for i in range(c...  6.5 us
    ppermute x2, starting transfers between devices, swap_tiles(): lax.ppermute(pair[1], AXES, cross)  5.91 us
    all_to_all x1, starting transfers between devices, local(): conv = lax.all_to_all(conv, 'rows', 0, 0, tiled=True)  5.38 us
  transfers between devices with their start and end apart: 18, of which 12 were waited for; matrix products, arithmetic and copies ran while one was open for 0% of the time, Pallas kernels for 15%

profile of v4, /device:TPU:56, one launch (start us, length us, event | category | flops | bytes accessed | tf_op | source)
XLA Modules:
  0.0 89.5 jit_solution(15057147085694920754)
XLA Ops:
  0.6 0.7 copy-done.2
  1.4 0.8 spread.1
  2.2 9.5 %all-to-all-start = ((bf16[16,2,32,256]{3,2,1,0:T(8,128)(2,1)}), bf16[16,2,32,256]{3,2,1,0:T(8,128)(2,1)S(1)}, u32[]{:S(2)}, u32[]{:S(2)}) async-start(bf16[16,2,32,256]{3,2,1,0:T(8,128)(2,1)} %spread.1), calls=%async_computation | async-start | bytes 1048576 | tf_op jit(solution)/shard_map/all_to_all | solution.py:286
  11.7 0.1 pad_add_fusion.place_ref
  11.8 0.6 split_tile.1
  12.4 6.9 %collective-permute-start = (bf16[10,32,128]{2,1,0:T(8,128)(2,1)S(1)}, bf16[10,32,128]{2,1,0:T(8,128)(2,1)S(1)}, u32[]{:S(2)}, u32[]{:S(2)}) collective-permute-start(bf16[10,32,128]{2,1,0:T(8,128)(2,1)S(1)} %get-tuple-element.30), channel_id=1, source_target_pairs={{0,0},{1,1},{2,2},{3,3},{4,32},{5,33},{6,34},{7,35},{8,64},{9,65},... | collective-permute-start | bytes 245768 | tf_op jit(solution)/shard_map/ppermute | solution.py:40
  19.4 2.7 %collective-permute-start.1 = (bf16[10,32,128]{2,1,0:T(8,128)(2,1)S(1)}, bf16[10,32,128]{2,1,0:T(8,128)(2,1)S(1)}, u32[]{:S(2)}, u32[]{:S(2)}) collective-permute-start(bf16[10,32,128]{2,1,0:T(8,128)(2,1)S(1)} %get-tuple-element.31), channel_id=1, source_target_pairs={{0,2},{1,3},{2,0},{3,1},{4,34},{5,35},{6,32},{7,33},{8,66},{9,67},... | collective-permute-start | bytes 245768 | tf_op jit(solution)/shard_map/ppermute | solution.py:40
  22.0 5.3 %all-to-all-done = bf16[16,2,32,256]{3,2,1,0:T(8,128)(2,1)S(1)} async-done(((bf16[16,2,32,256]{3,2,1,0:T(8,128)(2,1)}), bf16[16,2,32,256]{3,2,1,0:T(8,128)(2,1)S(1)}, u32[]{:S(2)}, u32[]{:S(2)}) %all-to-all-start) | async-done | bytes 524320 | tf_op jit(solution)/shard_map/all_to_all | solution.py:286
  27.3 4.1 %back_conv.1 = (bf16[4,16,32,128]{3,2,1,0:T(8,128)(2,1)S(1)}, f32[4,16,32,128]{3,2,1,0:T(8,128)S(1)}) custom-call(s32[3]{0:T(128)S(1)} %pad_add_fusion.place_ref, bf16[32,32,256]{2,1,0:T(8,128)(2,1)S(1)} %bitcast.11, bf16[1152,256]{1,0:T(8,128)(2,1)S(1)} %bitcast.14), custom_call_target="tpu_custom_call" | custom-call | flops 4000000000 | bytes 12000000 | tf_op jit(solution)/shard_map/back_conv/pallas_call | solution.py:18
  31.4 1.4 %collective-permute-done.same_ref = bf16[10,32,128]{2,1,0:T(8,128)(2,1)S(1)} collective-permute-done((bf16[10,32,128]{2,1,0:T(8,128)(2,1)S(1)}, bf16[10,32,128]{2,1,0:T(8,128)(2,1)S(1)}, u32[]{:S(2)}, u32[]{:S(2)}) %collective-permute-start) | collective-permute-done | bytes 81952 | tf_op jit(solution)/shard_map/ppermute | solution.py:40
  32.8 2.5 %collective-permute-done.1.other_ref = bf16[10,32,128]{2,1,0:T(8,128)(2,1)S(1)} collective-permute-done((bf16[10,32,128]{2,1,0:T(8,128)(2,1)S(1)}, bf16[10,32,128]{2,1,0:T(8,128)(2,1)S(1)}, u32[]{:S(2)}, u32[]{:S(2)}) %collective-permute-start.1) | collective-permute-done | bytes 81952 | tf_op jit(solution)/shard_map/ppermute | solution.py:40
  35.2 0.7 activate.1
  35.9 0.1 collective-permute-start.8
  36.0 0.6 collective-permute-start.6
  36.6 2.6 %collective-permute-start.4 = (bf16[16,32,128]{2,1,0:T(8,128)(2,1)S(1)}, bf16[16,32,128]{2,1,0:T(8,128)(2,1)S(1)}, u32[]{:S(2)}, u32[]{:S(2)}) collective-permute-start(bf16[16,32,128]{2,1,0:T(8,128)(2,1)S(1)} %get-tuple-element.39.refs_0_), channel_id=1, source_target_pairs={{0,64},{32,96},{64,128},{96,160},{128,192},{160,224},{192,0},{224,... | collective-permute-start | bytes 393224 | tf_op jit(solution)/shard_map/ppermute | solution.py:45
  39.2 4.3 %collective-permute-done.8.refs_6_ = bf16[16,32,128]{2,1,0:T(8,128)(2,1)S(1)} collective-permute-done((bf16[16,32,128]{2,1,0:T(8,128)(2,1)S(1)}, bf16[16,32,128]{2,1,0:T(8,128)(2,1)S(1)}, u32[]{:S(2)}, u32[]{:S(2)}) %collective-permute-start.8) | collective-permute-done | bytes 131104 | tf_op jit(solution)/shard_map/ppermute | solution.py:45
  43.6 0.0 collective-permute-start.9
  43.6 0.0 collective-permute-done.6.refs_4_
  43.6 0.5 collective-permute-start.7
  44.1 0.4 collective-permute-done.4.refs_2_
  44.5 0.5 collective-permute-start.2
  45.0 0.0 collective-permute-done.3.refs_1_
  45.0 0.0 collective-permute-done.9.refs_7_
  45.0 0.1 collective-permute-done.7.refs_5_
  45.1 0.7 collective-permute-done.5.refs_3_
  45.8 6.3 %forward.1 = (bf16[32,32,256]{2,1,0:T(8,128)(2,1)}, f32[1152,256]{1,0:T(8,128)S(1)}, bf16[1152,256]{1,0:T(8,128)(2,1)S(1)}) custom-call(s32[3]{0:T(128)S(1)} %pad_add_fusion.place_ref, bf16[16,32,128]{2,1,0:T(8,128)(2,1)S(1)} %get-tuple-element.39.refs_0_, bf16[16,32,128]{2,1,0:T(8,128)(2,1)S(1)} %collective-permute-done.3.refs_1_, ...), custom_call_target="tpu_custom_call" | custom-call | flops 6000000000 | bytes 18000000 | tf_op jit(solution)/shard_map/forward/pallas_call | solution.py:18
  52.1 0.0 copy-start.4
  52.1 0.0 collective-permute-done.2.cross_ref
  52.1 0.1 add_cores.1
  52.2 0.9 copy-done.4
  53.1 2.7 %collective-permute-start.15 = (bf16[1152,256]{1,0:T(8,128)(2,1)S(1)}, bf16[1152,256]{1,0:T(8,128)(2,1)S(1)}, u32[]{:S(2)}, u32[]{:S(2)}) collective-permute-start(bf16[1152,256]{1,0:T(8,128)(2,1)S(1)} %get-tuple-element.56), channel_id=1, source_target_pairs={{0,1},{1,0},{2,3},{3,2},{4,5},{5,4},{6,7},{7,6},{8,9},{9,8},{10,11... | collective-permute-start | bytes 1769480 | tf_op jit(solution)/shard_map/ppermute | solution.py:353
  55.8 2.3 %collective-permute-start.10 = (bf16[16,32,128]{2,1,0:T(8,128)(2,1)S(1)}, bf16[16,32,128]{2,1,0:T(8,128)(2,1)S(1)}, u32[]{:S(2)}, u32[]{:S(2)}) collective-permute-start(bf16[16,32,128]{2,1,0:T(8,128)(2,1)S(1)} %get-tuple-element.45), channel_id=1, source_target_pairs={{0,64},{32,96},{64,128},{96,160},{128,192},{160,224},{192,0},{224,... | collective-permute-start | bytes 393224 | tf_op jit(solution)/shard_map/ppermute | solution.py:45
  58.2 0.3 collective-permute-start.11
  58.5 0.5 collective-permute-start.12
  59.0 5.4 %all-to-all-start.1 = ((bf16[32,32,256]{2,1,0:T(8,128)(2,1)}), bf16[32,32,256]{2,1,0:T(8,128)(2,1)S(1)}, u32[]{:S(2)}, u32[]{:S(2)}) async-start(bf16[32,32,256]{2,1,0:T(8,128)(2,1)} %get-tuple-element.42), calls=%async_computation.1 | async-start | bytes 1048576 | tf_op jit(solution)/shard_map/all_to_all | solution.py:354
  64.4 0.0 collective-permute-done.10.refs_0_
  64.4 1.7 %collective-permute-done.11.refs_1_ = bf16[16,32,128]{2,1,0:T(8,128)(2,1)S(1)} collective-permute-done((bf16[16,32,128]{2,1,0:T(8,128)(2,1)S(1)}, bf16[16,32,128]{2,1,0:T(8,128)(2,1)S(1)}, u32[]{:S(2)}, u32[]{:S(2)}) %collective-permute-start.11) | collective-permute-done | bytes 131104 | tf_op jit(solution)/shard_map/ppermute | solution.py:45
  66.1 1.1 %collective-permute-done.12.refs_2_ = bf16[16,32,128]{2,1,0:T(8,128)(2,1)S(1)} collective-permute-done((bf16[16,32,128]{2,1,0:T(8,128)(2,1)S(1)}, bf16[16,32,128]{2,1,0:T(8,128)(2,1)S(1)}, u32[]{:S(2)}, u32[]{:S(2)}) %collective-permute-start.12) | collective-permute-done | bytes 131104 | tf_op jit(solution)/shard_map/ppermute | solution.py:45
  67.2 0.6 input_side.1
  67.8 6.5 %collective-permute-start.13 = (bf16[8,32,128]{2,1,0:T(8,128)(2,1)S(1)}, bf16[8,32,128]{2,1,0:T(8,128)(2,1)S(1)}, u32[]{:S(2)}, u32[]{:S(2)}) collective-permute-start(bf16[8,32,128]{2,1,0:T(8,128)(2,1)S(1)} %get-tuple-element.50), channel_id=1, source_target_pairs={{0,0},{1,1},{2,2},{3,3},{4,32},{5,33},{6,34},{7,35},{8,64},{9,65},... | collective-permute-start | bytes 196616 | tf_op jit(solution)/shard_map/ppermute | solution.py:40
  74.3 3.3 %collective-permute-start.14 = (bf16[8,32,128]{2,1,0:T(8,128)(2,1)S(1)}, bf16[8,32,128]{2,1,0:T(8,128)(2,1)S(1)}, u32[]{:S(2)}, u32[]{:S(2)}) collective-permute-start(bf16[8,32,128]{2,1,0:T(8,128)(2,1)S(1)} %get-tuple-element.51), channel_id=1, source_target_pairs={{0,2},{1,3},{2,0},{3,1},{4,34},{5,35},{6,32},{7,33},{8,66},{9,67},... | collective-permute-start | bytes 196616 | tf_op jit(solution)/shard_map/ppermute | solution.py:40
  77.6 0.0 collective-permute-done.15.arrived_ref
  77.6 1.1 %add_images.1 = f32[1152,256]{1,0:T(8,128)} custom-call(f32[1152,256]{1,0:T(8,128)S(1)} %copy-done.5, bf16[1152,256]{1,0:T(8,128)(2,1)S(1)} %collective-permute-done.15.arrived_ref), custom_call_target="tpu_custom_call" | custom-call | flops 60000002048 | bytes 180000000 | tf_op jit(solution)/shard_map/add_images/pallas_call | solution.py:18
  78.7 0.7 all-to-all-done.1
  79.4 0.7 pool.1
  80.1 6.0 %collective-permute-done.13.same_ref = bf16[8,32,128]{2,1,0:T(8,128)(2,1)S(1)} collective-permute-done((bf16[8,32,128]{2,1,0:T(8,128)(2,1)S(1)}, bf16[8,32,128]{2,1,0:T(8,128)(2,1)S(1)}, u32[]{:S(2)}, u32[]{:S(2)}) %collective-permute-start.13) | collective-permute-done | bytes 65568 | tf_op jit(solution)/shard_map/ppermute | solution.py:40
  86.1 2.1 %collective-permute-done.14.other_ref = bf16[8,32,128]{2,1,0:T(8,128)(2,1)S(1)} collective-permute-done((bf16[8,32,128]{2,1,0:T(8,128)(2,1)S(1)}, bf16[8,32,128]{2,1,0:T(8,128)(2,1)S(1)}, u32[]{:S(2)}, u32[]{:S(2)}) %collective-permute-start.14) | collective-permute-done | bytes 65568 | tf_op jit(solution)/shard_map/ppermute | solution.py:40
  88.2 1.2 %join_tile.1 = bf16[4,64,256]{2,1,0:T(8,128)(2,1)} custom-call(s32[3]{0:T(128)S(1)} %pad_add_fusion.place_ref, bf16[8,32,128]{2,1,0:T(8,128)(2,1)S(1)} %collective-permute-done.13.same_ref, bf16[8,32,128]{2,1,0:T(8,128)(2,1)S(1)} %collective-permute-done.14.other_ref), custom_call_target="tpu_custom_call" | custom-call | flops 1000000000 | bytes 3000000 | tf_op jit(solution)/shard_map/join_tile/pallas_call | solution.py:18
  (11 shorter events, 0.0 us)
Async XLA Ops:
  0.6 0.8 copy-start.2
  1.4 10.4 %copy-start.1 = (bf16[1,4,64,256]{3,2,1,0:T(8,128)(2,1)S(1)}, bf16[1,4,64,256]{3,2,1,0:T(8,128)(2,1)}, u32[]{:S(2)}) copy-start(bf16[1,4,64,256]{3,2,1,0:T(8,128)(2,1)} %param.3) | copy-start | bytes 393220
  1.4 10.4 %copy-start.3 = (bf16[1,2,32,256]{3,2,1,0:T(8,128)(2,1)S(1)}, bf16[1,2,32,256]{3,2,1,0:T(8,128)(2,1)}, u32[]{:S(2)}) copy-start(bf16[1,2,32,256]{3,2,1,0:T(8,128)(2,1)} %param.5) | copy-start | bytes 98308
  2.2 25.1 %all-to-all-start = ((bf16[16,2,32,256]{3,2,1,0:T(8,128)(2,1)}), bf16[16,2,32,256]{3,2,1,0:T(8,128)(2,1)S(1)}, u32[]{:S(2)}, u32[]{:S(2)}) async-start(bf16[16,2,32,256]{3,2,1,0:T(8,128)(2,1)} %spread.1), calls=%async_computation | async-start | bytes 1048576 | tf_op jit(solution)/shard_map/all_to_all | solution.py:286
  11.8 15.5 %copy-start = (bf16[3,3,128,256]{3,2,1,0:T(8,128)(2,1)S(1)}, bf16[3,3,128,256]{3,2,1,0:T(8,128)(2,1)}, u32[]{:S(2)}) copy-start(bf16[3,3,128,256]{3,2,1,0:T(8,128)(2,1)} %param.4) | copy-start | bytes 1769476
  12.4 20.4 %collective-permute-start = (bf16[10,32,128]{2,1,0:T(8,128)(2,1)S(1)}, bf16[10,32,128]{2,1,0:T(8,128)(2,1)S(1)}, u32[]{:S(2)}, u32[]{:S(2)}) collective-permute-start(bf16[10,32,128]{2,1,0:T(8,128)(2,1)S(1)} %get-tuple-element.30), channel_id=1, source_target_pairs={{0,0},{1,1},{2,2},{3,3},{4,32},{5,33},{6,34},{7,35},{8,64},{9,65},... | collective-permute-start | bytes 245768 | tf_op jit(solution)/shard_map/ppermute | solution.py:40
  19.4 15.9 %collective-permute-start.1 = (bf16[10,32,128]{2,1,0:T(8,128)(2,1)S(1)}, bf16[10,32,128]{2,1,0:T(8,128)(2,1)S(1)}, u32[]{:S(2)}, u32[]{:S(2)}) collective-permute-start(bf16[10,32,128]{2,1,0:T(8,128)(2,1)S(1)} %get-tuple-element.31), channel_id=1, source_target_pairs={{0,2},{1,3},{2,0},{3,1},{4,34},{5,35},{6,32},{7,33},{8,66},{9,67},... | collective-permute-start | bytes 245768 | tf_op jit(solution)/shard_map/ppermute | solution.py:40
  35.9 7.7 %collective-permute-start.8 = (bf16[16,32,128]{2,1,0:T(8,128)(2,1)S(1)}, bf16[16,32,128]{2,1,0:T(8,128)(2,1)S(1)}, u32[]{:S(2)}, u32[]{:S(2)}) collective-permute-start(bf16[16,32,128]{2,1,0:T(8,128)(2,1)S(1)} %get-tuple-element.39.refs_0_), channel_id=1, source_target_pairs={{0,192},{32,224},{64,0},{96,32},{128,64},{160,96},{192,128},{224,1... | collective-permute-start | bytes 393224 | tf_op jit(solution)/shard_map/ppermute | solution.py:45
  36.0 7.6 %collective-permute-start.6 = (bf16[16,32,128]{2,1,0:T(8,128)(2,1)S(1)}, bf16[16,32,128]{2,1,0:T(8,128)(2,1)S(1)}, u32[]{:S(2)}, u32[]{:S(2)}) collective-permute-start(bf16[16,32,128]{2,1,0:T(8,128)(2,1)S(1)} %get-tuple-element.39.refs_0_), channel_id=1, source_target_pairs={{0,128},{32,160},{64,192},{96,224},{128,0},{160,32},{192,64},{224,... | collective-permute-start | bytes 393224 | tf_op jit(solution)/shard_map/ppermute | solution.py:45
  36.6 7.9 %collective-permute-start.4 = (bf16[16,32,128]{2,1,0:T(8,128)(2,1)S(1)}, bf16[16,32,128]{2,1,0:T(8,128)(2,1)S(1)}, u32[]{:S(2)}, u32[]{:S(2)}) collective-permute-start(bf16[16,32,128]{2,1,0:T(8,128)(2,1)S(1)} %get-tuple-element.39.refs_0_), channel_id=1, source_target_pairs={{0,64},{32,96},{64,128},{96,160},{128,192},{160,224},{192,0},{224,... | collective-permute-start | bytes 393224 | tf_op jit(solution)/shard_map/ppermute | solution.py:45
  39.2 5.8 %collective-permute-start.3 = (bf16[16,32,128]{2,1,0:T(8,128)(2,1)S(1)}, bf16[16,32,128]{2,1,0:T(8,128)(2,1)S(1)}, u32[]{:S(2)}, u32[]{:S(2)}) collective-permute-start(bf16[16,32,128]{2,1,0:T(8,128)(2,1)S(1)} %get-tuple-element.39.refs_0_), channel_id=1, source_target_pairs={{0,32},{32,0},{64,96},{96,64},{128,160},{160,128},{192,224},{224,1... | collective-permute-start | bytes 393224 | tf_op jit(solution)/shard_map/ppermute | solution.py:49
  43.6 1.4 %collective-permute-start.9 = (bf16[16,32,128]{2,1,0:T(8,128)(2,1)S(1)}, bf16[16,32,128]{2,1,0:T(8,128)(2,1)S(1)}, u32[]{:S(2)}, u32[]{:S(2)}) collective-permute-start(bf16[16,32,128]{2,1,0:T(8,128)(2,1)S(1)} %collective-permute-done.8.refs_6_), channel_id=1, source_target_pairs={{0,32},{32,0},{64,96},{96,64},{128,160},{160,128},{192,224},{224,1... | collective-permute-start | bytes 393224 | tf_op jit(solution)/shard_map/ppermute | solution.py:49
  43.6 1.5 %collective-permute-start.7 = (bf16[16,32,128]{2,1,0:T(8,128)(2,1)S(1)}, bf16[16,32,128]{2,1,0:T(8,128)(2,1)S(1)}, u32[]{:S(2)}, u32[]{:S(2)}) collective-permute-start(bf16[16,32,128]{2,1,0:T(8,128)(2,1)S(1)} %collective-permute-done.6.refs_4_), channel_id=1, source_target_pairs={{0,32},{32,0},{64,96},{96,64},{128,160},{160,128},{192,224},{224,1... | collective-permute-start | bytes 393224 | tf_op jit(solution)/shard_map/ppermute | solution.py:49
  44.5 1.3 %collective-permute-start.5 = (bf16[16,32,128]{2,1,0:T(8,128)(2,1)S(1)}, bf16[16,32,128]{2,1,0:T(8,128)(2,1)S(1)}, u32[]{:S(2)}, u32[]{:S(2)}) collective-permute-start(bf16[16,32,128]{2,1,0:T(8,128)(2,1)S(1)} %collective-permute-done.4.refs_2_), channel_id=1, source_target_pairs={{0,32},{32,0},{64,96},{96,64},{128,160},{160,128},{192,224},{224,1... | collective-permute-start | bytes 393224 | tf_op jit(solution)/shard_map/ppermute | solution.py:49
  44.5 7.6 %collective-permute-start.2 = (bf16[4,16,32,128]{3,2,1,0:T(8,128)(2,1)S(1)}, bf16[4,16,32,128]{3,2,1,0:T(8,128)(2,1)S(1)}, u32[]{:S(2)}, u32[]{:S(2)}) collective-permute-start(bf16[4,16,32,128]{3,2,1,0:T(8,128)(2,1)S(1)} %get-tuple-element.35), channel_id=1, source_target_pairs={{0,32},{32,0},{64,96},{96,64},{128,160},{160,128},{192,224},{224,1... | collective-permute-start | bytes 1572872 | tf_op jit(solution)/shard_map/ppermute | solution.py:49
  52.1 1.0 %copy-start.4 = (f32[1152,256]{1,0:T(8,128)}, f32[1152,256]{1,0:T(8,128)S(1)}, u32[]{:S(2)}) copy-start(f32[1152,256]{1,0:T(8,128)S(1)} %get-tuple-element.55.keep_ref) | copy-start | bytes 3538948
  53.1 24.5 %collective-permute-start.15 = (bf16[1152,256]{1,0:T(8,128)(2,1)S(1)}, bf16[1152,256]{1,0:T(8,128)(2,1)S(1)}, u32[]{:S(2)}, u32[]{:S(2)}) collective-permute-start(bf16[1152,256]{1,0:T(8,128)(2,1)S(1)} %get-tuple-element.56), channel_id=1, source_target_pairs={{0,1},{1,0},{2,3},{3,2},{4,5},{5,4},{6,7},{7,6},{8,9},{9,8},{10,11... | collective-permute-start | bytes 1769480 | tf_op jit(solution)/shard_map/ppermute | solution.py:353
  55.8 8.6 %collective-permute-start.10 = (bf16[16,32,128]{2,1,0:T(8,128)(2,1)S(1)}, bf16[16,32,128]{2,1,0:T(8,128)(2,1)S(1)}, u32[]{:S(2)}, u32[]{:S(2)}) collective-permute-start(bf16[16,32,128]{2,1,0:T(8,128)(2,1)S(1)} %get-tuple-element.45), channel_id=1, source_target_pairs={{0,64},{32,96},{64,128},{96,160},{128,192},{160,224},{192,0},{224,... | collective-permute-start | bytes 393224 | tf_op jit(solution)/shard_map/ppermute | solution.py:45
  58.2 7.9 %collective-permute-start.11 = (bf16[16,32,128]{2,1,0:T(8,128)(2,1)S(1)}, bf16[16,32,128]{2,1,0:T(8,128)(2,1)S(1)}, u32[]{:S(2)}, u32[]{:S(2)}) collective-permute-start(bf16[16,32,128]{2,1,0:T(8,128)(2,1)S(1)} %get-tuple-element.46), channel_id=1, source_target_pairs={{0,128},{32,160},{64,192},{96,224},{128,0},{160,32},{192,64},{224,... | collective-permute-start | bytes 393224 | tf_op jit(solution)/shard_map/ppermute | solution.py:45
  58.5 8.7 %collective-permute-start.12 = (bf16[16,32,128]{2,1,0:T(8,128)(2,1)S(1)}, bf16[16,32,128]{2,1,0:T(8,128)(2,1)S(1)}, u32[]{:S(2)}, u32[]{:S(2)}) collective-permute-start(bf16[16,32,128]{2,1,0:T(8,128)(2,1)S(1)} %get-tuple-element.47), channel_id=1, source_target_pairs={{0,192},{32,224},{64,0},{96,32},{128,64},{160,96},{192,128},{224,1... | collective-permute-start | bytes 393224 | tf_op jit(solution)/shard_map/ppermute | solution.py:45
  59.0 20.4 %all-to-all-start.1 = ((bf16[32,32,256]{2,1,0:T(8,128)(2,1)}), bf16[32,32,256]{2,1,0:T(8,128)(2,1)S(1)}, u32[]{:S(2)}, u32[]{:S(2)}) async-start(bf16[32,32,256]{2,1,0:T(8,128)(2,1)} %get-tuple-element.42), calls=%async_computation.1 | async-start | bytes 1048576 | tf_op jit(solution)/shard_map/all_to_all | solution.py:354
  67.2 10.4 %copy-start.5 = (f32[1152,256]{1,0:T(8,128)S(1)}, f32[1152,256]{1,0:T(8,128)}, u32[]{:S(2)}) copy-start(f32[1152,256]{1,0:T(8,128)} %copy-done.4) | copy-start | bytes 3538948
  67.8 18.3 %collective-permute-start.13 = (bf16[8,32,128]{2,1,0:T(8,128)(2,1)S(1)}, bf16[8,32,128]{2,1,0:T(8,128)(2,1)S(1)}, u32[]{:S(2)}, u32[]{:S(2)}) collective-permute-start(bf16[8,32,128]{2,1,0:T(8,128)(2,1)S(1)} %get-tuple-element.50), channel_id=1, source_target_pairs={{0,0},{1,1},{2,2},{3,3},{4,32},{5,33},{6,34},{7,35},{8,64},{9,65},... | collective-permute-start | bytes 196616 | tf_op jit(solution)/shard_map/ppermute | solution.py:40
  74.3 13.9 %collective-permute-start.14 = (bf16[8,32,128]{2,1,0:T(8,128)(2,1)S(1)}, bf16[8,32,128]{2,1,0:T(8,128)(2,1)S(1)}, u32[]{:S(2)}, u32[]{:S(2)}) collective-permute-start(bf16[8,32,128]{2,1,0:T(8,128)(2,1)S(1)} %get-tuple-element.51), channel_id=1, source_target_pairs={{0,2},{1,3},{2,0},{3,1},{4,34},{5,35},{6,32},{7,33},{8,66},{9,67},... | collective-permute-start | bytes 196616 | tf_op jit(solution)/shard_map/ppermute | solution.py:40

commit v5 on v4

--- a/solution.py
+++ b/solution.py
@@ -5,6 +5,7 @@
 from jax.experimental.pallas import tpu as pltpu
 from jax.sharding import PartitionSpec as P
 
+MU_ACT = 15
 MU_POOL, MU_ADD, MU_JOIN, MU_IN, MU_BACK, MU_FWD = 10, 60, 1, 1, 4, 6
 AXES = ("filt", "rows", "rep")
 VMEM = pl.BlockSpec(memory_space=pltpu.VMEM)
@@ -71,7 +72,8 @@
         other_ref[2 * rows + m] = jnp.where(odd, low, high).astype(BF16)
 
 
-def spread(cot_ref, copies_ref):
+def spread(cot_ref, packed_ref, copies_ref):
+    del packed_ref
     for k in range(copies_ref.shape[0]):
         copies_ref[k] = cot_ref[...]
 
@@ -278,12 +280,28 @@
         features[0],
         cotangent[0],
     )
+    packed_same = same
     same, other = swap_tiles((same, other))
     steps = filt_count // 2
     (copies,) = call(
-        spread, [((row_count,) + cotangent.shape[1:], BF16)], [], 0, cotangent[0]
+        spread, [((row_count,) + cotangent.shape[1:], BF16)], [], 0, cotangent[0], packed_same, free=(1,)
     )
     cot = lax.all_to_all(copies, "rows", 0, 0, tiled=True).reshape(height, cells, channels)
+    act, slope, up = call(
+        activate,
+        [
+            ((2 * planes, cells, half), BF16),
+            ((2 * planes, cells, half), F32),
+            ((tile_rows, cells, half), F32),
+        ],
+        [],
+        1,
+        place,
+        same,
+        other,
+        micros=MU_ACT,
+    )
+    cot, _ = lax.optimization_barrier((cot, act))
     cross, keep = call(
         back_conv,
         [((steps, 2 * planes, cells, half), BF16), ((steps, 2 * planes, cells, half), F32)],
@@ -298,20 +316,6 @@
         kernel_flat,
         megabytes=20,
         micros=MU_BACK,
-    )
-    same, other, cross, keep = lax.optimization_barrier((same, other, cross, keep))
-    act, slope, up = call(
-        activate,
-        [
-            ((2 * planes, cells, half), BF16),
-            ((2 * planes, cells, half), F32),
-            ((tile_rows, cells, half), F32),
-        ],
-        [],
-        1,
-        place,
-        same,
-        other,
     )
     moved = [to_y(act, step) for step in range(1, steps)]
     chunks = []

time: 89.9 us -> 84 us (0.934)
  starting transfers between devices: 44.5 us -> 40.5 us
  waiting for transfers between devices: 26.3 us -> 23.4 us
    ppermute x2, starting transfers between devices: 13.4 us -> 8.83 us  [swap_tiles(): lax.ppermute(pair[0], AXES, stay)]
    ppermute x2, starting transfers between devices: 5.91 us -> 10.4 us  [swap_tiles(): lax.ppermute(pair[1], AXES, cross)]
    all_to_all x1, starting transfers between devices: 9.51 us -> 6.51 us  [local(): lax.all_to_all(copies, 'rows', 0, 0, tiled=True)]
    all_to_all x1, waiting for transfers between devices: 5.26 us -> 2.81 us  [local(): lax.all_to_all(copies, 'rows', 0, 0, tiled=True)]
    ppermute x2, waiting for transfers between devices: 4.56 us -> 2.11 us  [swap_tiles(): lax.ppermute(pair[1], AXES, cross)]
    ppermute x2, waiting for transfers between devices: 7.41 us -> 9.44 us  [swap_tiles(): lax.ppermute(pair[0], AXES, stay)]
    ppermute x6, waiting for transfers between devices: 7.53 us -> 9 us  [to_y(): lax.ppermute(block, 'filt', [(i, (i + 2 * step) % count) for i in range(c...]
    all_to_all x1, starting transfers between devices: 5.38 us -> 4.48 us  [local(): conv = lax.all_to_all(conv, 'rows', 0, 0, tiled=True)]
  transfers between devices with their start and end apart: 18 -> 18, of which waited for: 12 -> 9; matrix products, arithmetic and copies ran while one was open for 0% -> 0% of each run, Pallas kernels for 15% -> 17%
where the time goes in v5:
time: 84 us; the launch traced here: 83.5 us
  starting transfers between devices  40.5 us (48%)
  waiting for transfers between devices  23.4 us (28%)
  Pallas kernels  16.2 us (19%)
  local copies, waits for them, and re-layouts  2.54 us (3%)
    pallas_call x10, Pallas kernels, call(): pl.pallas_call(body, out_shape=[jax.ShapeDtypeStruct(shape, dtype) for sh...  16.2 us
    ppermute x2, starting transfers between devices, swap_tiles(): lax.ppermute(pair[1], AXES, cross)  10.4 us
    ppermute x2, waiting for transfers between devices, swap_tiles(): lax.ppermute(pair[0], AXES, stay)  9.44 us
    ppermute x6, waiting for transfers between devices, to_y(): lax.ppermute(block, 'filt', [(i, (i + 2 * step) % count) for i in range(c...  9 us
    ppermute x2, starting transfers between devices, swap_tiles(): lax.ppermute(pair[0], AXES, stay)  8.83 us
    ppermute x6, starting transfers between devices, to_y(): lax.ppermute(block, 'filt', [(i, (i + 2 * step) % count) for i in range(c...  6.6 us
    all_to_all x1, starting transfers between devices, local(): lax.all_to_all(copies, 'rows', 0, 0, tiled=True)  6.51 us
    all_to_all x1, starting transfers between devices, local(): conv = lax.all_to_all(conv, 'rows', 0, 0, tiled=True)  4.48 us
  transfers between devices with their start and end apart: 18, of which 9 were waited for; matrix products, arithmetic and copies ran while one was open for 0% of the time, Pallas kernels for 17%

profile of v5, /device:TPU:56, one launch (start us, length us, event | category | flops | bytes accessed | tf_op | source)
XLA Modules:
  0.0 83.5 jit_solution(8167547173458998226)
XLA Ops:
  0.7 0.1 pad_add_fusion.place_ref
  0.7 0.9 %copy-done.1 = bf16[1,4,64,256]{3,2,1,0:T(8,128)(2,1)S(1)} copy-done((bf16[1,4,64,256]{3,2,1,0:T(8,128)(2,1)S(1)}, bf16[1,4,64,256]{3,2,1,0:T(8,128)(2,1)}, u32[]{:S(2)}) %copy-start.1) | copy-done | bytes 131096
  1.6 0.8 copy-done.2
  2.4 0.6 split_tile.1
  3.0 6.5 %collective-permute-start.1 = (bf16[10,32,128]{2,1,0:T(8,128)(2,1)S(1)}, bf16[10,32,128]{2,1,0:T(8,128)(2,1)S(1)}, u32[]{:S(2)}, u32[]{:S(2)}) collective-permute-start(bf16[10,32,128]{2,1,0:T(8,128)(2,1)S(1)} %get-tuple-element.28), channel_id=1, source_target_pairs={{0,2},{1,3},{2,0},{3,1},{4,34},{5,35},{6,32},{7,33},{8,66},{9,67},... | collective-permute-start | bytes 245768 | tf_op jit(solution)/shard_map/ppermute | solution.py:41
  9.5 3.1 %collective-permute-start = (bf16[10,32,128]{2,1,0:T(8,128)(2,1)S(1)}, bf16[10,32,128]{2,1,0:T(8,128)(2,1)S(1)}, u32[]{:S(2)}, u32[]{:S(2)}) collective-permute-start(bf16[10,32,128]{2,1,0:T(8,128)(2,1)S(1)} %get-tuple-element.27.packed_ref), channel_id=1, source_target_pairs={{0,0},{1,1},{2,2},{3,3},{4,32},{5,33},{6,34},{7,35},{8,64},{9,65},... | collective-permute-start | bytes 245768 | tf_op jit(solution)/shard_map/ppermute | solution.py:41
  12.6 0.8 spread.1
  13.4 6.5 %all-to-all-start = ((bf16[16,2,32,256]{3,2,1,0:T(8,128)(2,1)}), bf16[16,2,32,256]{3,2,1,0:T(8,128)(2,1)S(1)}, u32[]{:S(2)}, u32[]{:S(2)}) async-start(bf16[16,2,32,256]{3,2,1,0:T(8,128)(2,1)} %spread.1), calls=%async_computation | async-start | bytes 1048576 | tf_op jit(solution)/shard_map/all_to_all | solution.py:289
  19.9 0.0 collective-permute-done.1.other_ref
  19.9 3.2 %collective-permute-done.same_ref = bf16[10,32,128]{2,1,0:T(8,128)(2,1)S(1)} collective-permute-done((bf16[10,32,128]{2,1,0:T(8,128)(2,1)S(1)}, bf16[10,32,128]{2,1,0:T(8,128)(2,1)S(1)}, u32[]{:S(2)}, u32[]{:S(2)}) %collective-permute-start) | collective-permute-done | bytes 81952 | tf_op jit(solution)/shard_map/ppermute | solution.py:41
  23.1 0.7 activate.1
  23.8 0.1 collective-permute-start.8
  23.9 2.4 %collective-permute-start.6 = (bf16[16,32,128]{2,1,0:T(8,128)(2,1)S(1)}, bf16[16,32,128]{2,1,0:T(8,128)(2,1)S(1)}, u32[]{:S(2)}, u32[]{:S(2)}) collective-permute-start(bf16[16,32,128]{2,1,0:T(8,128)(2,1)S(1)} %get-tuple-element.29.refs_0_), channel_id=1, source_target_pairs={{0,128},{32,160},{64,192},{96,224},{128,0},{160,32},{192,64},{224,... | collective-permute-start | bytes 393224 | tf_op jit(solution)/shard_map/ppermute | solution.py:46
  26.3 0.8 collective-permute-start.4
  27.1 0.0 collective-permute-start.3
  27.1 5.2 %collective-permute-done.8.refs_6_ = bf16[16,32,128]{2,1,0:T(8,128)(2,1)S(1)} collective-permute-done((bf16[16,32,128]{2,1,0:T(8,128)(2,1)S(1)}, bf16[16,32,128]{2,1,0:T(8,128)(2,1)S(1)}, u32[]{:S(2)}, u32[]{:S(2)}) %collective-permute-start.8) | collective-permute-done | bytes 131104 | tf_op jit(solution)/shard_map/ppermute | solution.py:46
  32.3 0.0 collective-permute-start.9
  32.3 0.0 collective-permute-done.6.refs_4_
  32.3 0.5 collective-permute-start.7
  32.8 0.1 collective-permute-done.4.refs_2_
  32.9 2.8 %all-to-all-done = bf16[16,2,32,256]{3,2,1,0:T(8,128)(2,1)S(1)} async-done(((bf16[16,2,32,256]{3,2,1,0:T(8,128)(2,1)}), bf16[16,2,32,256]{3,2,1,0:T(8,128)(2,1)S(1)}, u32[]{:S(2)}, u32[]{:S(2)}) %all-to-all-start) | async-done | bytes 524320 | tf_op jit(solution)/shard_map/all_to_all | solution.py:289
  35.7 4.1 %back_conv.1 = (bf16[4,16,32,128]{3,2,1,0:T(8,128)(2,1)S(1)}, f32[4,16,32,128]{3,2,1,0:T(8,128)S(1)}) custom-call(s32[3]{0:T(128)S(1)} %pad_add_fusion.place_ref, bf16[32,32,256]{2,1,0:T(8,128)(2,1)S(1)} %bitcast.11, bf16[1152,256]{1,0:T(8,128)(2,1)S(1)} %bitcast.14), custom_call_target="tpu_custom_call" | custom-call | flops 4000000000 | bytes 12000000 | tf_op jit(solution)/shard_map/back_conv/pallas_call | solution.py:19
  39.8 0.1 collective-permute-start.2
  39.9 0.0 collective-permute-done.3.refs_1_
  39.9 0.0 collective-permute-done.7.refs_5_
  39.9 0.0 collective-permute-done.5.refs_3_
  39.9 6.3 %forward.1 = (bf16[32,32,256]{2,1,0:T(8,128)(2,1)}, f32[1152,256]{1,0:T(8,128)S(1)}, bf16[1152,256]{1,0:T(8,128)(2,1)S(1)}) custom-call(s32[3]{0:T(128)S(1)} %pad_add_fusion.place_ref, bf16[16,32,128]{2,1,0:T(8,128)(2,1)S(1)} %get-tuple-element.29.refs_0_, bf16[16,32,128]{2,1,0:T(8,128)(2,1)S(1)} %collective-permute-done.3.refs_1_, ...), custom_call_target="tpu_custom_call" | custom-call | flops 6000000000 | bytes 18000000 | tf_op jit(solution)/shard_map/forward/pallas_call | solution.py:19
  46.2 0.0 copy-start.4
  46.2 0.0 collective-permute-done.2.cross_ref
  46.2 0.1 add_cores.1
  46.4 0.9 %copy-done.4 = f32[1152,256]{1,0:T(8,128)} copy-done((f32[1152,256]{1,0:T(8,128)}, f32[1152,256]{1,0:T(8,128)S(1)}, u32[]{:S(2)}) %copy-start.4) | copy-done | bytes 1179672
  47.2 3.0 %collective-permute-start.15 = (bf16[1152,256]{1,0:T(8,128)(2,1)S(1)}, bf16[1152,256]{1,0:T(8,128)(2,1)S(1)}, u32[]{:S(2)}, u32[]{:S(2)}) collective-permute-start(bf16[1152,256]{1,0:T(8,128)(2,1)S(1)} %get-tuple-element.50), channel_id=1, source_target_pairs={{0,1},{1,0},{2,3},{3,2},{4,5},{5,4},{6,7},{7,6},{8,9},{9,8},{10,11... | collective-permute-start | bytes 1769480 | tf_op jit(solution)/shard_map/ppermute | solution.py:357
  50.3 1.9 %collective-permute-start.10 = (bf16[16,32,128]{2,1,0:T(8,128)(2,1)S(1)}, bf16[16,32,128]{2,1,0:T(8,128)(2,1)S(1)}, u32[]{:S(2)}, u32[]{:S(2)}) collective-permute-start(bf16[16,32,128]{2,1,0:T(8,128)(2,1)S(1)} %get-tuple-element.39), channel_id=1, source_target_pairs={{0,64},{32,96},{64,128},{96,160},{128,192},{160,224},{192,0},{224,... | collective-permute-start | bytes 393224 | tf_op jit(solution)/shard_map/ppermute | solution.py:46
  52.1 0.7 collective-permute-start.11
  52.9 0.7 collective-permute-start.12
  53.6 4.5 %all-to-all-start.1 = ((bf16[32,32,256]{2,1,0:T(8,128)(2,1)}), bf16[32,32,256]{2,1,0:T(8,128)(2,1)S(1)}, u32[]{:S(2)}, u32[]{:S(2)}) async-start(bf16[32,32,256]{2,1,0:T(8,128)(2,1)} %get-tuple-element.36), calls=%async_computation.1 | async-start | bytes 1048576 | tf_op jit(solution)/shard_map/all_to_all | solution.py:358
  58.0 0.1 collective-permute-done.10.refs_0_
  58.1 1.9 %collective-permute-done.11.refs_1_ = bf16[16,32,128]{2,1,0:T(8,128)(2,1)S(1)} collective-permute-done((bf16[16,32,128]{2,1,0:T(8,128)(2,1)S(1)}, bf16[16,32,128]{2,1,0:T(8,128)(2,1)S(1)}, u32[]{:S(2)}, u32[]{:S(2)}) %collective-permute-start.11) | collective-permute-done | bytes 131104 | tf_op jit(solution)/shard_map/ppermute | solution.py:46
  60.0 1.7 %collective-permute-done.12.refs_2_ = bf16[16,32,128]{2,1,0:T(8,128)(2,1)S(1)} collective-permute-done((bf16[16,32,128]{2,1,0:T(8,128)(2,1)S(1)}, bf16[16,32,128]{2,1,0:T(8,128)(2,1)S(1)}, u32[]{:S(2)}, u32[]{:S(2)}) %collective-permute-start.12) | collective-permute-done | bytes 131104 | tf_op jit(solution)/shard_map/ppermute | solution.py:46
  61.8 0.6 input_side.1
  62.4 5.8 %collective-permute-start.13 = (bf16[8,32,128]{2,1,0:T(8,128)(2,1)S(1)}, bf16[8,32,128]{2,1,0:T(8,128)(2,1)S(1)}, u32[]{:S(2)}, u32[]{:S(2)}) collective-permute-start(bf16[8,32,128]{2,1,0:T(8,128)(2,1)S(1)} %get-tuple-element.44), channel_id=1, source_target_pairs={{0,0},{1,1},{2,2},{3,3},{4,32},{5,33},{6,34},{7,35},{8,64},{9,65},... | collective-permute-start | bytes 196616 | tf_op jit(solution)/shard_map/ppermute | solution.py:41
  68.2 3.9 %collective-permute-start.14 = (bf16[8,32,128]{2,1,0:T(8,128)(2,1)S(1)}, bf16[8,32,128]{2,1,0:T(8,128)(2,1)S(1)}, u32[]{:S(2)}, u32[]{:S(2)}) collective-permute-start(bf16[8,32,128]{2,1,0:T(8,128)(2,1)S(1)} %get-tuple-element.45), channel_id=1, source_target_pairs={{0,2},{1,3},{2,0},{3,1},{4,34},{5,35},{6,32},{7,33},{8,66},{9,67},... | collective-permute-start | bytes 196616 | tf_op jit(solution)/shard_map/ppermute | solution.py:41
  72.1 1.1 %add_images.1 = f32[1152,256]{1,0:T(8,128)} custom-call(f32[1152,256]{1,0:T(8,128)S(1)} %copy-done.5, bf16[1152,256]{1,0:T(8,128)(2,1)S(1)} %collective-permute-done.15.arrived_ref), custom_call_target="tpu_custom_call" | custom-call | flops 60000002048 | bytes 180000000 | tf_op jit(solution)/shard_map/add_images/pallas_call | solution.py:19
  73.2 0.0 all-to-all-done.1
  73.2 0.7 pool.1
  73.9 6.3 %collective-permute-done.13.same_ref = bf16[8,32,128]{2,1,0:T(8,128)(2,1)S(1)} collective-permute-done((bf16[8,32,128]{2,1,0:T(8,128)(2,1)S(1)}, bf16[8,32,128]{2,1,0:T(8,128)(2,1)S(1)}, u32[]{:S(2)}, u32[]{:S(2)}) %collective-permute-start.13) | collective-permute-done | bytes 65568 | tf_op jit(solution)/shard_map/ppermute | solution.py:41
  80.2 2.1 %collective-permute-done.14.other_ref = bf16[8,32,128]{2,1,0:T(8,128)(2,1)S(1)} collective-permute-done((bf16[8,32,128]{2,1,0:T(8,128)(2,1)S(1)}, bf16[8,32,128]{2,1,0:T(8,128)(2,1)S(1)}, u32[]{:S(2)}, u32[]{:S(2)}) %collective-permute-start.14) | collective-permute-done | bytes 65568 | tf_op jit(solution)/shard_map/ppermute | solution.py:41
  82.3 1.2 %join_tile.1 = bf16[4,64,256]{2,1,0:T(8,128)(2,1)} custom-call(s32[3]{0:T(128)S(1)} %pad_add_fusion.place_ref, bf16[8,32,128]{2,1,0:T(8,128)(2,1)S(1)} %collective-permute-done.13.same_ref, bf16[8,32,128]{2,1,0:T(8,128)(2,1)S(1)} %collective-permute-done.14.other_ref), custom_call_target="tpu_custom_call" | custom-call | flops 1000000000 | bytes 3000000 | tf_op jit(solution)/shard_map/join_tile/pallas_call | solution.py:19
  (11 shorter events, 0.0 us)
Async XLA Ops:
  0.7 0.9 %copy-start.1 = (bf16[1,4,64,256]{3,2,1,0:T(8,128)(2,1)S(1)}, bf16[1,4,64,256]{3,2,1,0:T(8,128)(2,1)}, u32[]{:S(2)}) copy-start(bf16[1,4,64,256]{3,2,1,0:T(8,128)(2,1)} %param.3) | copy-start | bytes 393220
  1.6 0.8 copy-start.2
  2.4 10.2 %copy-start.3 = (bf16[1,2,32,256]{3,2,1,0:T(8,128)(2,1)S(1)}, bf16[1,2,32,256]{3,2,1,0:T(8,128)(2,1)}, u32[]{:S(2)}) copy-start(bf16[1,2,32,256]{3,2,1,0:T(8,128)(2,1)} %param.5) | copy-start | bytes 98308
  3.0 16.9 %collective-permute-start.1 = (bf16[10,32,128]{2,1,0:T(8,128)(2,1)S(1)}, bf16[10,32,128]{2,1,0:T(8,128)(2,1)S(1)}, u32[]{:S(2)}, u32[]{:S(2)}) collective-permute-start(bf16[10,32,128]{2,1,0:T(8,128)(2,1)S(1)} %get-tuple-element.28), channel_id=1, source_target_pairs={{0,2},{1,3},{2,0},{3,1},{4,34},{5,35},{6,32},{7,33},{8,66},{9,67},... | collective-permute-start | bytes 245768 | tf_op jit(solution)/shard_map/ppermute | solution.py:41
  9.5 13.6 %collective-permute-start = (bf16[10,32,128]{2,1,0:T(8,128)(2,1)S(1)}, bf16[10,32,128]{2,1,0:T(8,128)(2,1)S(1)}, u32[]{:S(2)}, u32[]{:S(2)}) collective-permute-start(bf16[10,32,128]{2,1,0:T(8,128)(2,1)S(1)} %get-tuple-element.27.packed_ref), channel_id=1, source_target_pairs={{0,0},{1,1},{2,2},{3,3},{4,32},{5,33},{6,34},{7,35},{8,64},{9,65},... | collective-permute-start | bytes 245768 | tf_op jit(solution)/shard_map/ppermute | solution.py:41
  13.4 22.3 %all-to-all-start = ((bf16[16,2,32,256]{3,2,1,0:T(8,128)(2,1)}), bf16[16,2,32,256]{3,2,1,0:T(8,128)(2,1)S(1)}, u32[]{:S(2)}, u32[]{:S(2)}) async-start(bf16[16,2,32,256]{3,2,1,0:T(8,128)(2,1)} %spread.1), calls=%async_computation | async-start | bytes 1048576 | tf_op jit(solution)/shard_map/all_to_all | solution.py:289
  19.9 15.8 %copy-start = (bf16[3,3,128,256]{3,2,1,0:T(8,128)(2,1)S(1)}, bf16[3,3,128,256]{3,2,1,0:T(8,128)(2,1)}, u32[]{:S(2)}) copy-start(bf16[3,3,128,256]{3,2,1,0:T(8,128)(2,1)} %param.4) | copy-start | bytes 1769476
  23.8 8.5 %collective-permute-start.8 = (bf16[16,32,128]{2,1,0:T(8,128)(2,1)S(1)}, bf16[16,32,128]{2,1,0:T(8,128)(2,1)S(1)}, u32[]{:S(2)}, u32[]{:S(2)}) collective-permute-start(bf16[16,32,128]{2,1,0:T(8,128)(2,1)S(1)} %get-tuple-element.29.refs_0_), channel_id=1, source_target_pairs={{0,192},{32,224},{64,0},{96,32},{128,64},{160,96},{192,128},{224,1... | collective-permute-start | bytes 393224 | tf_op jit(solution)/shard_map/ppermute | solution.py:46
  23.9 8.4 %collective-permute-start.6 = (bf16[16,32,128]{2,1,0:T(8,128)(2,1)S(1)}, bf16[16,32,128]{2,1,0:T(8,128)(2,1)S(1)}, u32[]{:S(2)}, u32[]{:S(2)}) collective-permute-start(bf16[16,32,128]{2,1,0:T(8,128)(2,1)S(1)} %get-tuple-element.29.refs_0_), channel_id=1, source_target_pairs={{0,128},{32,160},{64,192},{96,224},{128,0},{160,32},{192,64},{224,... | collective-permute-start | bytes 393224 | tf_op jit(solution)/shard_map/ppermute | solution.py:46
  26.3 6.6 %collective-permute-start.4 = (bf16[16,32,128]{2,1,0:T(8,128)(2,1)S(1)}, bf16[16,32,128]{2,1,0:T(8,128)(2,1)S(1)}, u32[]{:S(2)}, u32[]{:S(2)}) collective-permute-start(bf16[16,32,128]{2,1,0:T(8,128)(2,1)S(1)} %get-tuple-element.29.refs_0_), channel_id=1, source_target_pairs={{0,64},{32,96},{64,128},{96,160},{128,192},{160,224},{192,0},{224,... | collective-permute-start | bytes 393224 | tf_op jit(solution)/shard_map/ppermute | solution.py:46
  27.1 12.8 %collective-permute-start.3 = (bf16[16,32,128]{2,1,0:T(8,128)(2,1)S(1)}, bf16[16,32,128]{2,1,0:T(8,128)(2,1)S(1)}, u32[]{:S(2)}, u32[]{:S(2)}) collective-permute-start(bf16[16,32,128]{2,1,0:T(8,128)(2,1)S(1)} %get-tuple-element.29.refs_0_), channel_id=1, source_target_pairs={{0,32},{32,0},{64,96},{96,64},{128,160},{160,128},{192,224},{224,1... | collective-permute-start | bytes 393224 | tf_op jit(solution)/shard_map/ppermute | solution.py:50
  32.3 7.7 %collective-permute-start.9 = (bf16[16,32,128]{2,1,0:T(8,128)(2,1)S(1)}, bf16[16,32,128]{2,1,0:T(8,128)(2,1)S(1)}, u32[]{:S(2)}, u32[]{:S(2)}) collective-permute-start(bf16[16,32,128]{2,1,0:T(8,128)(2,1)S(1)} %collective-permute-done.8.refs_6_), channel_id=1, source_target_pairs={{0,32},{32,0},{64,96},{96,64},{128,160},{160,128},{192,224},{224,1... | collective-permute-start | bytes 393224 | tf_op jit(solution)/shard_map/ppermute | solution.py:50
  32.3 7.7 %collective-permute-start.7 = (bf16[16,32,128]{2,1,0:T(8,128)(2,1)S(1)}, bf16[16,32,128]{2,1,0:T(8,128)(2,1)S(1)}, u32[]{:S(2)}, u32[]{:S(2)}) collective-permute-start(bf16[16,32,128]{2,1,0:T(8,128)(2,1)S(1)} %collective-permute-done.6.refs_4_), channel_id=1, source_target_pairs={{0,32},{32,0},{64,96},{96,64},{128,160},{160,128},{192,224},{224,1... | collective-permute-start | bytes 393224 | tf_op jit(solution)/shard_map/ppermute | solution.py:50
  32.9 7.1 %collective-permute-start.5 = (bf16[16,32,128]{2,1,0:T(8,128)(2,1)S(1)}, bf16[16,32,128]{2,1,0:T(8,128)(2,1)S(1)}, u32[]{:S(2)}, u32[]{:S(2)}) collective-permute-start(bf16[16,32,128]{2,1,0:T(8,128)(2,1)S(1)} %collective-permute-done.4.refs_2_), channel_id=1, source_target_pairs={{0,32},{32,0},{64,96},{96,64},{128,160},{160,128},{192,224},{224,1... | collective-permute-start | bytes 393224 | tf_op jit(solution)/shard_map/ppermute | solution.py:50
  39.8 6.4 %collective-permute-start.2 = (bf16[4,16,32,128]{3,2,1,0:T(8,128)(2,1)S(1)}, bf16[4,16,32,128]{3,2,1,0:T(8,128)(2,1)S(1)}, u32[]{:S(2)}, u32[]{:S(2)}) collective-permute-start(bf16[4,16,32,128]{3,2,1,0:T(8,128)(2,1)S(1)} %get-tuple-element.32), channel_id=1, source_target_pairs={{0,32},{32,0},{64,96},{96,64},{128,160},{160,128},{192,224},{224,1... | collective-permute-start | bytes 1572872 | tf_op jit(solution)/shard_map/ppermute | solution.py:50
  46.2 1.0 %copy-start.4 = (f32[1152,256]{1,0:T(8,128)}, f32[1152,256]{1,0:T(8,128)S(1)}, u32[]{:S(2)}) copy-start(f32[1152,256]{1,0:T(8,128)S(1)} %get-tuple-element.49.keep_ref) | copy-start | bytes 3538948
  47.2 24.9 %collective-permute-start.15 = (bf16[1152,256]{1,0:T(8,128)(2,1)S(1)}, bf16[1152,256]{1,0:T(8,128)(2,1)S(1)}, u32[]{:S(2)}, u32[]{:S(2)}) collective-permute-start(bf16[1152,256]{1,0:T(8,128)(2,1)S(1)} %get-tuple-element.50), channel_id=1, source_target_pairs={{0,1},{1,0},{2,3},{3,2},{4,5},{5,4},{6,7},{7,6},{8,9},{9,8},{10,11... | collective-permute-start | bytes 1769480 | tf_op jit(solution)/shard_map/ppermute | solution.py:357
  50.3 7.8 %collective-permute-start.10 = (bf16[16,32,128]{2,1,0:T(8,128)(2,1)S(1)}, bf16[16,32,128]{2,1,0:T(8,128)(2,1)S(1)}, u32[]{:S(2)}, u32[]{:S(2)}) collective-permute-start(bf16[16,32,128]{2,1,0:T(8,128)(2,1)S(1)} %get-tuple-element.39), channel_id=1, source_target_pairs={{0,64},{32,96},{64,128},{96,160},{128,192},{160,224},{192,0},{224,... | collective-permute-start | bytes 393224 | tf_op jit(solution)/shard_map/ppermute | solution.py:46
  52.1 7.9 %collective-permute-start.11 = (bf16[16,32,128]{2,1,0:T(8,128)(2,1)S(1)}, bf16[16,32,128]{2,1,0:T(8,128)(2,1)S(1)}, u32[]{:S(2)}, u32[]{:S(2)}) collective-permute-start(bf16[16,32,128]{2,1,0:T(8,128)(2,1)S(1)} %get-tuple-element.40), channel_id=1, source_target_pairs={{0,128},{32,160},{64,192},{96,224},{128,0},{160,32},{192,64},{224,... | collective-permute-start | bytes 393224 | tf_op jit(solution)/shard_map/ppermute | solution.py:46
  52.9 8.9 %collective-permute-start.12 = (bf16[16,32,128]{2,1,0:T(8,128)(2,1)S(1)}, bf16[16,32,128]{2,1,0:T(8,128)(2,1)S(1)}, u32[]{:S(2)}, u32[]{:S(2)}) collective-permute-start(bf16[16,32,128]{2,1,0:T(8,128)(2,1)S(1)} %get-tuple-element.41), channel_id=1, source_target_pairs={{0,192},{32,224},{64,0},{96,32},{128,64},{160,96},{192,128},{224,1... | collective-permute-start | bytes 393224 | tf_op jit(solution)/shard_map/ppermute | solution.py:46
  53.6 19.7 %all-to-all-start.1 = ((bf16[32,32,256]{2,1,0:T(8,128)(2,1)}), bf16[32,32,256]{2,1,0:T(8,128)(2,1)S(1)}, u32[]{:S(2)}, u32[]{:S(2)}) async-start(bf16[32,32,256]{2,1,0:T(8,128)(2,1)} %get-tuple-element.36), calls=%async_computation.1 | async-start | bytes 1048576 | tf_op jit(solution)/shard_map/all_to_all | solution.py:358
  61.8 10.3 %copy-start.5 = (f32[1152,256]{1,0:T(8,128)S(1)}, f32[1152,256]{1,0:T(8,128)}, u32[]{:S(2)}) copy-start(f32[1152,256]{1,0:T(8,128)} %copy-done.4) | copy-start | bytes 3538948
  62.4 17.8 %collective-permute-start.13 = (bf16[8,32,128]{2,1,0:T(8,128)(2,1)S(1)}, bf16[8,32,128]{2,1,0:T(8,128)(2,1)S(1)}, u32[]{:S(2)}, u32[]{:S(2)}) collective-permute-start(bf16[8,32,128]{2,1,0:T(8,128)(2,1)S(1)} %get-tuple-element.44), channel_id=1, source_target_pairs={{0,0},{1,1},{2,2},{3,3},{4,32},{5,33},{6,34},{7,35},{8,64},{9,65},... | collective-permute-start | bytes 196616 | tf_op jit(solution)/shard_map/ppermute | solution.py:41
  68.2 14.1 %collective-permute-start.14 = (bf16[8,32,128]{2,1,0:T(8,128)(2,1)S(1)}, bf16[8,32,128]{2,1,0:T(8,128)(2,1)S(1)}, u32[]{:S(2)}, u32[]{:S(2)}) collective-permute-start(bf16[8,32,128]{2,1,0:T(8,128)(2,1)S(1)} %get-tuple-element.45), channel_id=1, source_target_pairs={{0,2},{1,3},{2,0},{3,1},{4,34},{5,35},{6,32},{7,33},{8,66},{9,67},... | collective-permute-start | bytes 196616 | tf_op jit(solution)/shard_map/ppermute | solution.py:41

commit v6 on v5

--- a/solution.py
+++ b/solution.py
@@ -167,39 +167,43 @@
     def plane(i, a, b):
         return act_ref[4 * i + 2 * a + b].astype(F32)
 
+    def split(sums):
+        coarse = [box.astype(BF16) for box in sums]
+        return coarse, [(box - part.astype(F32)).astype(BF16) for box, part in zip(sums, coarse)]
+
     def put(i, p, even, odd):
         before = jnp.where(column == 0, 0.0, pltpu.roll(odd, 1, 0))
         after = jnp.where(column == cells - 1, 0.0, pltpu.roll(even, cells - 1, 0))
         rows = pl.ds(pl.multiple_of(i * cells, cells), cells)
-        return rows, (before + even, even + odd, odd + after)
-
-    def store(rows, p, sums):
-        for q, box in enumerate(sums):
-            coarse = box.astype(BF16)
+        return rows, split((before + even, even + odd, odd + after))
+
+    def store(rows, p, parts):
+        for q, (coarse, fine) in enumerate(zip(*parts)):
             lanes = slice((3 * p + q) * half, (3 * p + q + 1) * half)
             coarse_ref[rows, lanes] = coarse
-            fine_ref[rows, lanes] = (box - coarse.astype(F32)).astype(BF16)
+            fine_ref[rows, lanes] = fine
 
     rows, sums = put(0, 0, plane(0, 0, 0), plane(0, 0, 1))
     store(rows, 0, sums)
     rows, sums = put(height - 1, 2, plane(height - 1, 1, 0), plane(height - 1, 1, 1))
     store(rows, 2, sums)
 
-    def whole(i, _):
-        rows, sums = put(i, 1, plane(i, 0, 0) + plane(i, 1, 0), plane(i, 0, 1) + plane(i, 1, 1))
+    def whole(i, upper, lower):
+        rows, sums = put(i, 1, upper[0] + lower[0], upper[1] + lower[1])
         store(rows, 1, sums)
-        return 0
-
-    def between(i, _):
-        rows, sums = put(
-            i, 0, plane(i - 1, 1, 0) + plane(i, 0, 0), plane(i - 1, 1, 1) + plane(i, 0, 1)
-        )
+
+    def step(i, last):
+        upper = plane(i, 0, 0), plane(i, 0, 1)
+        lower = plane(i, 1, 0), plane(i, 1, 1)
+        rows, sums = put(i, 0, last[0] + upper[0], last[1] + upper[1])
         store(rows, 0, sums)
         store(pl.ds(pl.multiple_of((i - 1) * cells, cells), cells), 2, sums)
-        return 0
-
-    lax.fori_loop(0, height, whole, 0, unroll=4)
-    lax.fori_loop(1, height, between, 0, unroll=4)
+        whole(i, upper, lower)
+        return lower
+
+    lower = plane(0, 1, 0), plane(0, 1, 1)
+    whole(0, (plane(0, 0, 0), plane(0, 0, 1)), lower)
+    lax.fori_loop(1, height, step, lower, unroll=4)
 
     conv = jnp.dot(coarse_ref[...], kernel_ref[...], preferred_element_type=F32)
     conv = conv + jnp.dot(fine_ref[...], kernel_ref[...], preferred_element_type=F32)

time: 84 us -> 84 us (level)
  transfers between devices with their start and end apart: 18 -> 18, of which waited for: 9 -> 8; matrix products, arithmetic and copies ran while one was open for 0% -> 0% of each run, Pallas kernels for 17% -> 17%
where the time goes in v6:
time: 84 us; the launch traced here: 83.5 us
  starting transfers between devices  40.5 us (48%)
  waiting for transfers between devices  23.4 us (28%)
  Pallas kernels  16.3 us (19%)
  local copies, waits for them, and re-layouts  2.54 us (3%)
    pallas_call x10, Pallas kernels, call(): pl.pallas_call(body, out_shape=[jax.ShapeDtypeStruct(shape, dtype) for sh...  16.3 us
    ppermute x2, starting transfers between devices, swap_tiles(): lax.ppermute(pair[1], AXES, cross)  10.4 us
    ppermute x2, waiting for transfers between devices, swap_tiles(): lax.ppermute(pair[0], AXES, stay)  9.43 us
    ppermute x6, waiting for transfers between devices, to_y(): lax.ppermute(block, 'filt', [(i, (i + 2 * step) % count) for i in range(c...  8.99 us
    ppermute x2, starting transfers between devices, swap_tiles(): lax.ppermute(pair[0], AXES, stay)  8.83 us
    ppermute x6, starting transfers between devices, to_y(): lax.ppermute(block, 'filt', [(i, (i + 2 * step) % count) for i in range(c...  6.59 us
    all_to_all x1, starting transfers between devices, local(): lax.all_to_all(copies, 'rows', 0, 0, tiled=True)  6.51 us
    all_to_all x1, starting transfers between devices, local(): conv = lax.all_to_all(conv, 'rows', 0, 0, tiled=True)  4.48 us
  transfers between devices with their start and end apart: 18, of which 8 were waited for; matrix products, arithmetic and copies ran while one was open for 0% of the time, Pallas kernels for 17%

profile of v6, /device:TPU:56, one launch (start us, length us, event | category | flops | bytes accessed | tf_op | source)
XLA Modules:
  0.0 83.5 jit_solution(8081128122640529750)
XLA Ops:
  0.7 0.1 pad_add_fusion.place_ref
  0.7 0.9 %copy-done.1 = bf16[1,4,64,256]{3,2,1,0:T(8,128)(2,1)S(1)} copy-done((bf16[1,4,64,256]{3,2,1,0:T(8,128)(2,1)S(1)}, bf16[1,4,64,256]{3,2,1,0:T(8,128)(2,1)}, u32[]{:S(2)}) %copy-start.1) | copy-done | bytes 131096
  1.6 0.8 copy-done.2
  2.4 0.6 split_tile.1
  3.0 6.5 %collective-permute-start.1 = (bf16[10,32,128]{2,1,0:T(8,128)(2,1)S(1)}, bf16[10,32,128]{2,1,0:T(8,128)(2,1)S(1)}, u32[]{:S(2)}, u32[]{:S(2)}) collective-permute-start(bf16[10,32,128]{2,1,0:T(8,128)(2,1)S(1)} %get-tuple-element.28), channel_id=1, source_target_pairs={{0,2},{1,3},{2,0},{3,1},{4,34},{5,35},{6,32},{7,33},{8,66},{9,67},... | collective-permute-start | bytes 245768 | tf_op jit(solution)/shard_map/ppermute | solution.py:41
  9.5 3.1 %collective-permute-start = (bf16[10,32,128]{2,1,0:T(8,128)(2,1)S(1)}, bf16[10,32,128]{2,1,0:T(8,128)(2,1)S(1)}, u32[]{:S(2)}, u32[]{:S(2)}) collective-permute-start(bf16[10,32,128]{2,1,0:T(8,128)(2,1)S(1)} %get-tuple-element.27.packed_ref), channel_id=1, source_target_pairs={{0,0},{1,1},{2,2},{3,3},{4,32},{5,33},{6,34},{7,35},{8,64},{9,65},... | collective-permute-start | bytes 245768 | tf_op jit(solution)/shard_map/ppermute | solution.py:41
  12.6 0.8 spread.1
  13.4 6.5 %all-to-all-start = ((bf16[16,2,32,256]{3,2,1,0:T(8,128)(2,1)}), bf16[16,2,32,256]{3,2,1,0:T(8,128)(2,1)S(1)}, u32[]{:S(2)}, u32[]{:S(2)}) async-start(bf16[16,2,32,256]{3,2,1,0:T(8,128)(2,1)} %spread.1), calls=%async_computation | async-start | bytes 1048576 | tf_op jit(solution)/shard_map/all_to_all | solution.py:293
  19.9 0.0 collective-permute-done.1.other_ref
  19.9 3.2 %collective-permute-done.same_ref = bf16[10,32,128]{2,1,0:T(8,128)(2,1)S(1)} collective-permute-done((bf16[10,32,128]{2,1,0:T(8,128)(2,1)S(1)}, bf16[10,32,128]{2,1,0:T(8,128)(2,1)S(1)}, u32[]{:S(2)}, u32[]{:S(2)}) %collective-permute-start) | collective-permute-done | bytes 81952 | tf_op jit(solution)/shard_map/ppermute | solution.py:41
  23.1 0.7 activate.1
  23.8 0.1 collective-permute-start.8
  23.9 2.4 %collective-permute-start.6 = (bf16[16,32,128]{2,1,0:T(8,128)(2,1)S(1)}, bf16[16,32,128]{2,1,0:T(8,128)(2,1)S(1)}, u32[]{:S(2)}, u32[]{:S(2)}) collective-permute-start(bf16[16,32,128]{2,1,0:T(8,128)(2,1)S(1)} %get-tuple-element.29.refs_0_), channel_id=1, source_target_pairs={{0,128},{32,160},{64,192},{96,224},{128,0},{160,32},{192,64},{224,... | collective-permute-start | bytes 393224 | tf_op jit(solution)/shard_map/ppermute | solution.py:46
  26.3 0.8 collective-permute-start.4
  27.1 0.0 collective-permute-start.3
  27.1 5.2 %collective-permute-done.8.refs_6_ = bf16[16,32,128]{2,1,0:T(8,128)(2,1)S(1)} collective-permute-done((bf16[16,32,128]{2,1,0:T(8,128)(2,1)S(1)}, bf16[16,32,128]{2,1,0:T(8,128)(2,1)S(1)}, u32[]{:S(2)}, u32[]{:S(2)}) %collective-permute-start.8) | collective-permute-done | bytes 131104 | tf_op jit(solution)/shard_map/ppermute | solution.py:46
  32.3 0.0 collective-permute-start.9
  32.3 0.0 collective-permute-done.6.refs_4_
  32.3 0.5 collective-permute-start.7
  32.8 0.1 collective-permute-done.4.refs_2_
  32.9 2.8 %all-to-all-done = bf16[16,2,32,256]{3,2,1,0:T(8,128)(2,1)S(1)} async-done(((bf16[16,2,32,256]{3,2,1,0:T(8,128)(2,1)}), bf16[16,2,32,256]{3,2,1,0:T(8,128)(2,1)S(1)}, u32[]{:S(2)}, u32[]{:S(2)}) %all-to-all-start) | async-done | bytes 524320 | tf_op jit(solution)/shard_map/all_to_all | solution.py:293
  35.7 4.1 %back_conv.1 = (bf16[4,16,32,128]{3,2,1,0:T(8,128)(2,1)S(1)}, f32[4,16,32,128]{3,2,1,0:T(8,128)S(1)}) custom-call(s32[3]{0:T(128)S(1)} %pad_add_fusion.place_ref, bf16[32,32,256]{2,1,0:T(8,128)(2,1)S(1)} %bitcast.11, bf16[1152,256]{1,0:T(8,128)(2,1)S(1)} %bitcast.14), custom_call_target="tpu_custom_call" | custom-call | flops 4000000000 | bytes 12000000 | tf_op jit(solution)/shard_map/back_conv/pallas_call | solution.py:19
  39.8 0.1 collective-permute-start.2
  39.9 0.0 collective-permute-done.3.refs_1_
  39.9 0.0 collective-permute-done.7.refs_5_
  39.9 0.0 collective-permute-done.5.refs_3_
  39.9 6.3 %forward.1 = (bf16[32,32,256]{2,1,0:T(8,128)(2,1)}, f32[1152,256]{1,0:T(8,128)S(1)}, bf16[1152,256]{1,0:T(8,128)(2,1)S(1)}) custom-call(s32[3]{0:T(128)S(1)} %pad_add_fusion.place_ref, bf16[16,32,128]{2,1,0:T(8,128)(2,1)S(1)} %get-tuple-element.29.refs_0_, bf16[16,32,128]{2,1,0:T(8,128)(2,1)S(1)} %collective-permute-done.3.refs_1_, ...), custom_call_target="tpu_custom_call" | custom-call | flops 6000000000 | bytes 18000000 | tf_op jit(solution)/shard_map/forward/pallas_call | solution.py:19
  46.2 0.0 copy-start.4
  46.2 0.0 collective-permute-done.2.cross_ref
  46.3 0.1 add_cores.1
  46.4 0.9 %copy-done.4 = f32[1152,256]{1,0:T(8,128)} copy-done((f32[1152,256]{1,0:T(8,128)}, f32[1152,256]{1,0:T(8,128)S(1)}, u32[]{:S(2)}) %copy-start.4) | copy-done | bytes 1179672
  47.3 3.0 %collective-permute-start.15 = (bf16[1152,256]{1,0:T(8,128)(2,1)S(1)}, bf16[1152,256]{1,0:T(8,128)(2,1)S(1)}, u32[]{:S(2)}, u32[]{:S(2)}) collective-permute-start(bf16[1152,256]{1,0:T(8,128)(2,1)S(1)} %get-tuple-element.50), channel_id=1, source_target_pairs={{0,1},{1,0},{2,3},{3,2},{4,5},{5,4},{6,7},{7,6},{8,9},{9,8},{10,11... | collective-permute-start | bytes 1769480 | tf_op jit(solution)/shard_map/ppermute | solution.py:361
  50.3 1.9 %collective-permute-start.10 = (bf16[16,32,128]{2,1,0:T(8,128)(2,1)S(1)}, bf16[16,32,128]{2,1,0:T(8,128)(2,1)S(1)}, u32[]{:S(2)}, u32[]{:S(2)}) collective-permute-start(bf16[16,32,128]{2,1,0:T(8,128)(2,1)S(1)} %get-tuple-element.39), channel_id=1, source_target_pairs={{0,64},{32,96},{64,128},{96,160},{128,192},{160,224},{192,0},{224,... | collective-permute-start | bytes 393224 | tf_op jit(solution)/shard_map/ppermute | solution.py:46
  52.1 0.8 collective-permute-start.11
  52.9 0.7 collective-permute-start.12
  53.6 4.5 %all-to-all-start.1 = ((bf16[32,32,256]{2,1,0:T(8,128)(2,1)}), bf16[32,32,256]{2,1,0:T(8,128)(2,1)S(1)}, u32[]{:S(2)}, u32[]{:S(2)}) async-start(bf16[32,32,256]{2,1,0:T(8,128)(2,1)} %get-tuple-element.36), calls=%async_computation.1 | async-start | bytes 1048576 | tf_op jit(solution)/shard_map/all_to_all | solution.py:362
  58.1 0.1 collective-permute-done.10.refs_0_
  58.1 1.9 %collective-permute-done.11.refs_1_ = bf16[16,32,128]{2,1,0:T(8,128)(2,1)S(1)} collective-permute-done((bf16[16,32,128]{2,1,0:T(8,128)(2,1)S(1)}, bf16[16,32,128]{2,1,0:T(8,128)(2,1)S(1)}, u32[]{:S(2)}, u32[]{:S(2)}) %collective-permute-start.11) | collective-permute-done | bytes 131104 | tf_op jit(solution)/shard_map/ppermute | solution.py:46
  60.0 1.7 %collective-permute-done.12.refs_2_ = bf16[16,32,128]{2,1,0:T(8,128)(2,1)S(1)} collective-permute-done((bf16[16,32,128]{2,1,0:T(8,128)(2,1)S(1)}, bf16[16,32,128]{2,1,0:T(8,128)(2,1)S(1)}, u32[]{:S(2)}, u32[]{:S(2)}) %collective-permute-start.12) | collective-permute-done | bytes 131104 | tf_op jit(solution)/shard_map/ppermute | solution.py:46
  61.8 0.6 input_side.1
  62.4 5.8 %collective-permute-start.13 = (bf16[8,32,128]{2,1,0:T(8,128)(2,1)S(1)}, bf16[8,32,128]{2,1,0:T(8,128)(2,1)S(1)}, u32[]{:S(2)}, u32[]{:S(2)}) collective-permute-start(bf16[8,32,128]{2,1,0:T(8,128)(2,1)S(1)} %get-tuple-element.44), channel_id=1, source_target_pairs={{0,0},{1,1},{2,2},{3,3},{4,32},{5,33},{6,34},{7,35},{8,64},{9,65},... | collective-permute-start | bytes 196616 | tf_op jit(solution)/shard_map/ppermute | solution.py:41
  68.2 3.9 %collective-permute-start.14 = (bf16[8,32,128]{2,1,0:T(8,128)(2,1)S(1)}, bf16[8,32,128]{2,1,0:T(8,128)(2,1)S(1)}, u32[]{:S(2)}, u32[]{:S(2)}) collective-permute-start(bf16[8,32,128]{2,1,0:T(8,128)(2,1)S(1)} %get-tuple-element.45), channel_id=1, source_target_pairs={{0,2},{1,3},{2,0},{3,1},{4,34},{5,35},{6,32},{7,33},{8,66},{9,67},... | collective-permute-start | bytes 196616 | tf_op jit(solution)/shard_map/ppermute | solution.py:41
  72.1 1.1 %add_images.1 = f32[1152,256]{1,0:T(8,128)} custom-call(f32[1152,256]{1,0:T(8,128)S(1)} %copy-done.5, bf16[1152,256]{1,0:T(8,128)(2,1)S(1)} %collective-permute-done.15.arrived_ref), custom_call_target="tpu_custom_call" | custom-call | flops 60000002048 | bytes 180000000 | tf_op jit(solution)/shard_map/add_images/pallas_call | solution.py:19
  73.2 0.0 all-to-all-done.1
  73.2 0.7 pool.1
  73.9 6.3 %collective-permute-done.13.same_ref = bf16[8,32,128]{2,1,0:T(8,128)(2,1)S(1)} collective-permute-done((bf16[8,32,128]{2,1,0:T(8,128)(2,1)S(1)}, bf16[8,32,128]{2,1,0:T(8,128)(2,1)S(1)}, u32[]{:S(2)}, u32[]{:S(2)}) %collective-permute-start.13) | collective-permute-done | bytes 65568 | tf_op jit(solution)/shard_map/ppermute | solution.py:41
  80.2 2.1 %collective-permute-done.14.other_ref = bf16[8,32,128]{2,1,0:T(8,128)(2,1)S(1)} collective-permute-done((bf16[8,32,128]{2,1,0:T(8,128)(2,1)S(1)}, bf16[8,32,128]{2,1,0:T(8,128)(2,1)S(1)}, u32[]{:S(2)}, u32[]{:S(2)}) %collective-permute-start.14) | collective-permute-done | bytes 65568 | tf_op jit(solution)/shard_map/ppermute | solution.py:41
  82.3 1.2 %join_tile.1 = bf16[4,64,256]{2,1,0:T(8,128)(2,1)} custom-call(s32[3]{0:T(128)S(1)} %pad_add_fusion.place_ref, bf16[8,32,128]{2,1,0:T(8,128)(2,1)S(1)} %collective-permute-done.13.same_ref, bf16[8,32,128]{2,1,0:T(8,128)(2,1)S(1)} %collective-permute-done.14.other_ref), custom_call_target="tpu_custom_call" | custom-call | flops 1000000000 | bytes 3000000 | tf_op jit(solution)/shard_map/join_tile/pallas_call | solution.py:19
  (11 shorter events, 0.0 us)
Async XLA Ops:
  0.7 0.9 %copy-start.1 = (bf16[1,4,64,256]{3,2,1,0:T(8,128)(2,1)S(1)}, bf16[1,4,64,256]{3,2,1,0:T(8,128)(2,1)}, u32[]{:S(2)}) copy-start(bf16[1,4,64,256]{3,2,1,0:T(8,128)(2,1)} %param.3) | copy-start | bytes 393220
  1.6 0.8 copy-start.2
  2.4 10.2 %copy-start.3 = (bf16[1,2,32,256]{3,2,1,0:T(8,128)(2,1)S(1)}, bf16[1,2,32,256]{3,2,1,0:T(8,128)(2,1)}, u32[]{:S(2)}) copy-start(bf16[1,2,32,256]{3,2,1,0:T(8,128)(2,1)} %param.5) | copy-start | bytes 98308
  3.0 16.9 %collective-permute-start.1 = (bf16[10,32,128]{2,1,0:T(8,128)(2,1)S(1)}, bf16[10,32,128]{2,1,0:T(8,128)(2,1)S(1)}, u32[]{:S(2)}, u32[]{:S(2)}) collective-permute-start(bf16[10,32,128]{2,1,0:T(8,128)(2,1)S(1)} %get-tuple-element.28), channel_id=1, source_target_pairs={{0,2},{1,3},{2,0},{3,1},{4,34},{5,35},{6,32},{7,33},{8,66},{9,67},... | collective-permute-start | bytes 245768 | tf_op jit(solution)/shard_map/ppermute | solution.py:41
  9.5 13.6 %collective-permute-start = (bf16[10,32,128]{2,1,0:T(8,128)(2,1)S(1)}, bf16[10,32,128]{2,1,0:T(8,128)(2,1)S(1)}, u32[]{:S(2)}, u32[]{:S(2)}) collective-permute-start(bf16[10,32,128]{2,1,0:T(8,128)(2,1)S(1)} %get-tuple-element.27.packed_ref), channel_id=1, source_target_pairs={{0,0},{1,1},{2,2},{3,3},{4,32},{5,33},{6,34},{7,35},{8,64},{9,65},... | collective-permute-start | bytes 245768 | tf_op jit(solution)/shard_map/ppermute | solution.py:41
  13.4 22.3 %all-to-all-start = ((bf16[16,2,32,256]{3,2,1,0:T(8,128)(2,1)}), bf16[16,2,32,256]{3,2,1,0:T(8,128)(2,1)S(1)}, u32[]{:S(2)}, u32[]{:S(2)}) async-start(bf16[16,2,32,256]{3,2,1,0:T(8,128)(2,1)} %spread.1), calls=%async_computation | async-start | bytes 1048576 | tf_op jit(solution)/shard_map/all_to_all | solution.py:293
  19.9 15.8 %copy-start = (bf16[3,3,128,256]{3,2,1,0:T(8,128)(2,1)S(1)}, bf16[3,3,128,256]{3,2,1,0:T(8,128)(2,1)}, u32[]{:S(2)}) copy-start(bf16[3,3,128,256]{3,2,1,0:T(8,128)(2,1)} %param.4) | copy-start | bytes 1769476
  23.8 8.5 %collective-permute-start.8 = (bf16[16,32,128]{2,1,0:T(8,128)(2,1)S(1)}, bf16[16,32,128]{2,1,0:T(8,128)(2,1)S(1)}, u32[]{:S(2)}, u32[]{:S(2)}) collective-permute-start(bf16[16,32,128]{2,1,0:T(8,128)(2,1)S(1)} %get-tuple-element.29.refs_0_), channel_id=1, source_target_pairs={{0,192},{32,224},{64,0},{96,32},{128,64},{160,96},{192,128},{224,1... | collective-permute-start | bytes 393224 | tf_op jit(solution)/shard_map/ppermute | solution.py:46
  23.9 8.4 %collective-permute-start.6 = (bf16[16,32,128]{2,1,0:T(8,128)(2,1)S(1)}, bf16[16,32,128]{2,1,0:T(8,128)(2,1)S(1)}, u32[]{:S(2)}, u32[]{:S(2)}) collective-permute-start(bf16[16,32,128]{2,1,0:T(8,128)(2,1)S(1)} %get-tuple-element.29.refs_0_), channel_id=1, source_target_pairs={{0,128},{32,160},{64,192},{96,224},{128,0},{160,32},{192,64},{224,... | collective-permute-start | bytes 393224 | tf_op jit(solution)/shard_map/ppermute | solution.py:46
  26.3 6.6 %collective-permute-start.4 = (bf16[16,32,128]{2,1,0:T(8,128)(2,1)S(1)}, bf16[16,32,128]{2,1,0:T(8,128)(2,1)S(1)}, u32[]{:S(2)}, u32[]{:S(2)}) collective-permute-start(bf16[16,32,128]{2,1,0:T(8,128)(2,1)S(1)} %get-tuple-element.29.refs_0_), channel_id=1, source_target_pairs={{0,64},{32,96},{64,128},{96,160},{128,192},{160,224},{192,0},{224,... | collective-permute-start | bytes 393224 | tf_op jit(solution)/shard_map/ppermute | solution.py:46
  27.1 12.8 %collective-permute-start.3 = (bf16[16,32,128]{2,1,0:T(8,128)(2,1)S(1)}, bf16[16,32,128]{2,1,0:T(8,128)(2,1)S(1)}, u32[]{:S(2)}, u32[]{:S(2)}) collective-permute-start(bf16[16,32,128]{2,1,0:T(8,128)(2,1)S(1)} %get-tuple-element.29.refs_0_), channel_id=1, source_target_pairs={{0,32},{32,0},{64,96},{96,64},{128,160},{160,128},{192,224},{224,1... | collective-permute-start | bytes 393224 | tf_op jit(solution)/shard_map/ppermute | solution.py:50
  32.3 7.7 %collective-permute-start.9 = (bf16[16,32,128]{2,1,0:T(8,128)(2,1)S(1)}, bf16[16,32,128]{2,1,0:T(8,128)(2,1)S(1)}, u32[]{:S(2)}, u32[]{:S(2)}) collective-permute-start(bf16[16,32,128]{2,1,0:T(8,128)(2,1)S(1)} %collective-permute-done.8.refs_6_), channel_id=1, source_target_pairs={{0,32},{32,0},{64,96},{96,64},{128,160},{160,128},{192,224},{224,1... | collective-permute-start | bytes 393224 | tf_op jit(solution)/shard_map/ppermute | solution.py:50
  32.3 7.7 %collective-permute-start.7 = (bf16[16,32,128]{2,1,0:T(8,128)(2,1)S(1)}, bf16[16,32,128]{2,1,0:T(8,128)(2,1)S(1)}, u32[]{:S(2)}, u32[]{:S(2)}) collective-permute-start(bf16[16,32,128]{2,1,0:T(8,128)(2,1)S(1)} %collective-permute-done.6.refs_4_), channel_id=1, source_target_pairs={{0,32},{32,0},{64,96},{96,64},{128,160},{160,128},{192,224},{224,1... | collective-permute-start | bytes 393224 | tf_op jit(solution)/shard_map/ppermute | solution.py:50
  32.9 7.1 %collective-permute-start.5 = (bf16[16,32,128]{2,1,0:T(8,128)(2,1)S(1)}, bf16[16,32,128]{2,1,0:T(8,128)(2,1)S(1)}, u32[]{:S(2)}, u32[]{:S(2)}) collective-permute-start(bf16[16,32,128]{2,1,0:T(8,128)(2,1)S(1)} %collective-permute-done.4.refs_2_), channel_id=1, source_target_pairs={{0,32},{32,0},{64,96},{96,64},{128,160},{160,128},{192,224},{224,1... | collective-permute-start | bytes 393224 | tf_op jit(solution)/shard_map/ppermute | solution.py:50
  39.8 6.4 %collective-permute-start.2 = (bf16[4,16,32,128]{3,2,1,0:T(8,128)(2,1)S(1)}, bf16[4,16,32,128]{3,2,1,0:T(8,128)(2,1)S(1)}, u32[]{:S(2)}, u32[]{:S(2)}) collective-permute-start(bf16[4,16,32,128]{3,2,1,0:T(8,128)(2,1)S(1)} %get-tuple-element.32), channel_id=1, source_target_pairs={{0,32},{32,0},{64,96},{96,64},{128,160},{160,128},{192,224},{224,1... | collective-permute-start | bytes 1572872 | tf_op jit(solution)/shard_map/ppermute | solution.py:50
  46.2 1.0 %copy-start.4 = (f32[1152,256]{1,0:T(8,128)}, f32[1152,256]{1,0:T(8,128)S(1)}, u32[]{:S(2)}) copy-start(f32[1152,256]{1,0:T(8,128)S(1)} %get-tuple-element.49.keep_ref) | copy-start | bytes 3538948
  47.3 24.9 %collective-permute-start.15 = (bf16[1152,256]{1,0:T(8,128)(2,1)S(1)}, bf16[1152,256]{1,0:T(8,128)(2,1)S(1)}, u32[]{:S(2)}, u32[]{:S(2)}) collective-permute-start(bf16[1152,256]{1,0:T(8,128)(2,1)S(1)} %get-tuple-element.50), channel_id=1, source_target_pairs={{0,1},{1,0},{2,3},{3,2},{4,5},{5,4},{6,7},{7,6},{8,9},{9,8},{10,11... | collective-permute-start | bytes 1769480 | tf_op jit(solution)/shard_map/ppermute | solution.py:361
  50.3 7.8 %collective-permute-start.10 = (bf16[16,32,128]{2,1,0:T(8,128)(2,1)S(1)}, bf16[16,32,128]{2,1,0:T(8,128)(2,1)S(1)}, u32[]{:S(2)}, u32[]{:S(2)}) collective-permute-start(bf16[16,32,128]{2,1,0:T(8,128)(2,1)S(1)} %get-tuple-element.39), channel_id=1, source_target_pairs={{0,64},{32,96},{64,128},{96,160},{128,192},{160,224},{192,0},{224,... | collective-permute-start | bytes 393224 | tf_op jit(solution)/shard_map/ppermute | solution.py:46
  52.1 7.9 %collective-permute-start.11 = (bf16[16,32,128]{2,1,0:T(8,128)(2,1)S(1)}, bf16[16,32,128]{2,1,0:T(8,128)(2,1)S(1)}, u32[]{:S(2)}, u32[]{:S(2)}) collective-permute-start(bf16[16,32,128]{2,1,0:T(8,128)(2,1)S(1)} %get-tuple-element.40), channel_id=1, source_target_pairs={{0,128},{32,160},{64,192},{96,224},{128,0},{160,32},{192,64},{224,... | collective-permute-start | bytes 393224 | tf_op jit(solution)/shard_map/ppermute | solution.py:46
  52.9 8.9 %collective-permute-start.12 = (bf16[16,32,128]{2,1,0:T(8,128)(2,1)S(1)}, bf16[16,32,128]{2,1,0:T(8,128)(2,1)S(1)}, u32[]{:S(2)}, u32[]{:S(2)}) collective-permute-start(bf16[16,32,128]{2,1,0:T(8,128)(2,1)S(1)} %get-tuple-element.41), channel_id=1, source_target_pairs={{0,192},{32,224},{64,0},{96,32},{128,64},{160,96},{192,128},{224,1... | collective-permute-start | bytes 393224 | tf_op jit(solution)/shard_map/ppermute | solution.py:46
  53.6 19.7 %all-to-all-start.1 = ((bf16[32,32,256]{2,1,0:T(8,128)(2,1)}), bf16[32,32,256]{2,1,0:T(8,128)(2,1)S(1)}, u32[]{:S(2)}, u32[]{:S(2)}) async-start(bf16[32,32,256]{2,1,0:T(8,128)(2,1)} %get-tuple-element.36), calls=%async_computation.1 | async-start | bytes 1048576 | tf_op jit(solution)/shard_map/all_to_all | solution.py:362
  61.8 10.3 %copy-start.5 = (f32[1152,256]{1,0:T(8,128)S(1)}, f32[1152,256]{1,0:T(8,128)}, u32[]{:S(2)}) copy-start(f32[1152,256]{1,0:T(8,128)} %copy-done.4) | copy-start | bytes 3538948
  62.4 17.8 %collective-permute-start.13 = (bf16[8,32,128]{2,1,0:T(8,128)(2,1)S(1)}, bf16[8,32,128]{2,1,0:T(8,128)(2,1)S(1)}, u32[]{:S(2)}, u32[]{:S(2)}) collective-permute-start(bf16[8,32,128]{2,1,0:T(8,128)(2,1)S(1)} %get-tuple-element.44), channel_id=1, source_target_pairs={{0,0},{1,1},{2,2},{3,3},{4,32},{5,33},{6,34},{7,35},{8,64},{9,65},... | collective-permute-start | bytes 196616 | tf_op jit(solution)/shard_map/ppermute | solution.py:41
  68.2 14.1 %collective-permute-start.14 = (bf16[8,32,128]{2,1,0:T(8,128)(2,1)S(1)}, bf16[8,32,128]{2,1,0:T(8,128)(2,1)S(1)}, u32[]{:S(2)}, u32[]{:S(2)}) collective-permute-start(bf16[8,32,128]{2,1,0:T(8,128)(2,1)S(1)} %get-tuple-element.45), channel_id=1, source_target_pairs={{0,2},{1,3},{2,0},{3,1},{4,34},{5,35},{6,32},{7,33},{8,66},{9,67},... | collective-permute-start | bytes 196616 | tf_op jit(solution)/shard_map/ppermute | solution.py:41

commit v7 on v5

--- a/solution.py
+++ b/solution.py
@@ -6,7 +6,7 @@
 from jax.sharding import PartitionSpec as P
 
 MU_ACT = 15
-MU_POOL, MU_ADD, MU_JOIN, MU_IN, MU_BACK, MU_FWD = 10, 60, 1, 1, 4, 6
+MU_POOL, MU_ADD, MU_JOIN, MU_IN, MU_BACK, MU_FWD = 10, 20, 1, 1, 4, 6
 AXES = ("filt", "rows", "rep")
 VMEM = pl.BlockSpec(memory_space=pltpu.VMEM)
 ANY = pl.BlockSpec(memory_space=pl.ANY)
@@ -146,7 +146,7 @@
 
 
 def forward(place_ref, *refs):
-    chunks, (cot_ref, kernel_ref, conv_ref, keep_ref, send_ref, act_ref, coarse_ref, fine_ref, arrived) = refs[:-9], refs[-9:]
+    chunks, (kernel_ref, conv_ref, coarse_ref, act_ref, fine_ref, arrived) = refs[:-6], refs[-6:]
     steps = len(chunks) // 2
     planes, cells, half = chunks[0].shape
     height = act_ref.shape[0] // 4
@@ -204,6 +204,9 @@
     conv = jnp.dot(coarse_ref[...], kernel_ref[...], preferred_element_type=F32)
     conv = conv + jnp.dot(fine_ref[...], kernel_ref[...], preferred_element_type=F32)
     conv_ref[...] = conv.astype(BF16).reshape(conv_ref.shape)
+
+
+def kernel_side(coarse_ref, cot_ref, keep_ref, send_ref):
     grad = lax.dot_general(
         coarse_ref[...],
         cot_ref[...].reshape(coarse_ref.shape[0], -1),
@@ -301,7 +304,27 @@
         other,
         micros=MU_ACT,
     )
-    cot, _ = lax.optimization_barrier((cot, act))
+    moved = [to_y(act, step) for step in range(1, steps)]
+    chunks = []
+    for block in [act] + moved:
+        chunks += [block, to_core(block)]
+    conv, coarse = call(
+        forward,
+        [((height, cells, channels), BF16), ((height * cells, 9 * half), BF16)],
+        [
+            pltpu.VMEM((4 * height, cells, half), BF16),
+            pltpu.VMEM((height * cells, 9 * half), BF16),
+            pltpu.SemaphoreType.DMA((2 * steps,)),
+        ],
+        1,
+        place,
+        *chunks,
+        kernel_flat,
+        megabytes=20,
+        micros=MU_FWD,
+        free=range(1, 1 + 2 * steps),
+    )
+    cot, _ = lax.optimization_barrier((cot, conv))
     cross, keep = call(
         back_conv,
         [((steps, 2 * planes, cells, half), BF16), ((steps, 2 * planes, cells, half), F32)],
@@ -317,11 +340,6 @@
         megabytes=20,
         micros=MU_BACK,
     )
-    moved = [to_y(act, step) for step in range(1, steps)]
-    chunks = []
-    for block in [act] + moved:
-        chunks += [block, to_core(block)]
-
     own, *terms = call(
         add_cores,
         [((2 * planes, cells, half), F32)] + [((2 * planes, cells, half), BF16)] * (steps - 1),
@@ -331,27 +349,14 @@
         to_core(cross),
     )
     terms = [to_y(term, step) for step, term in enumerate(terms, 1)]
-    conv, kernel_term, outgoing = call(
-        forward,
-        [
-            ((height, cells, channels), BF16),
-            ((9 * half, channels), F32),
-            ((9 * half, channels), BF16),
-        ],
-        [
-            pltpu.VMEM((4 * height, cells, half), BF16),
-            pltpu.VMEM((height * cells, 9 * half), BF16),
-            pltpu.VMEM((height * cells, 9 * half), BF16),
-            pltpu.SemaphoreType.DMA((2 * steps,)),
-        ],
-        1,
-        place,
-        *chunks,
+    kernel_term, outgoing = call(
+        kernel_side,
+        [((9 * half, channels), F32), ((9 * half, channels), BF16)],
+        [],
+        0,
+        coarse,
         cot,
-        kernel_flat,
         megabytes=20,
-        micros=MU_FWD,
-        free=range(1, 1 + 2 * steps),
     )
     own, conv, outgoing = lax.optimization_barrier((own, conv, outgoing))
     arrived = lax.ppermute(outgoing, "rep", [(0, 1), (1, 0)])

time: 84 us -> 84.4 us (level)
  starting transfers between devices: 40.5 us -> 41.6 us
    all_to_all x1, waiting for transfers between devices: 2.81 us -> 0.01 us  [local(): lax.all_to_all(copies, 'rows', 0, 0, tiled=True)]
    ppermute x5, waiting for transfers between devices: 0.01 us -> 2.25 us  [to_core(): lax.ppermute(block, 'filt', [(i, i ^ 1) for i in range(lax.axis_size('fil...]
    ppermute x2, starting transfers between devices: 10.4 us -> 8.9 us  [swap_tiles(): lax.ppermute(pair[1], AXES, cross)]
    ppermute x2, starting transfers between devices: 8.83 us -> 10.3 us  [swap_tiles(): lax.ppermute(pair[0], AXES, stay)]
    all_to_all x1, starting transfers between devices: 4.48 us -> 5.89 us  [local(): conv = lax.all_to_all(conv, 'rows', 0, 0, tiled=True)]
    ppermute x6, waiting for transfers between devices: 9 us -> 7.65 us  [to_y(): lax.ppermute(block, 'filt', [(i, (i + 2 * step) % count) for i in range(c...]
    all_to_all x1, waiting for transfers between devices: 0.01 us -> 1.04 us  [local(): conv = lax.all_to_all(conv, 'rows', 0, 0, tiled=True)]
    unnamed x12 -> x20, local copies, waits for them, and re-layouts: 2.54 us -> 2.38 us
  transfers between devices with their start and end apart: 18 -> 18, of which waited for: 9 -> 12; matrix products, arithmetic and copies ran while one was open for 0% -> 0% of each run, Pallas kernels for 17% -> 12%
where the time goes in v7:
time: 84.4 us; the launch traced here: 84 us
  starting transfers between devices  41.6 us (49%)
  waiting for transfers between devices  22.7 us (27%)
  Pallas kernels  16.4 us (19%)
  local copies, waits for them, and re-layouts  2.38 us (3%)
    pallas_call x11, Pallas kernels, call(): pl.pallas_call(body, out_shape=[jax.ShapeDtypeStruct(shape, dtype) for sh...  16.4 us
    ppermute x2, starting transfers between devices, swap_tiles(): lax.ppermute(pair[0], AXES, stay)  10.3 us
    ppermute x2, waiting for transfers between devices, swap_tiles(): lax.ppermute(pair[0], AXES, stay)  9.7 us
    ppermute x2, starting transfers between devices, swap_tiles(): lax.ppermute(pair[1], AXES, cross)  8.9 us
    ppermute x6, waiting for transfers between devices, to_y(): lax.ppermute(block, 'filt', [(i, (i + 2 * step) % count) for i in range(c...  7.65 us
    all_to_all x1, starting transfers between devices, local(): lax.all_to_all(copies, 'rows', 0, 0, tiled=True)  6.51 us
    ppermute x6, starting transfers between devices, to_y(): lax.ppermute(block, 'filt', [(i, (i + 2 * step) % count) for i in range(c...  6.44 us
    all_to_all x1, starting transfers between devices, local(): conv = lax.all_to_all(conv, 'rows', 0, 0, tiled=True)  5.89 us
  transfers between devices with their start and end apart: 18, of which 12 were waited for; matrix products, arithmetic and copies ran while one was open for 0% of the time, Pallas kernels for 12%

profile of v7, /device:TPU:56, one launch (start us, length us, event | category | flops | bytes accessed | tf_op | source)
XLA Modules:
  0.0 84.0 jit_solution(12986795367387523799)
XLA Ops:
  0.7 0.1 pad_add_fusion.place_ref
  0.7 0.9 %copy-done.1 = bf16[1,4,64,256]{3,2,1,0:T(8,128)(2,1)S(1)} copy-done((bf16[1,4,64,256]{3,2,1,0:T(8,128)(2,1)S(1)}, bf16[1,4,64,256]{3,2,1,0:T(8,128)(2,1)}, u32[]{:S(2)}) %copy-start.1) | copy-done | bytes 131096
  1.6 0.8 copy-done.2
  2.4 0.6 split_tile.1
  3.0 0.0 copy-start.8
  3.0 6.5 %collective-permute-start.1 = (bf16[10,32,128]{2,1,0:T(8,128)(2,1)S(1)}, bf16[10,32,128]{2,1,0:T(8,128)(2,1)S(1)}, u32[]{:S(2)}, u32[]{:S(2)}) collective-permute-start(bf16[10,32,128]{2,1,0:T(8,128)(2,1)S(1)} %get-tuple-element.29), channel_id=1, source_target_pairs={{0,2},{1,3},{2,0},{3,1},{4,34},{5,35},{6,32},{7,33},{8,66},{9,67},... | collective-permute-start | bytes 245768 | tf_op jit(solution)/shard_map/ppermute | solution.py:41
  9.5 3.1 %collective-permute-start = (bf16[10,32,128]{2,1,0:T(8,128)(2,1)S(1)}, bf16[10,32,128]{2,1,0:T(8,128)(2,1)S(1)}, u32[]{:S(2)}, u32[]{:S(2)}) collective-permute-start(bf16[10,32,128]{2,1,0:T(8,128)(2,1)S(1)} %get-tuple-element.28.packed_ref), channel_id=1, source_target_pairs={{0,0},{1,1},{2,2},{3,3},{4,32},{5,33},{6,34},{7,35},{8,64},{9,65},... | collective-permute-start | bytes 245768 | tf_op jit(solution)/shard_map/ppermute | solution.py:41
  12.6 0.8 spread.1
  13.4 6.5 %all-to-all-start = ((bf16[16,2,32,256]{3,2,1,0:T(8,128)(2,1)}), bf16[16,2,32,256]{3,2,1,0:T(8,128)(2,1)S(1)}, u32[]{:S(2)}, u32[]{:S(2)}) async-start(bf16[16,2,32,256]{3,2,1,0:T(8,128)(2,1)} %spread.1), calls=%async_computation | async-start | bytes 1048576 | tf_op jit(solution)/shard_map/all_to_all | solution.py:292
  19.9 0.0 collective-permute-done.1.other_ref
  20.0 3.2 %collective-permute-done.same_ref = bf16[10,32,128]{2,1,0:T(8,128)(2,1)S(1)} collective-permute-done((bf16[10,32,128]{2,1,0:T(8,128)(2,1)S(1)}, bf16[10,32,128]{2,1,0:T(8,128)(2,1)S(1)}, u32[]{:S(2)}, u32[]{:S(2)}) %collective-permute-start) | collective-permute-done | bytes 81952 | tf_op jit(solution)/shard_map/ppermute | solution.py:41
  23.1 0.7 activate.1
  23.8 0.7 copy-done.6
  24.5 0.0 collective-permute-start.7
  24.5 2.4 %collective-permute-start.5 = (bf16[16,32,128]{2,1,0:T(8,128)(2,1)S(1)}, bf16[16,32,128]{2,1,0:T(8,128)(2,1)S(1)}, u32[]{:S(2)}, u32[]{:S(2)}) collective-permute-start(bf16[16,32,128]{2,1,0:T(8,128)(2,1)S(1)} %get-tuple-element.30.refs_0_), channel_id=1, source_target_pairs={{0,128},{32,160},{64,192},{96,224},{128,0},{160,32},{192,64},{224,... | collective-permute-start | bytes 393224 | tf_op jit(solution)/shard_map/ppermute | solution.py:46
  26.9 0.8 collective-permute-start.3
  27.7 5.2 %collective-permute-done.7.refs_6_ = bf16[16,32,128]{2,1,0:T(8,128)(2,1)S(1)} collective-permute-done((bf16[16,32,128]{2,1,0:T(8,128)(2,1)S(1)}, bf16[16,32,128]{2,1,0:T(8,128)(2,1)S(1)}, u32[]{:S(2)}, u32[]{:S(2)}) %collective-permute-start.7) | collective-permute-done | bytes 131104 | tf_op jit(solution)/shard_map/ppermute | solution.py:46
  32.9 0.5 collective-permute-start.6
  33.4 0.1 collective-permute-done.3.refs_2_
  33.5 0.0 collective-permute-start.4
  33.5 0.0 collective-permute-done.2.refs_1_
  33.5 0.7 collective-permute-done.8.refs_7_
  34.2 0.2 collective-permute-done.6.refs_5_
  34.4 0.4 collective-permute-done.4.refs_3_
  34.9 5.6 %forward.1 = (bf16[32,32,256]{2,1,0:T(8,128)(2,1)}, bf16[1024,1152]{1,0:T(8,128)(2,1)S(1)}) custom-call(s32[3]{0:T(128)S(1)} %pad_add_fusion.place_ref, bf16[16,32,128]{2,1,0:T(8,128)(2,1)S(1)} %get-tuple-element.30.refs_0_, bf16[16,32,128]{2,1,0:T(8,128)(2,1)S(1)} %collective-permute-done.2.refs_1_, ...), custom_call_target="tpu_custom_call" | custom-call | flops 6000000000 | bytes 18000000 | tf_op jit(solution)/shard_map/forward/pallas_call | solution.py:19
  40.5 0.0 all-to-all-done
  40.5 4.1 %back_conv.1 = (bf16[4,16,32,128]{3,2,1,0:T(8,128)(2,1)S(1)}, f32[4,16,32,128]{3,2,1,0:T(8,128)S(1)}) custom-call(s32[3]{0:T(128)S(1)} %pad_add_fusion.place_ref, bf16[32,32,256]{2,1,0:T(8,128)(2,1)S(1)} %bitcast.11, bf16[1152,256]{1,0:T(8,128)(2,1)S(1)} %bitcast.15), custom_call_target="tpu_custom_call" | custom-call | flops 4000000000 | bytes 12000000 | tf_op jit(solution)/shard_map/back_conv/pallas_call | solution.py:19
  44.6 0.2 collective-permute-start.9
  44.8 0.8 kernel_side.1
  45.7 0.0 copy-start.4
  45.7 0.9 %collective-permute-done.9.cross_ref = bf16[4,16,32,128]{3,2,1,0:T(8,128)(2,1)S(1)} collective-permute-done((bf16[4,16,32,128]{3,2,1,0:T(8,128)(2,1)S(1)}, bf16[4,16,32,128]{3,2,1,0:T(8,128)(2,1)S(1)}, u32[]{:S(2)}, u32[]{:S(2)}) %collective-permute-start.9) | collective-permute-done | bytes 524320 | tf_op jit(solution)/shard_map/ppermute | solution.py:50
  46.6 0.1 add_cores.1
  46.7 2.8 %collective-permute-start.15 = (bf16[1152,256]{1,0:T(8,128)(2,1)S(1)}, bf16[1152,256]{1,0:T(8,128)(2,1)S(1)}, u32[]{:S(2)}, u32[]{:S(2)}) collective-permute-start(bf16[1152,256]{1,0:T(8,128)(2,1)S(1)} %get-tuple-element.52), channel_id=1, source_target_pairs={{0,1},{1,0},{2,3},{3,2},{4,5},{5,4},{6,7},{7,6},{8,9},{9,8},{10,11... | collective-permute-start | bytes 1769480 | tf_op jit(solution)/shard_map/ppermute | solution.py:362
  49.5 2.3 %collective-permute-start.10 = (bf16[16,32,128]{2,1,0:T(8,128)(2,1)S(1)}, bf16[16,32,128]{2,1,0:T(8,128)(2,1)S(1)}, u32[]{:S(2)}, u32[]{:S(2)}) collective-permute-start(bf16[16,32,128]{2,1,0:T(8,128)(2,1)S(1)} %get-tuple-element.41), channel_id=1, source_target_pairs={{0,64},{32,96},{64,128},{96,160},{128,192},{160,224},{192,0},{224,... | collective-permute-start | bytes 393224 | tf_op jit(solution)/shard_map/ppermute | solution.py:46
  51.9 0.0 collective-permute-start.11
  51.9 0.8 %collective-permute-start.12 = (bf16[16,32,128]{2,1,0:T(8,128)(2,1)S(1)}, bf16[16,32,128]{2,1,0:T(8,128)(2,1)S(1)}, u32[]{:S(2)}, u32[]{:S(2)}) collective-permute-start(bf16[16,32,128]{2,1,0:T(8,128)(2,1)S(1)} %get-tuple-element.43), channel_id=1, source_target_pairs={{0,192},{32,224},{64,0},{96,32},{128,64},{160,96},{192,128},{224,1... | collective-permute-start | bytes 393224 | tf_op jit(solution)/shard_map/ppermute | solution.py:46
  52.7 5.9 %all-to-all-start.1 = ((bf16[32,32,256]{2,1,0:T(8,128)(2,1)}), bf16[32,32,256]{2,1,0:T(8,128)(2,1)S(1)}, u32[]{:S(2)}, u32[]{:S(2)}) async-start(bf16[32,32,256]{2,1,0:T(8,128)(2,1)} %get-tuple-element.38), calls=%async_computation.1 | async-start | bytes 1048576 | tf_op jit(solution)/shard_map/all_to_all | solution.py:363
  58.6 1.1 %collective-permute-done.11.refs_1_ = bf16[16,32,128]{2,1,0:T(8,128)(2,1)S(1)} collective-permute-done((bf16[16,32,128]{2,1,0:T(8,128)(2,1)S(1)}, bf16[16,32,128]{2,1,0:T(8,128)(2,1)S(1)}, u32[]{:S(2)}, u32[]{:S(2)}) %collective-permute-start.11) | collective-permute-done | bytes 131104 | tf_op jit(solution)/shard_map/ppermute | solution.py:46
  59.8 1.2 %collective-permute-done.12.refs_2_ = bf16[16,32,128]{2,1,0:T(8,128)(2,1)S(1)} collective-permute-done((bf16[16,32,128]{2,1,0:T(8,128)(2,1)S(1)}, bf16[16,32,128]{2,1,0:T(8,128)(2,1)S(1)}, u32[]{:S(2)}, u32[]{:S(2)}) %collective-permute-start.12) | collective-permute-done | bytes 131104 | tf_op jit(solution)/shard_map/ppermute | solution.py:46
  61.0 0.6 input_side.1
  61.6 7.2 %collective-permute-start.13 = (bf16[8,32,128]{2,1,0:T(8,128)(2,1)S(1)}, bf16[8,32,128]{2,1,0:T(8,128)(2,1)S(1)}, u32[]{:S(2)}, u32[]{:S(2)}) collective-permute-start(bf16[8,32,128]{2,1,0:T(8,128)(2,1)S(1)} %get-tuple-element.46), channel_id=1, source_target_pairs={{0,0},{1,1},{2,2},{3,3},{4,32},{5,33},{6,34},{7,35},{8,64},{9,65},... | collective-permute-start | bytes 196616 | tf_op jit(solution)/shard_map/ppermute | solution.py:41
  68.9 2.4 %collective-permute-start.14 = (bf16[8,32,128]{2,1,0:T(8,128)(2,1)S(1)}, bf16[8,32,128]{2,1,0:T(8,128)(2,1)S(1)}, u32[]{:S(2)}, u32[]{:S(2)}) collective-permute-start(bf16[8,32,128]{2,1,0:T(8,128)(2,1)S(1)} %get-tuple-element.47), channel_id=1, source_target_pairs={{0,2},{1,3},{2,0},{3,1},{4,34},{5,35},{6,32},{7,33},{8,66},{9,67},... | collective-permute-start | bytes 196616 | tf_op jit(solution)/shard_map/ppermute | solution.py:41
  71.3 1.1 %add_images.1 = f32[1152,256]{1,0:T(8,128)} custom-call(f32[1152,256]{1,0:T(8,128)S(1)} %copy-done.5, bf16[1152,256]{1,0:T(8,128)(2,1)S(1)} %collective-permute-done.15.arrived_ref), custom_call_target="tpu_custom_call" | custom-call | flops 20000000000 | bytes 60000000 | tf_op jit(solution)/shard_map/add_images/pallas_call | solution.py:19
  72.4 1.0 %all-to-all-done.1 = bf16[32,32,256]{2,1,0:T(8,128)(2,1)S(1)} async-done(((bf16[32,32,256]{2,1,0:T(8,128)(2,1)}), bf16[32,32,256]{2,1,0:T(8,128)(2,1)S(1)}, u32[]{:S(2)}, u32[]{:S(2)}) %all-to-all-start.1) | async-done | bytes 524320 | tf_op jit(solution)/shard_map/all_to_all | solution.py:363
  73.4 0.7 pool.1
  74.1 6.5 %collective-permute-done.13.same_ref = bf16[8,32,128]{2,1,0:T(8,128)(2,1)S(1)} collective-permute-done((bf16[8,32,128]{2,1,0:T(8,128)(2,1)S(1)}, bf16[8,32,128]{2,1,0:T(8,128)(2,1)S(1)}, u32[]{:S(2)}, u32[]{:S(2)}) %collective-permute-start.13) | collective-permute-done | bytes 65568 | tf_op jit(solution)/shard_map/ppermute | solution.py:41
  80.6 2.1 %collective-permute-done.14.other_ref = bf16[8,32,128]{2,1,0:T(8,128)(2,1)S(1)} collective-permute-done((bf16[8,32,128]{2,1,0:T(8,128)(2,1)S(1)}, bf16[8,32,128]{2,1,0:T(8,128)(2,1)S(1)}, u32[]{:S(2)}, u32[]{:S(2)}) %collective-permute-start.14) | collective-permute-done | bytes 65568 | tf_op jit(solution)/shard_map/ppermute | solution.py:41
  82.7 1.2 %join_tile.1 = bf16[4,64,256]{2,1,0:T(8,128)(2,1)} custom-call(s32[3]{0:T(128)S(1)} %pad_add_fusion.place_ref, bf16[8,32,128]{2,1,0:T(8,128)(2,1)S(1)} %collective-permute-done.13.same_ref, bf16[8,32,128]{2,1,0:T(8,128)(2,1)S(1)} %collective-permute-done.14.other_ref), custom_call_target="tpu_custom_call" | custom-call | flops 1000000000 | bytes 3000000 | tf_op jit(solution)/shard_map/join_tile/pallas_call | solution.py:19
  (20 shorter events, 0.0 us)
Async XLA Ops:
  0.7 0.9 %copy-start.1 = (bf16[1,4,64,256]{3,2,1,0:T(8,128)(2,1)S(1)}, bf16[1,4,64,256]{3,2,1,0:T(8,128)(2,1)}, u32[]{:S(2)}) copy-start(bf16[1,4,64,256]{3,2,1,0:T(8,128)(2,1)} %param.3) | copy-start | bytes 393220
  1.6 0.8 copy-start.2
  2.4 10.2 %copy-start.3 = (bf16[1,2,32,256]{3,2,1,0:T(8,128)(2,1)S(1)}, bf16[1,2,32,256]{3,2,1,0:T(8,128)(2,1)}, u32[]{:S(2)}) copy-start(bf16[1,2,32,256]{3,2,1,0:T(8,128)(2,1)} %param.5) | copy-start | bytes 98308
  3.0 10.4 %copy-start.8 = (f32[2,32,256]{2,1,0:T(8,128)}, f32[2,32,256]{2,1,0:T(8,128)S(1)}, u32[]{:S(2)}) copy-start(f32[2,32,256]{2,1,0:T(8,128)S(1)} %get-tuple-element.39.cells_ref) | copy-start | bytes 196612
  3.0 16.9 %collective-permute-start.1 = (bf16[10,32,128]{2,1,0:T(8,128)(2,1)S(1)}, bf16[10,32,128]{2,1,0:T(8,128)(2,1)S(1)}, u32[]{:S(2)}, u32[]{:S(2)}) collective-permute-start(bf16[10,32,128]{2,1,0:T(8,128)(2,1)S(1)} %get-tuple-element.29), channel_id=1, source_target_pairs={{0,2},{1,3},{2,0},{3,1},{4,34},{5,35},{6,32},{7,33},{8,66},{9,67},... | collective-permute-start | bytes 245768 | tf_op jit(solution)/shard_map/ppermute | solution.py:41
  9.5 13.6 %collective-permute-start = (bf16[10,32,128]{2,1,0:T(8,128)(2,1)S(1)}, bf16[10,32,128]{2,1,0:T(8,128)(2,1)S(1)}, u32[]{:S(2)}, u32[]{:S(2)}) collective-permute-start(bf16[10,32,128]{2,1,0:T(8,128)(2,1)S(1)} %get-tuple-element.28.packed_ref), channel_id=1, source_target_pairs={{0,0},{1,1},{2,2},{3,3},{4,32},{5,33},{6,34},{7,35},{8,64},{9,65},... | collective-permute-start | bytes 245768 | tf_op jit(solution)/shard_map/ppermute | solution.py:41
  13.4 27.1 %all-to-all-start = ((bf16[16,2,32,256]{3,2,1,0:T(8,128)(2,1)}), bf16[16,2,32,256]{3,2,1,0:T(8,128)(2,1)S(1)}, u32[]{:S(2)}, u32[]{:S(2)}) async-start(bf16[16,2,32,256]{3,2,1,0:T(8,128)(2,1)} %spread.1), calls=%async_computation | async-start | bytes 1048576 | tf_op jit(solution)/shard_map/all_to_all | solution.py:292
  19.9 14.9 %copy-start = (bf16[3,3,128,256]{3,2,1,0:T(8,128)(2,1)S(1)}, bf16[3,3,128,256]{3,2,1,0:T(8,128)(2,1)}, u32[]{:S(2)}) copy-start(bf16[3,3,128,256]{3,2,1,0:T(8,128)(2,1)} %param.4) | copy-start | bytes 1769476
  23.8 0.7 copy-start.6
  24.5 8.4 %collective-permute-start.7 = (bf16[16,32,128]{2,1,0:T(8,128)(2,1)S(1)}, bf16[16,32,128]{2,1,0:T(8,128)(2,1)S(1)}, u32[]{:S(2)}, u32[]{:S(2)}) collective-permute-start(bf16[16,32,128]{2,1,0:T(8,128)(2,1)S(1)} %get-tuple-element.30.refs_0_), channel_id=1, source_target_pairs={{0,192},{32,224},{64,0},{96,32},{128,64},{160,96},{192,128},{224,1... | collective-permute-start | bytes 393224 | tf_op jit(solution)/shard_map/ppermute | solution.py:46
  24.5 8.4 %collective-permute-start.5 = (bf16[16,32,128]{2,1,0:T(8,128)(2,1)S(1)}, bf16[16,32,128]{2,1,0:T(8,128)(2,1)S(1)}, u32[]{:S(2)}, u32[]{:S(2)}) collective-permute-start(bf16[16,32,128]{2,1,0:T(8,128)(2,1)S(1)} %get-tuple-element.30.refs_0_), channel_id=1, source_target_pairs={{0,128},{32,160},{64,192},{96,224},{128,0},{160,32},{192,64},{224,... | collective-permute-start | bytes 393224 | tf_op jit(solution)/shard_map/ppermute | solution.py:46
  26.9 6.6 %collective-permute-start.3 = (bf16[16,32,128]{2,1,0:T(8,128)(2,1)S(1)}, bf16[16,32,128]{2,1,0:T(8,128)(2,1)S(1)}, u32[]{:S(2)}, u32[]{:S(2)}) collective-permute-start(bf16[16,32,128]{2,1,0:T(8,128)(2,1)S(1)} %get-tuple-element.30.refs_0_), channel_id=1, source_target_pairs={{0,64},{32,96},{64,128},{96,160},{128,192},{160,224},{192,0},{224,... | collective-permute-start | bytes 393224 | tf_op jit(solution)/shard_map/ppermute | solution.py:46
  27.7 5.8 %collective-permute-start.2 = (bf16[16,32,128]{2,1,0:T(8,128)(2,1)S(1)}, bf16[16,32,128]{2,1,0:T(8,128)(2,1)S(1)}, u32[]{:S(2)}, u32[]{:S(2)}) collective-permute-start(bf16[16,32,128]{2,1,0:T(8,128)(2,1)S(1)} %get-tuple-element.30.refs_0_), channel_id=1, source_target_pairs={{0,32},{32,0},{64,96},{96,64},{128,160},{160,128},{192,224},{224,1... | collective-permute-start | bytes 393224 | tf_op jit(solution)/shard_map/ppermute | solution.py:50
  32.9 1.3 %collective-permute-start.8 = (bf16[16,32,128]{2,1,0:T(8,128)(2,1)S(1)}, bf16[16,32,128]{2,1,0:T(8,128)(2,1)S(1)}, u32[]{:S(2)}, u32[]{:S(2)}) collective-permute-start(bf16[16,32,128]{2,1,0:T(8,128)(2,1)S(1)} %collective-permute-done.7.refs_6_), channel_id=1, source_target_pairs={{0,32},{32,0},{64,96},{96,64},{128,160},{160,128},{192,224},{224,1... | collective-permute-start | bytes 393224 | tf_op jit(solution)/shard_map/ppermute | solution.py:50
  32.9 1.5 %collective-permute-start.6 = (bf16[16,32,128]{2,1,0:T(8,128)(2,1)S(1)}, bf16[16,32,128]{2,1,0:T(8,128)(2,1)S(1)}, u32[]{:S(2)}, u32[]{:S(2)}) collective-permute-start(bf16[16,32,128]{2,1,0:T(8,128)(2,1)S(1)} %collective-permute-done.5.refs_4_), channel_id=1, source_target_pairs={{0,32},{32,0},{64,96},{96,64},{128,160},{160,128},{192,224},{224,1... | collective-permute-start | bytes 393224 | tf_op jit(solution)/shard_map/ppermute | solution.py:50
  33.5 1.3 %collective-permute-start.4 = (bf16[16,32,128]{2,1,0:T(8,128)(2,1)S(1)}, bf16[16,32,128]{2,1,0:T(8,128)(2,1)S(1)}, u32[]{:S(2)}, u32[]{:S(2)}) collective-permute-start(bf16[16,32,128]{2,1,0:T(8,128)(2,1)S(1)} %collective-permute-done.3.refs_2_), channel_id=1, source_target_pairs={{0,32},{32,0},{64,96},{96,64},{128,160},{160,128},{192,224},{224,1... | collective-permute-start | bytes 393224 | tf_op jit(solution)/shard_map/ppermute | solution.py:50
  44.6 2.0 %collective-permute-start.9 = (bf16[4,16,32,128]{3,2,1,0:T(8,128)(2,1)S(1)}, bf16[4,16,32,128]{3,2,1,0:T(8,128)(2,1)S(1)}, u32[]{:S(2)}, u32[]{:S(2)}) collective-permute-start(bf16[4,16,32,128]{3,2,1,0:T(8,128)(2,1)S(1)} %get-tuple-element.34), channel_id=1, source_target_pairs={{0,32},{32,0},{64,96},{96,64},{128,160},{160,128},{192,224},{224,1... | collective-permute-start | bytes 1572872 | tf_op jit(solution)/shard_map/ppermute | solution.py:50
  45.7 1.0 %copy-start.4 = (f32[1152,256]{1,0:T(8,128)}, f32[1152,256]{1,0:T(8,128)S(1)}, u32[]{:S(2)}) copy-start(f32[1152,256]{1,0:T(8,128)S(1)} %get-tuple-element.51.keep_ref) | copy-start | bytes 3538948
  46.6 14.4 %copy-start.7 = (f32[16,32,128]{2,1,0:T(8,128)S(1)}, f32[16,32,128]{2,1,0:T(8,128)}, u32[]{:S(2)}) copy-start(f32[16,32,128]{2,1,0:T(8,128)} %copy-done.6) | copy-start | bytes 786436
  46.7 24.5 %collective-permute-start.15 = (bf16[1152,256]{1,0:T(8,128)(2,1)S(1)}, bf16[1152,256]{1,0:T(8,128)(2,1)S(1)}, u32[]{:S(2)}, u32[]{:S(2)}) collective-permute-start(bf16[1152,256]{1,0:T(8,128)(2,1)S(1)} %get-tuple-element.52), channel_id=1, source_target_pairs={{0,1},{1,0},{2,3},{3,2},{4,5},{5,4},{6,7},{7,6},{8,9},{9,8},{10,11... | collective-permute-start | bytes 1769480 | tf_op jit(solution)/shard_map/ppermute | solution.py:362
  49.5 9.1 %collective-permute-start.10 = (bf16[16,32,128]{2,1,0:T(8,128)(2,1)S(1)}, bf16[16,32,128]{2,1,0:T(8,128)(2,1)S(1)}, u32[]{:S(2)}, u32[]{:S(2)}) collective-permute-start(bf16[16,32,128]{2,1,0:T(8,128)(2,1)S(1)} %get-tuple-element.41), channel_id=1, source_target_pairs={{0,64},{32,96},{64,128},{96,160},{128,192},{160,224},{192,0},{224,... | collective-permute-start | bytes 393224 | tf_op jit(solution)/shard_map/ppermute | solution.py:46
  51.9 7.9 %collective-permute-start.11 = (bf16[16,32,128]{2,1,0:T(8,128)(2,1)S(1)}, bf16[16,32,128]{2,1,0:T(8,128)(2,1)S(1)}, u32[]{:S(2)}, u32[]{:S(2)}) collective-permute-start(bf16[16,32,128]{2,1,0:T(8,128)(2,1)S(1)} %get-tuple-element.42), channel_id=1, source_target_pairs={{0,128},{32,160},{64,192},{96,224},{128,0},{160,32},{192,64},{224,... | collective-permute-start | bytes 393224 | tf_op jit(solution)/shard_map/ppermute | solution.py:46
  51.9 9.1 %collective-permute-start.12 = (bf16[16,32,128]{2,1,0:T(8,128)(2,1)S(1)}, bf16[16,32,128]{2,1,0:T(8,128)(2,1)S(1)}, u32[]{:S(2)}, u32[]{:S(2)}) collective-permute-start(bf16[16,32,128]{2,1,0:T(8,128)(2,1)S(1)} %get-tuple-element.43), channel_id=1, source_target_pairs={{0,192},{32,224},{64,0},{96,32},{128,64},{160,96},{192,128},{224,1... | collective-permute-start | bytes 393224 | tf_op jit(solution)/shard_map/ppermute | solution.py:46
  52.7 20.7 %all-to-all-start.1 = ((bf16[32,32,256]{2,1,0:T(8,128)(2,1)}), bf16[32,32,256]{2,1,0:T(8,128)(2,1)S(1)}, u32[]{:S(2)}, u32[]{:S(2)}) async-start(bf16[32,32,256]{2,1,0:T(8,128)(2,1)} %get-tuple-element.38), calls=%async_computation.1 | async-start | bytes 1048576 | tf_op jit(solution)/shard_map/all_to_all | solution.py:363
  61.0 10.2 %copy-start.5 = (f32[1152,256]{1,0:T(8,128)S(1)}, f32[1152,256]{1,0:T(8,128)}, u32[]{:S(2)}) copy-start(f32[1152,256]{1,0:T(8,128)} %copy-done.4) | copy-start | bytes 3538948
  61.6 19.0 %collective-permute-start.13 = (bf16[8,32,128]{2,1,0:T(8,128)(2,1)S(1)}, bf16[8,32,128]{2,1,0:T(8,128)(2,1)S(1)}, u32[]{:S(2)}, u32[]{:S(2)}) collective-permute-start(bf16[8,32,128]{2,1,0:T(8,128)(2,1)S(1)} %get-tuple-element.46), channel_id=1, source_target_pairs={{0,0},{1,1},{2,2},{3,3},{4,32},{5,33},{6,34},{7,35},{8,64},{9,65},... | collective-permute-start | bytes 196616 | tf_op jit(solution)/shard_map/ppermute | solution.py:41
  68.9 13.9 %collective-permute-start.14 = (bf16[8,32,128]{2,1,0:T(8,128)(2,1)S(1)}, bf16[8,32,128]{2,1,0:T(8,128)(2,1)S(1)}, u32[]{:S(2)}, u32[]{:S(2)}) collective-permute-start(bf16[8,32,128]{2,1,0:T(8,128)(2,1)S(1)} %get-tuple-element.47), channel_id=1, source_target_pairs={{0,2},{1,3},{2,0},{3,1},{4,34},{5,35},{6,32},{7,33},{8,66},{9,67},... | collective-permute-start | bytes 196616 | tf_op jit(solution)/shard_map/ppermute | solution.py:41
  71.3 2.2 %copy-start.9 = (f32[2,32,256]{2,1,0:T(8,128)S(1)}, f32[2,32,256]{2,1,0:T(8,128)}, u32[]{:S(2)}) copy-start(f32[2,32,256]{2,1,0:T(8,128)} %copy-done.8) | copy-start | bytes 196612
